TPU v7x, 128 devices: a whole 4x4x4 slice. The times are simulated.
128 devices in a mesh: row: 8 (over z_lo, x), col: 16 (over y, z_hi, core).
Axes of the slice: x: 4, y: 4, z: 4 (z_hi: 2, z_lo: 2; z = z_hi * 2 + z_lo), core: 2. Of those that a mesh axis runs over, the one named last changes fastest.
Arguments:
- tokens: bfloat16 [512, 512, 384], P('row', 'col'), may hold values from -25 to 25
- tissue: int32 [512, 512], P('row', 'col'), may hold values from 0 to 1, as said below
- cotangent: bfloat16 [512, 512, 384], P('row', 'col'), may hold values from -6 to 6
- packed_weight: bfloat16 [384, 1152], replicated, may hold values from -0.3125 to 0.3125
- output_weight: bfloat16 [384, 384], replicated, may hold values from -0.3125 to 0.3125
Outputs:
- layer_out: bfloat16 [512, 512, 384], P('row', 'col')
- grad_tokens: bfloat16 [512, 512, 384], P('row', 'col')
- grad_packed: float32 [384, 1152], replicated
- grad_output: float32 [384, 384], replicated
Inputs may be any that keep to these rules, and one draw needn't show every extreme that they name: 1 marks a tissue token, 0 background.
All inputs are finite; a program needn't handle non-finite values.
Results may differ from a plain program's by a relative error of at most 0.004.
The roundings to bfloat16 on the way count: a program that leaves them out, or rounds other values in their place, can miss the bound.
Values may be sent and summed in bfloat16 or wider, within the bound.
No kernel may reach another device: no remote copies, remote signals or barrier semaphores. Data moves between devices by JAX's collectives and lax.ppermute only.
A program may use at most 128 MiB of HBM per device.

v0:
```python
import jax
import jax.numpy as jnp
from jax import lax
from jax.sharding import PartitionSpec as P

HEADS = 6
HEAD = 64
KERNEL = 7
RADIUS = 3


band_rows = 8


def extended(cells, sides, width):
    for axis, dim in sides:
        count = lax.axis_size(axis)
        ends = count - 1
        head = lax.slice_in_dim(cells, 0, width, axis=dim)
        tail = lax.slice_in_dim(cells, cells.shape[dim] - width, cells.shape[dim], axis=dim)
        cells = jnp.concatenate(
            [
                lax.ppermute(tail, axis, [(i, (i + 1) % count) for i in range(ends)]),
                cells,
                lax.ppermute(head, axis, [((i + 1) % count, i) for i in range(ends)]),
            ],
            axis=dim,
        )
    return cells


def per_device(tokens, tissue, cotangent, packed_weight, output_weight):
    rows_dev, cols_dev, width = tokens.shape
    grid_rows = rows_dev * lax.axis_size("row")
    grid_cols = cols_dev * lax.axis_size("col")
    row_base = lax.axis_index("row") * rows_dev
    col_base = lax.axis_index("col") * cols_dev
    ext_cols = cols_dev + 2 * RADIUS
    key_rows = band_rows + 2 * RADIUS
    band_count = rows_dev // band_rows
    factor = HEAD ** (-0.5)
    total_scale = float(grid_rows * grid_cols) ** (-0.5)
    token_rows = tokens.reshape(-1, width)
    tissue_float = tissue.reshape(-1, 1).astype(jnp.float32)
    packed = jnp.dot(token_rows, packed_weight, preferred_element_type=jnp.float32).astype(
        jnp.bfloat16
    )
    queries = packed[:, :width].reshape(rows_dev, cols_dev, width)
    key_value = packed[:, width:].reshape(rows_dev, cols_dev, 2 * width)
    tissue_ext = extended(tissue, (("row", 0), ("col", 1)), RADIUS)
    halo_pairs = extended(key_value, (("row", 0), ("col", 1)), RADIUS)
    col_ids = jnp.arange(cols_dev, dtype=jnp.int32)
    key_cols = jnp.arange(ext_cols, dtype=jnp.int32)
    col_start = jnp.clip(col_base + col_ids - RADIUS, 0, grid_cols - KERNEL) - col_base + RADIUS
    col_inside = (key_cols[None, :] >= col_start[:, None]) & (
        key_cols[None, :] < col_start[:, None] + KERNEL
    )
    col_self = key_cols[None, :] == col_ids[:, None] + RADIUS
    band_ids = jnp.arange(band_rows, dtype=jnp.int32)
    key_band = jnp.arange(key_rows, dtype=jnp.int32)

    def allowed_keys(band_first):
        query_rows = band_first + band_ids
        row_start = (
            jnp.clip(row_base + query_rows - RADIUS, 0, grid_rows - KERNEL) - row_base + RADIUS
        )
        key_global = band_first + key_band
        row_inside = (key_global[None, :] >= row_start[:, None]) & (
            key_global[None, :] < row_start[:, None] + KERNEL
        )
        row_self = key_global[None, :] == query_rows[:, None] + RADIUS
        tissue_keys = lax.dynamic_slice_in_dim(tissue_ext, band_first, key_rows, 0) == 1
        window = row_inside[:, None, :, None] & col_inside[None, :, None, :]
        keep_key = tissue_keys[None, None] | row_self[:, None, :, None] & col_self[None, :, None, :]
        return (window & keep_key).reshape(band_rows * cols_dev, key_rows * ext_cols)

    def band_inputs(band_first):
        query_band = lax.dynamic_slice_in_dim(queries, band_first, band_rows, 0).reshape(
            -1, HEADS, HEAD
        )
        key_pair = lax.dynamic_slice_in_dim(halo_pairs, band_first, key_rows, 0).reshape(
            -1, 2 * width
        )
        key_heads = key_pair[:, :width].reshape(-1, HEADS, HEAD)
        value_heads = key_pair[:, width:].reshape(-1, HEADS, HEAD)
        return (query_band, key_heads, value_heads)

    def weights(query_band, key_heads, allowed):
        scores = (
            jnp.einsum("qhd,khd->hqk", query_band, key_heads, preferred_element_type=jnp.float32)
            * factor
        )
        scores = jnp.where(allowed[None], scores, -jnp.inf)
        row_top = jnp.max(scores, axis=-1, keepdims=True)
        exp_terms = jnp.where(allowed[None], jnp.exp(scores - row_top), 0.0)
        return exp_terms / jnp.sum(exp_terms, axis=-1, keepdims=True)

    def forward_compute(band_first):
        query_band, key_heads, value_heads = band_inputs(band_first)
        prob_low = weights(query_band, key_heads, allowed_keys(band_first)).astype(jnp.bfloat16)
        mixture = jnp.einsum(
            "hqk,khd->qhd", prob_low, value_heads, preferred_element_type=jnp.float32
        )
        return mixture.reshape(-1, width)

    def forward_band(band_index):
        band_first = band_index * band_rows
        return forward_compute(band_first)

    mixture = lax.map(forward_band, jnp.arange(band_count, dtype=jnp.int32)).reshape(-1, width)
    attended = (tissue_float * mixture).astype(jnp.bfloat16)
    layer_out = (
        token_rows.astype(jnp.float32)
        + jnp.dot(attended, output_weight, preferred_element_type=jnp.float32)
    ).astype(jnp.bfloat16)
    cotangent_rows = cotangent.reshape(-1, width)
    output_partial = lax.dot_general(
        attended, cotangent_rows, (((0,), (0,)), ((), ())), preferred_element_type=jnp.float32
    )
    grad_att = (
        tissue_float
        * lax.dot_general(
            cotangent_rows,
            output_weight,
            (((1,), (1,)), ((), ())),
            preferred_element_type=jnp.float32,
        )
    ).astype(jnp.bfloat16)
    grad_grid = grad_att.reshape(rows_dev, cols_dev, width)

    def backward_band(accumulated, band_index):
        band_first = band_index * band_rows
        query_band, key_heads, value_heads = band_inputs(band_first)
        prob_full = weights(query_band, key_heads, allowed_keys(band_first))
        prob_low = prob_full.astype(jnp.bfloat16)
        grad_band = lax.dynamic_slice_in_dim(grad_grid, band_first, band_rows, 0).reshape(
            -1, HEADS, HEAD
        )
        prob_slope = jnp.einsum(
            "qhd,khd->hqk", grad_band, value_heads, preferred_element_type=jnp.float32
        )
        prob_delta = jnp.sum(prob_full * prob_slope, axis=-1, keepdims=True)
        score_grad = (prob_full * (prob_slope - prob_delta) * factor).astype(jnp.bfloat16)
        query_grad = jnp.einsum(
            "hqk,khd->qhd", score_grad, key_heads, preferred_element_type=jnp.float32
        ).reshape(-1, width)
        key_grad = jnp.einsum(
            "hqk,qhd->khd", score_grad, query_band, preferred_element_type=jnp.float32
        ).reshape(key_rows, ext_cols, width)
        value_grad = jnp.einsum(
            "hqk,qhd->khd", prob_low, grad_band, preferred_element_type=jnp.float32
        ).reshape(key_rows, ext_cols, width)
        grad_piece = jnp.concatenate([key_grad, value_grad], axis=-1)
        current = lax.dynamic_slice_in_dim(accumulated, band_first, key_rows, 0)
        return (
            lax.dynamic_update_slice_in_dim(accumulated, current + grad_piece, band_first, 0),
            query_grad,
        )

    start_grid = jnp.zeros((rows_dev + 2 * RADIUS, ext_cols, 2 * width), jnp.float32)
    accumulated, query_grads = lax.scan(
        backward_band, start_grid, jnp.arange(band_count, dtype=jnp.int32)
    )
    query_grads = query_grads.reshape(-1, width)
    rim_pair = jnp.concatenate(
        [accumulated[:, :RADIUS], accumulated[:, RADIUS + cols_dev :]], axis=1
    )
    beside = extended(rim_pair, (("col", 1),), RADIUS)
    inner_part = accumulated[:, RADIUS : RADIUS + cols_dev]
    inner_part = (
        inner_part.at[:, :RADIUS]
        .add(beside[:, :RADIUS])
        .at[:, cols_dev - RADIUS :]
        .add(beside[:, 3 * RADIUS :])
    )
    row_pair = jnp.concatenate([inner_part[:RADIUS], inner_part[RADIUS + rows_dev :]], axis=0)
    row_beside = extended(row_pair, (("row", 0),), RADIUS)
    inner_part = inner_part[RADIUS : RADIUS + rows_dev]
    inner_part = (
        inner_part.at[:RADIUS]
        .add(row_beside[:RADIUS])
        .at[rows_dev - RADIUS :]
        .add(row_beside[3 * RADIUS :])
    )
    packed_grad = jnp.concatenate([query_grads, inner_part.reshape(-1, 2 * width)], axis=1).astype(
        jnp.bfloat16
    )
    grad_tokens = (
        cotangent_rows.astype(jnp.float32)
        + lax.dot_general(
            packed_grad, packed_weight, (((1,), (1,)), ((), ())), preferred_element_type=jnp.float32
        )
    ).astype(jnp.bfloat16)
    packed_partial = lax.dot_general(
        token_rows, packed_grad, (((0,), (0,)), ((), ())), preferred_element_type=jnp.float32
    )
    packed_sum, output_sum = lax.psum((packed_partial, output_partial), ("row", "col"))
    return (
        layer_out.reshape(rows_dev, cols_dev, width),
        grad_tokens.reshape(rows_dev, cols_dev, width),
        packed_sum * total_scale,
        output_sum * total_scale,
    )


def solution(mesh):
    in_specs = (P("row", "col", None), P("row", "col"), P("row", "col", None), P(), P())
    out_specs = (P("row", "col", None), P("row", "col", None), P(), P())
    return jax.shard_map(
        per_device, mesh=mesh, in_specs=in_specs, out_specs=out_specs, check_vma=False
    )
```

profile of v0, /device:TPU:1, one launch (start us, length us, event | category | flops | bytes accessed | tf_op | source)
XLA Modules:
  0.0 790.8 jit_solution(2455933786183643482)
XLA Ops:
  30.1 6.9 collective-permute-start.2
  61.9 338.3 %while.39 = (s32[]{:T(128)}, f32[70,38,768]{2,1,0:T(8,128)}, bf16[8,256,384]{2,1,0:T(8,128)(2,1)}, s32[8]{0:T(128)S(1)}, bf16[64,32,384]{2,1,0:T(8,128)(2,1)}, /...) while((s32[]{:T(128)}, f32[70,38,768]{2,1,0:T(8,128)}, ...), condition=%wide.region_8.9_spmd.clone.clone.clone, body=%wide.region_4.8_spmd.clone.clone.sunk.clone | while | flops 541509952 | bytes 52770708 | solution.py:161
  82.9 6.9 fusion.166
  118.3 6.0 fusion.168
  125.1 6.9 fusion.166
  167.4 6.9 fusion.166
  209.6 6.9 fusion.166
  251.8 6.9 fusion.166
  294.0 6.9 fusion.166
  336.3 6.9 fusion.166
  378.5 6.9 fusion.166
  400.2 6.2 copy.56
  417.5 154.2 %while.38 = (s32[]{:T(128)}, f32[8,256,384]{2,1,0:T(8,128)}, s32[8]{0:T(128)S(1)}, bf16[70,38,768]{2,1,0:T(8,128)(2,1)}, s32[]{:T(128)}, /*index=5*/s32[70,38]{1...) while((s32[]{:T(128)}, f32[8,256,384]{2,1,0:T(8,128)}, ...), condition=%wide.region_3.4_spmd.clone.clone.clone, body=%wide.region_0.3_spmd.clone.clone.sunk.clone | while | flops 217096512 | bytes 24763208 | solution.py:110
  426.8 6.2 fusion.150
  446.1 6.2 fusion.150
  465.4 6.2 fusion.150
  484.6 6.2 fusion.150
  503.9 6.2 fusion.150
  523.1 6.2 fusion.150
  542.4 6.2 fusion.150
  561.7 6.2 fusion.150
  576.0 9.9 %scatter-add.14 = f32[70,32,768]{2,1,0:T(8,128)} dynamic-update-slice(f32[70,32,768]{2,1,0:T(8,128)} %slice.194, f32[70,3,768]{2,1,0:T(4,128)S(1)} %copy_add_fusion, s32[]{:T(128)} %constant.283.clone.1, s32[]{:T(128)} %constant.283.clone.1, s32[]{:T(128)} %constant.283.clone.1) | dynamic-update-slice | bytes 1290244 | tf_op jit(solution)/shard_map/scatter-add | solution.py:172
  587.9 9.2 %scatter-add.15 = f32[70,32,768]{2,1,0:T(8,128)} dynamic-update-slice(f32[70,32,768]{2,1,0:T(8,128)} %scatter-add.14, f32[70,3,768]{2,1,0:T(4,128)S(1)} %slice_add_fusion, s32[]{:T(128)} %constant.283.clone.1, s32[]{:T(128)} %constant.294.clone.1, s32[]{:T(128)} %constant.283.clone.1) | dynamic-update-slice | bytes 1290244 | tf_op jit(solution)/shard_map/scatter-add | solution.py:174
  628.5 150.6 %all-reduce.3.cloned.1.call-done = (f32[384,1152]{0,1:T(8,128)}, f32[384,384]{1,0:T(8,128)}) async-done(((f32[384,1152]{0,1:T(8,128)}, f32[384,384]{1,0:T(8,128)}), (f32[384,1152]{0,1:T(8,128)}, f32[384,384]{1,0:T(8,128)})) %all-reduce.3.cloned.1.call-update) | async-done | bytes 2359312 | tf_op jit(solution)/shard_map/psum | solution.py:197
  (596 shorter events, 469.1 us)
Async XLA Ops:
  7.2 771.9 %all-reduce.3.cloned.1.call-start = ((), (), s32[]{:S(2)}) async-start(), calls=%async_computation | async-start | bytes 4718592 | tf_op jit(solution)/shard_map/psum | solution.py:197
  8.3 9.8 %copy-start.14 = (s32[64,32]{0,1:T(8,128)S(1)}, s32[64,32]{0,1:T(8,128)}, u32[]{:S(2)}) copy-start(s32[64,32]{0,1:T(8,128)} %param.18) | copy-start | bytes 24580
  12.5 13.4 %copy-start.5 = (bf16[2048,1152]{1,0:T(8,128)(2,1)}, bf16[2048,1152]{1,0:T(8,128)(2,1)S(1)}, u32[]{:S(2)}) copy-start(bf16[2048,1152]{1,0:T(8,128)(2,1)S(1)} %convolution_convert_fusion) | copy-start | bytes 14155780
  12.6 13.6 %copy-start.9 = (bf16[64,32,384]{2,1,0:T(8,128)(2,1)S(1)}, bf16[64,32,384]{2,1,0:T(8,128)(2,1)}, u32[]{:S(2)}) copy-start(bf16[64,32,384]{2,1,0:T(8,128)(2,1)} %param.19) | copy-start | bytes 4718596
  12.6 13.6 %copy-start.15 = (bf16[384,384]{1,0:T(8,128)(2,1)S(1)}, bf16[384,384]{1,0:T(8,128)(2,1)}, u32[]{:S(2)}) copy-start(bf16[384,384]{1,0:T(8,128)(2,1)} %param.21) | copy-start | bytes 884740
  12.6 17.1 %collective-permute-start = (bf16[3,32,768]{2,1,0:T(8,128)(2,1)S(1)}, bf16[3,32,768]{2,1,0:T(8,128)(2,1)S(1)}, u32[]{:S(2)}, u32[]{:S(2)}) collective-permute-start(bf16[3,32,768]{2,1,0:T(8,128)(2,1)S(1)} %bitcast.152), channel_id=1, source_target_pairs={{0,16},{16,32},{32,48},{48,64},{64,80},{80,96},{96,112},{1,17},{17... | collective-permute-start | bytes 442376 | tf_op jit(solution)/shard_map/ppermute | solution.py:23
  16.8 12.9 %collective-permute-start.1 = (bf16[3,32,768]{2,1,0:T(8,128)(2,1)S(1)}, bf16[3,32,768]{2,1,0:T(8,128)(2,1)S(1)}, u32[]{:S(2)}, u32[]{:S(2)}) collective-permute-start(bf16[3,32,768]{2,1,0:T(8,128)(2,1)S(1)} %bitcast.151), channel_id=1, source_target_pairs={{16,0},{32,16},{48,32},{64,48},{80,64},{96,80},{112,96},{17,1},{33... | collective-permute-start | bytes 442376 | tf_op jit(solution)/shard_map/ppermute | solution.py:25
  18.8 20.1 %collective-permute-start.4 = (s32[3,32]{0,1:T(8,128)}, s32[3,32]{0,1:T(8,128)S(1)}, u32[]{:S(2)}, u32[]{:S(2)}) collective-permute-start(s32[3,32]{0,1:T(8,128)} %get-tuple-element.640), channel_id=1, source_target_pairs={{0,16},{16,32},{32,48},{48,64},{64,80},{80,96},{96,112},{1,17},{17... | collective-permute-start | bytes 1160 | tf_op jit(solution)/shard_map/ppermute | solution.py:23
  22.8 16.1 %collective-permute-start.5 = (s32[3,32]{0,1:T(8,128)}, s32[3,32]{0,1:T(8,128)}, u32[]{:S(2)}, u32[]{:S(2)}) collective-permute-start(s32[3,32]{0,1:T(8,128)} %get-tuple-element.641), channel_id=1, source_target_pairs={{16,0},{32,16},{48,32},{64,48},{80,64},{96,80},{112,96},{17,1},{33... | collective-permute-start | bytes 1160 | tf_op jit(solution)/shard_map/ppermute | solution.py:25
  30.1 22.1 %collective-permute-start.2 = (bf16[70,3,768]{2,1,0:T(4,128)(2,1)S(1)}, bf16[70,3,768]{2,1,0:T(4,128)(2,1)S(1)}, u32[]{:S(2)}, u32[]{:S(2)}) collective-permute-start(bf16[70,3,768]{2,1,0:T(4,128)(2,1)S(1)} %get-tuple-element.636), channel_id=1, source_target_pairs={{0,1},{1,2},{2,3},{3,4},{4,5},{5,6},{6,7},{7,8},{8,9},{9,10},{10,1... | collective-permute-start | bytes 967688 | tf_op jit(solution)/shard_map/ppermute | solution.py:23
  37.0 15.2 %collective-permute-start.3 = (bf16[70,3,768]{2,1,0:T(4,128)(2,1)S(1)}, bf16[70,3,768]{2,1,0:T(4,128)(2,1)S(1)}, u32[]{:S(2)}, u32[]{:S(2)}) collective-permute-start(bf16[70,3,768]{2,1,0:T(4,128)(2,1)S(1)} %get-tuple-element.637), channel_id=1, source_target_pairs={{1,0},{2,1},{3,2},{4,3},{5,4},{6,5},{7,6},{8,7},{9,8},{10,9},{11,1... | collective-permute-start | bytes 967688 | tf_op jit(solution)/shard_map/ppermute | solution.py:25
  39.7 10.5 %collective-permute-start.6 = (s32[70,3]{0,1:T(4,128)S(1)}, s32[70,3]{0,1:T(4,128)S(1)}, u32[]{:S(2)}, u32[]{:S(2)}) collective-permute-start(s32[70,3]{0,1:T(4,128)S(1)} %get-tuple-element.638), channel_id=1, source_target_pairs={{0,1},{1,2},{2,3},{3,4},{4,5},{5,6},{6,7},{7,8},{8,9},{9,10},{10,1... | collective-permute-start | bytes 2528 | tf_op jit(solution)/shard_map/ppermute | solution.py:23
  44.8 6.4 collective-permute-start.7
  67.8 5.0 copy-start.3
  152.3 5.0 copy-start.3
  236.7 5.0 copy-start.3
  279.0 5.0 copy-start.3
  363.4 5.0 copy-start.3
  400.2 6.2 copy-start.1
  411.4 162.4 %collective-permute-start.8 = (f32[70,3,768]{2,0,1:T(8,128)}, f32[70,3,768]{2,0,1:T(8,128)}, u32[]{:S(2)}, u32[]{:S(2)}) collective-permute-start(f32[70,3,768]{2,0,1:T(8,128)} %get-tuple-element.631), channel_id=1, source_target_pairs={{0,1},{1,2},{2,3},{3,4},{4,5},{5,6},{6,7},{7,8},{8,9},{9,10},{10,1... | collective-permute-start | bytes 1935368 | tf_op jit(solution)/shard_map/ppermute | solution.py:23
  415.5 170.3 %collective-permute-start.9 = (f32[70,3,768]{2,0,1:T(8,128)}, f32[70,3,768]{2,0,1:T(8,128)}, u32[]{:S(2)}, u32[]{:S(2)}) collective-permute-start(f32[70,3,768]{2,0,1:T(8,128)} %get-tuple-element.630), channel_id=1, source_target_pairs={{1,0},{2,1},{3,2},{4,3},{5,4},{6,5},{7,6},{8,7},{9,8},{10,9},{11,1... | collective-permute-start | bytes 1935368 | tf_op jit(solution)/shard_map/ppermute | solution.py:25
  417.5 154.2 %copy-start.19 = (f32[8,256]{1,0:T(8,128)S(1)}, f32[8,256]{1,0:T(8,128)}, u32[]{:S(2)}) copy-start(f32[8,256]{1,0:T(8,128)} %convert_element_type.72) | copy-start | bytes 24580
  598.2 12.6 %collective-permute-start.10 = (f32[3,32,768]{2,1,0:T(8,128)S(1)}, f32[3,32,768]{2,1,0:T(8,128)S(1)}, u32[]{:S(2)}, u32[]{:S(2)}) collective-permute-start(f32[3,32,768]{2,1,0:T(8,128)S(1)} %get-tuple-element.633), channel_id=1, source_target_pairs={{0,16},{16,32},{32,48},{48,64},{64,80},{80,96},{96,112},{1,17},{17... | collective-permute-start | bytes 884744 | tf_op jit(solution)/shard_map/ppermute | solution.py:23
  602.5 9.9 %collective-permute-start.11 = (f32[3,32,768]{2,1,0:T(8,128)S(1)}, f32[3,32,768]{2,1,0:T(8,128)S(1)}, u32[]{:S(2)}, u32[]{:S(2)}) collective-permute-start(f32[3,32,768]{2,1,0:T(8,128)S(1)} %get-tuple-element.632), channel_id=1, source_target_pairs={{16,0},{32,16},{48,32},{64,48},{80,64},{96,80},{112,96},{17,1},{33... | collective-permute-start | bytes 884744 | tf_op jit(solution)/shard_map/ppermute | solution.py:25
  (23 other events, 73.5 us)
Sparse Core Ops, SparseCore 0:
  619.5 159.5 all-reduce.2
where the time goes:
time: 800 us; the launch traced here: 791 us
  matrix products  234 us (29%)
  local copies, waits for them, and re-layouts  225 us (28%)
  waiting for transfers between devices  152 us (19%)
  other arithmetic  113 us (14%)
  starting transfers between devices  38.5 us (5%)
  between operations  14.9 us (2%)
  loops' own time  13.3 us (2%)
    psum x1, waiting for transfers between devices, per_device(): lax.psum((packed_partial, output_partial), ('row', 'col'))  151 us
    dot_general x8, matrix products, backward_band(): jnp.einsum('hqk,qhd->khd', score_grad, query_band, preferred_element_type...  54.9 us
    sub x8, other arithmetic, weights(): exp_terms = jnp.where(allowed[None], jnp.exp(scores - row_top), 0.0)  49.9 us
    dot_general x8, matrix products, backward_band(): jnp.einsum('hqk,khd->qhd', score_grad, key_heads, preferred_element_type=...  47.8 us
    dot_general x8, matrix products, backward_band(): jnp.einsum('hqk,qhd->khd', prob_low, grad_band, preferred_element_type=jn...  28.8 us
    ppermute x6, starting transfers between devices, extended(): lax.ppermute(tail, axis, [(i, (i + 1) % count) for i in range(ends)])  28.6 us
    dynamic_update_slice x8, other arithmetic, backward_band(): lax.dynamic_update_slice_in_dim(accumulated, current + grad_piece, band_f...  26.8 us
    sub x8, matrix products, weights(): exp_terms = jnp.where(allowed[None], jnp.exp(scores - row_top), 0.0)  25.2 us
  transfers between devices with their start and end apart: 13, of which 3 were waited for; matrix products, arithmetic and copies ran while one was open for 24% of the time, Pallas kernels for 0%

commit v1 on v0

v1 whole, which is shorter than its diff:
```python
import functools

import jax
import jax.numpy as jnp
from jax import lax
from jax.experimental import pallas as pl
from jax.experimental.pallas import tpu as pltpu
from jax.sharding import PartitionSpec as P

HEADS = 6
HEAD = 64
KERNEL = 7
RADIUS = 3
PAIR = 2 * HEAD
PAIRS = HEADS // 2
SIDE = 8
TILE_ROWS = 4
FACTOR = HEAD ** (-0.5)
NEG = float("-inf")
f32 = jnp.float32
bf16 = jnp.bfloat16


def dims(lhs, rhs):
    return (((lhs,), (rhs,)), ((), ()))


def attention_kernel(
    own_ref, side_ref, cot_ref, wp_ref, wo_ref, tis_own_ref, tis_side_ref, win_ref, self_ref, gate_ref,
    att_ref, dq_ref, dkv_own_ref, dkv_side_ref,
    q_s, g_s, kv_own_s, kv_side_s,
):
    rows_own, width = own_ref.shape
    rows_side = side_ref.shape[0]
    tokens_dev = cot_ref.shape[0]
    cols = (rows_own - tokens_dev) // (2 * RADIUS)
    halo = RADIUS * cols
    tile = TILE_ROWS * cols
    tiles = tokens_dev // tile
    own_keys = (TILE_ROWS + 2 * RADIUS) * cols
    side_keys = (TILE_ROWS + 2 * RADIUS) * SIDE

    kv_own_s[...] = jnp.dot(
        own_ref[...], wp_ref[:, width:], preferred_element_type=f32
    ).astype(bf16)
    kv_side_s[...] = jnp.dot(
        side_ref[...], wp_ref[:, width:], preferred_element_type=f32
    ).astype(bf16)
    q_s[...] = (
        jnp.dot(
            own_ref[halo : halo + tokens_dev, :], wp_ref[:, :width], preferred_element_type=f32
        ).astype(bf16)
        * FACTOR
    ).astype(bf16)
    g_s[...] = lax.dot_general(
        cot_ref[...], wo_ref[...], dims(1, 1), preferred_element_type=f32
    ).astype(bf16)
    dkv_own_ref[...] = jnp.zeros_like(dkv_own_ref)
    dkv_side_ref[...] = jnp.zeros_like(dkv_side_ref)

    first_head = lax.broadcasted_iota(jnp.int32, (tile, PAIR), 1) < HEAD

    def split(block):
        zero = jnp.zeros_like(block)
        return jnp.concatenate(
            [jnp.where(first_head, block, zero), jnp.where(first_head, zero, block)], axis=0
        )

    def joined(both):
        return jnp.concatenate([both[:HEAD, :tile], both[HEAD:, tile:]], axis=0).T

    def step(index, carry):
        q_at = pl.ds(pl.multiple_of(index * tile, tile), tile)
        own_at = pl.ds(pl.multiple_of(index * tile, tile), own_keys)
        side_at = pl.ds(pl.multiple_of(index * TILE_ROWS * SIDE, TILE_ROWS * SIDE), side_keys)
        kind = jnp.where(index == 0, 0, jnp.where(index == tiles - 1, 2, 1))
        tis_keys = jnp.concatenate([tis_own_ref[own_at, :], tis_side_ref[side_at, :]], axis=0)
        bias = jnp.maximum(tis_keys, self_ref[...]) + win_ref[kind]
        bias = jnp.concatenate([bias, bias], axis=1)
        gate = gate_ref[index]
        for pair in range(PAIRS):
            at = slice(pair * PAIR, (pair + 1) * PAIR)
            v_at = slice(width + pair * PAIR, width + (pair + 1) * PAIR)
            keys = jnp.concatenate([kv_own_s[own_at, at], kv_side_s[side_at, at]], axis=0)
            values = jnp.concatenate([kv_own_s[own_at, v_at], kv_side_s[side_at, v_at]], axis=0)
            query = split(q_s[q_at, at])
            grad = split(g_s[q_at, at])
            scores = lax.dot_general(keys, query, dims(1, 1), preferred_element_type=f32) + bias
            top = jnp.max(scores, axis=0, keepdims=True)
            terms = jnp.exp(scores - top)
            total = jnp.sum(terms, axis=0, keepdims=True)
            slope = lax.dot_general(values, grad, dims(1, 1), preferred_element_type=f32)
            inverse = 1.0 / total
            delta = jnp.sum(terms * slope, axis=0, keepdims=True) * inverse
            probs = terms * (inverse * gate)
            probs_low = probs.astype(bf16)
            score_grad = (probs * (slope - delta)).astype(bf16)
            mix = lax.dot_general(values, probs_low, dims(0, 0), preferred_element_type=f32)
            att_ref[q_at, at] = joined(mix).astype(bf16)
            dq = lax.dot_general(keys, score_grad, dims(0, 0), preferred_element_type=f32)
            dq_ref[q_at, at] = (joined(dq) * FACTOR).astype(bf16)
            dk = jnp.dot(score_grad, query, preferred_element_type=f32)
            dv = jnp.dot(probs_low, grad, preferred_element_type=f32)
            dkv_own_ref[own_at, at] += dk[:own_keys]
            dkv_side_ref[side_at, at] += dk[own_keys:]
            dkv_own_ref[own_at, v_at] += dv[:own_keys]
            dkv_side_ref[side_at, v_at] += dv[own_keys:]
        return carry

    lax.fori_loop(0, tiles, step, 0)


def attention(own, side, cot, wp, wo, tis_own, tis_side, win, self_bias, gate):
    tokens_dev, width = cot.shape
    vmem = pl.BlockSpec(memory_space=pltpu.VMEM)
    return pl.pallas_call(
        attention_kernel,
        out_shape=[
            jax.ShapeDtypeStruct((tokens_dev, width), bf16),
            jax.ShapeDtypeStruct((tokens_dev, width), bf16),
            jax.ShapeDtypeStruct((own.shape[0], 2 * width), f32),
            jax.ShapeDtypeStruct((side.shape[0], 2 * width), f32),
        ],
        in_specs=[vmem] * 10,
        out_specs=[vmem] * 4,
        scratch_shapes=[
            pltpu.VMEM((tokens_dev, width), bf16),
            pltpu.VMEM((tokens_dev, width), bf16),
            pltpu.VMEM((own.shape[0], 2 * width), bf16),
            pltpu.VMEM((side.shape[0], 2 * width), bf16),
        ],
        compiler_params=pltpu.CompilerParams(vmem_limit_bytes=56 * 1024 * 1024),
        name="attention",
    )(own, side, cot, wp, wo, tis_own, tis_side, win, self_bias, gate)


def to_next(array, axis):
    count = lax.axis_size(axis)
    return lax.ppermute(array, axis, [(i, (i + 1) % count) for i in range(count)])


def to_last(array, axis):
    count = lax.axis_size(axis)
    return lax.ppermute(array, axis, [((i + 1) % count, i) for i in range(count)])


def total_over_devices(partial):
    axes = ("row", "col")
    count = lax.axis_size("row") * lax.axis_size("col")
    rows, cols = partial.shape
    pieces = partial.astype(bf16).reshape(count, rows * cols // count // 128, 128)
    pieces = lax.all_to_all(pieces, axes, 0, 0, tiled=True)
    mine = jnp.sum(pieces.astype(f32), axis=0).astype(bf16)
    copies = jnp.broadcast_to(mine[None], (count,) + mine.shape)
    whole = lax.all_to_all(copies, axes, 0, 0, tiled=True)
    return whole.astype(f32).reshape(rows, cols)


def mask_parts(rows_dev, cols_dev):
    row_base = lax.axis_index("row") * rows_dev
    col_base = lax.axis_index("col") * cols_dev
    grid_rows = rows_dev * lax.axis_size("row")
    grid_cols = cols_dev * lax.axis_size("col")
    key_rows = TILE_ROWS + 2 * RADIUS
    far = -(2 ** 20)
    side_cols = [i - RADIUS for i in range(RADIUS)] + [cols_dev + i for i in range(RADIUS)]
    side_cols += [far] * (SIDE - len(side_cols))
    col_own = jnp.tile(jnp.arange(cols_dev, dtype=jnp.int32), key_rows)
    col_side = jnp.tile(jnp.array(side_cols, jnp.int32), key_rows)
    key_col = jnp.concatenate([col_own, col_side])
    row_ids = jnp.arange(key_rows, dtype=jnp.int32) - RADIUS
    key_row = jnp.concatenate([jnp.repeat(row_ids, cols_dev), jnp.repeat(row_ids, SIDE)])
    query_col = jnp.tile(jnp.arange(cols_dev, dtype=jnp.int32), TILE_ROWS)
    query_row = jnp.repeat(jnp.arange(TILE_ROWS, dtype=jnp.int32), cols_dev)
    same = (key_col[:, None] == query_col[None, :]) & (key_row[:, None] == query_row[None, :])
    self_bias = jnp.where(same, 0.0, NEG).astype(f32)

    def inside(key, query, base, extent):
        start = jnp.clip(base + query - RADIUS, 0, extent - KERNEL)
        offset = (base + key)[:, None] - start[None, :]
        return (offset >= 0) & (offset < KERNEL)

    col_in = inside(key_col, query_col, col_base, grid_cols)
    kinds = []
    for first in (0, 2 * TILE_ROWS, rows_dev - TILE_ROWS):
        row_in = inside(key_row, query_row, row_base + first, grid_rows)
        kinds.append(jnp.where(col_in & row_in, 0.0, NEG).astype(f32))
    return jnp.stack(kinds), self_bias


def per_device(tokens, tissue, cotangent, packed_weight, output_weight):
    rows_dev, cols_dev, width = tokens.shape
    ext_rows = rows_dev + 2 * RADIUS
    total_scale = float(rows_dev * lax.axis_size("row") * cols_dev * lax.axis_size("col")) ** (-0.5)
    token_rows = tokens.reshape(-1, width)
    cotangent_rows = cotangent.reshape(-1, width)

    with_tissue = lambda a, b: jnp.concatenate([a, b.astype(bf16)[..., None]], axis=-1)
    above = to_next(with_tissue(tokens[-RADIUS:], tissue[-RADIUS:]), "row")
    below = to_last(with_tissue(tokens[:RADIUS], tissue[:RADIUS]), "row")
    left_cols = with_tissue(tokens[:, :RADIUS], tissue[:, :RADIUS])
    right_cols = with_tissue(tokens[:, -RADIUS:], tissue[:, -RADIUS:])
    left_cols = jnp.concatenate([above[:, :RADIUS], left_cols, below[:, :RADIUS]], axis=0)
    right_cols = jnp.concatenate([above[:, -RADIUS:], right_cols, below[:, -RADIUS:]], axis=0)
    from_left = to_next(right_cols, "col")
    from_right = to_last(left_cols, "col")
    pad = jnp.zeros((ext_rows, SIDE - 2 * RADIUS, width + 1), bf16)
    side = jnp.concatenate([from_left, from_right, pad], axis=1).reshape(-1, width + 1)
    own = jnp.concatenate([above[..., :width], tokens, below[..., :width]], axis=0).reshape(
        -1, width
    )
    tis_own = jnp.concatenate([above[..., width], tissue.astype(bf16), below[..., width]], axis=0)

    def lanes(mask):
        bias = jnp.where(mask.reshape(-1, 1) > 0.5, 0.0, NEG).astype(f32)
        return jnp.broadcast_to(bias, (bias.shape[0], TILE_ROWS * cols_dev))

    win, self_bias = mask_parts(rows_dev, cols_dev)
    gate = tissue.reshape(-1, 1, TILE_ROWS * cols_dev).astype(f32)
    gate = jnp.concatenate([gate, gate], axis=2)
    side_tokens = side[:, :width]
    attended, dq, dkv_own, dkv_side = attention(
        own, side_tokens, cotangent_rows, packed_weight, output_weight,
        lanes(tis_own), lanes(side[:, width]), win, self_bias, gate,
    )

    contract = functools.partial(lax.dot_general, preferred_element_type=f32)
    output_partial = contract(attended, cotangent_rows, dims(0, 0))
    q_partial = contract(token_rows, dq, dims(0, 0))
    kv_partial = contract(own, dkv_own.astype(bf16), dims(0, 0)) + contract(
        side_tokens, dkv_side.astype(bf16), dims(0, 0)
    )
    partial = jnp.concatenate([q_partial, kv_partial, output_partial], axis=1)

    dkv_side = dkv_side.reshape(ext_rows, SIDE, 2 * width)
    dkv_own = dkv_own.reshape(ext_rows, cols_dev, 2 * width)
    to_left = to_last(dkv_side[:, :RADIUS].astype(bf16), "col")
    to_right = to_next(dkv_side[:, RADIUS : 2 * RADIUS].astype(bf16), "col")
    middle = jnp.zeros((ext_rows, cols_dev - 2 * RADIUS, 2 * width), bf16)
    dkv_own = dkv_own + jnp.concatenate([to_right, middle, to_left], axis=1).astype(f32)
    to_above = to_last(dkv_own[:RADIUS].astype(bf16), "row")
    to_below = to_next(dkv_own[-RADIUS:].astype(bf16), "row")
    middle = jnp.zeros((rows_dev - 2 * RADIUS, cols_dev, 2 * width), bf16)
    dkv = dkv_own[RADIUS:-RADIUS] + jnp.concatenate([to_below, middle, to_above], axis=0).astype(f32)
    dkv = dkv.astype(bf16).reshape(-1, 2 * width)

    layer_out = (
        token_rows.astype(f32) + jnp.dot(attended, output_weight, preferred_element_type=f32)
    ).astype(bf16)
    grad_tokens = (
        cotangent_rows.astype(f32)
        + contract(dq, packed_weight[:, :width], dims(1, 1))
        + contract(dkv, packed_weight[:, width:], dims(1, 1))
    ).astype(bf16)
    sums = total_over_devices(partial) * total_scale
    return (
        layer_out.reshape(rows_dev, cols_dev, width),
        grad_tokens.reshape(rows_dev, cols_dev, width),
        sums[:, : 3 * width],
        sums[:, 3 * width :],
    )


def solution(mesh):
    in_specs = (P("row", "col", None), P("row", "col"), P("row", "col", None), P(), P())
    out_specs = (P("row", "col", None), P("row", "col", None), P(), P())
    return jax.shard_map(
        per_device, mesh=mesh, in_specs=in_specs, out_specs=out_specs, check_vma=False
    )
```

time: 800 us -> 170 us (0.21); the launches traced: 791 us -> 170 us
  matrix products: 234 us -> 20.6 us
  local copies, waits for them, and re-layouts: 225 us -> 21.7 us
  waiting for transfers between devices: 152 us -> 36.5 us
  other arithmetic: 113 us -> 17.2 us
  Pallas kernels: 0 us -> 44.4 us
  between operations: 14.9 us -> 1.01 us
  loops' own time: 13.3 us -> 0 us
  starting transfers between devices: 38.5 us -> 28.4 us
    dot_general x54 -> x7, matrix products: 208 us -> 20.6 us  [the longest x1 4.6 us: per_device(): contract(own, dkv_own.astype(bf16), dims(0, 0))]
    psum x1 -> x0, waiting for transfers between devices: 151 us -> none  [per_device(): lax.psum((packed_partial, output_partial), ('row', 'col'))]
    sub x8 -> x1, other arithmetic: 49.9 us -> 0.01 us  [mask_parts(): row_ids = jnp.arange(key_rows, dtype=jnp.int32) - RADIUS]
    dynamic_slice x48 -> x0, local copies, waits for them, and re-layouts: 46.4 us -> none  [the longest x16 19.5 us: band_inputs(): lax.dynamic_slice_in_dim(halo_pairs, band_first, key_rows, 0)]
    pallas_call x0 -> x1, Pallas kernels: none -> 44.4 us  [attention(): pl.pallas_call(attention_kernel, out_shape=[jax.ShapeDtypeStruct((tokens_...]
    reshape x72 -> x1, local copies, waits for them, and re-layouts: 38.7 us -> 0.08 us  [mask_parts(): query_row = jnp.repeat(jnp.arange(TILE_ROWS, dtype=jnp.int32), cols_dev)]
    transpose x16 -> x0, local copies, waits for them, and re-layouts: 37 us -> none  [the longest x8 18.5 us: backward_band(): jnp.einsum('hqk,qhd->khd', score_grad, query_band, preferred_element_type...]
    dynamic_update_slice x8 -> x0, other arithmetic: 26.8 us -> none  [backward_band(): lax.dynamic_update_slice_in_dim(accumulated, current + grad_piece, band_f...]
  transfers between devices with their start and end apart: 13 -> 10, of which waited for: 3 -> 5; matrix products, arithmetic and copies ran while one was open for 24% -> 17% of each run, Pallas kernels for 0% -> 0%
where the time goes in v1:
time: 170 us
  Pallas kernels  44.4 us (26%)
  waiting for transfers between devices  36.5 us (21%)
  starting transfers between devices  28.4 us (17%)
  local copies, waits for them, and re-layouts  21.7 us (13%)
  matrix products  20.6 us (12%)
  other arithmetic  17.2 us (10%)
    pallas_call x1, Pallas kernels, attention(): pl.pallas_call(attention_kernel, out_shape=[jax.ShapeDtypeStruct((tokens_...  44.4 us
    ppermute x4, waiting for transfers between devices, to_next(): lax.ppermute(array, axis, [(i, (i + 1) % count) for i in range(count)])  20 us
    all_to_all x1, waiting for transfers between devices, total_over_devices(): whole = lax.all_to_all(copies, axes, 0, 0, tiled=True)  11.7 us
    ppermute x4, starting transfers between devices, to_next(): lax.ppermute(array, axis, [(i, (i + 1) % count) for i in range(count)])  11 us
    all_to_all x1, starting transfers between devices, total_over_devices(): pieces = lax.all_to_all(pieces, axes, 0, 0, tiled=True)  6.72 us
    ppermute x4, starting transfers between devices, to_last(): lax.ppermute(array, axis, [((i + 1) % count, i) for i in range(count)])  5.53 us
    all_to_all x1, starting transfers between devices, total_over_devices(): whole = lax.all_to_all(copies, axes, 0, 0, tiled=True)  5.11 us
    ppermute x4, waiting for transfers between devices, to_last(): lax.ppermute(array, axis, [((i + 1) % count, i) for i in range(count)])  4.83 us
  transfers between devices with their start and end apart: 10, of which 5 were waited for; matrix products, arithmetic and copies ran while one was open for 17% of the time, Pallas kernels for 0%

profile of v1, /device:TPU:1, one launch (start us, length us, event | category | flops | bytes accessed | tf_op | source)
XLA Modules:
  0.0 169.8 jit_solution(15592372967603798454)
XLA Ops:
  2.8 2.1 %collective-permute-start = (bf16[3,32,385]{2,1,0:T(8,128)(2,1)S(1)}, bf16[3,32,385]{2,1,0:T(8,128)(2,1)S(1)}, u32[]{:S(2)}, u32[]{:S(2)}) collective-permute-start(bf16[3,32,385]{2,1,0:T(8,128)(2,1)S(1)} %pad_maximum_fusion.5), channel_id=1, source_target_pairs={{0,16},{16,32},{32,48},{48,64},{64,80},{80,96},{96,112},{112,0},{1... | collective-permute-start | bytes 221768 | tf_op jit(solution)/shard_map/ppermute | solution.py:139
  5.3 2.7 %collective-permute-start.1 = (bf16[3,32,385]{2,1,0:T(8,128)(2,1)S(1)}, bf16[3,32,385]{2,1,0:T(8,128)(2,1)S(1)}, u32[]{:S(2)}, u32[]{:S(2)}) collective-permute-start(bf16[3,32,385]{2,1,0:T(8,128)(2,1)S(1)} %pad_maximum_fusion.6), channel_id=1, source_target_pairs={{16,0},{32,16},{48,32},{64,48},{80,64},{96,80},{112,96},{0,112},{1... | collective-permute-start | bytes 221768 | tf_op jit(solution)/shard_map/ppermute | solution.py:144
  14.3 4.5 %collective-permute-start.2 = (bf16[70,3,385]{2,0,1:T(8,128)(2,1)S(1)}, bf16[70,3,385]{2,0,1:T(8,128)(2,1)S(1)}, u32[]{:S(2)}, u32[]{:S(2)}) collective-permute-start(bf16[70,3,385]{2,0,1:T(8,128)(2,1)S(1)} %pad_maximum_fusion.3), channel_id=1, source_target_pairs={{0,1},{1,2},{2,3},{3,4},{4,5},{5,6},{6,7},{7,8},{8,9},{9,10},{10,1... | collective-permute-start | bytes 485108 | tf_op jit(solution)/shard_map/ppermute | solution.py:139
  21.4 2.7 %collective-permute-done.2 = bf16[70,3,385]{2,0,1:T(8,128)(2,1)S(1)} collective-permute-done((bf16[70,3,385]{2,0,1:T(8,128)(2,1)S(1)}, bf16[70,3,385]{2,0,1:T(8,128)(2,1)S(1)}, u32[]{:S(2)}, u32[]{:S(2)}) %collective-permute-start.2) | collective-permute-done | bytes 161732 | tf_op jit(solution)/shard_map/ppermute | solution.py:139
  24.1 1.9 %collective-permute-done.3 = bf16[70,3,385]{2,0,1:T(8,128)(2,1)S(1)} collective-permute-done((bf16[70,3,385]{2,0,1:T(8,128)(2,1)S(1)}, bf16[70,3,385]{2,0,1:T(8,128)(2,1)S(1)}, u32[]{:S(2)}, u32[]{:S(2)}) %collective-permute-start.3) | collective-permute-done | bytes 161732 | tf_op jit(solution)/shard_map/ppermute | solution.py:144
  29.5 44.4 %attention.1 = (bf16[2048,384]{1,0:T(8,128)(2,1)}, bf16[2048,384]{1,0:T(8,128)(2,1)}, f32[2240,768]{1,0:T(8,128)}, f32[560,768]{1,0:T(8,128)}) custom-call(bf16[2240,384]{1,0:T(8,128)(2,1)} %bitcast.40, bf16[560,384]{1,0:T(8,128)(2,1)} %slice.126.side_ref, bf16[2048,384]{1,0:T(8,128)(2,1)} %bitcast.42, bf16[384,1152]{1,0:T(8,128)(2,1)} %wp_ref.1, ...), custom_call_target="tpu_custom_call" | custom-call | tf_op jit(solution)/shard_map/attention/pallas_call | solution.py:116
  73.9 3.2 %fusion.11 = f32[384,768]{1,0:T(8,128)} fusion(f32[560,768]{1,0:T(8,128)} %get-tuple-element.11, bf16[560,385]{1,0:T(8,128)(2,1)S(1)} %bitcast.47), kind=kOutput, calls=%fused_computation.19 | convolution fusion | flops 330731520 | bytes 3330048 | tf_op jit(solution)/shard_map/dot_general | solution.py:230
  80.3 2.6 %convolution_convert_fusion = bf16[384,384]{1,0:T(8,128)(2,1)S(1)} fusion(bf16[2048,384]{1,0:T(8,128)(2,1)S(1)} %copy-done.7, bf16[2048,384]{1,0:T(8,128)(2,1)} %bitcast.43), kind=kOutput, calls=%fused_computation.11 | convolution fusion | flops 604127232 | bytes 3440640 | tf_op jit(solution)/shard_map/dot_general | solution.py:228
  82.9 4.6 %fusion.6 = bf16[384,768]{1,0:T(8,128)(2,1)S(1)} fusion(f32[384,768]{1,0:T(8,128)S(1)} %copy-done.10, bf16[2240,384]{1,0:T(8,128)(2,1)S(1)} %bitcast.41, f32[2240,768]{1,0:T(8,128)} %get-tuple-element.10), kind=kOutput, calls=%fused_computation.10 | convolution fusion | flops 1323515904 | bytes 10371072 | tf_op jit(solution)/shard_map/dot_general | solution.py:230
  87.6 2.3 %convert_element_type.71 = bf16[128,36,128]{2,1,0:T(8,128)(2,1)} reshape(bf16[384,1536]{1,0:T(8,128)(2,1)S(1)} %pad_maximum_fusion.1) | data formatting | bytes 2359296 | tf_op jit(solution)/shard_map/convert_element_type | solution.py:151
  89.9 6.7 %all-to-all-start = ((bf16[128,36,128]{2,1,0:T(8,128)(2,1)}), bf16[128,36,128]{2,1,0:T(8,128)(2,1)}, u32[]{:S(2)}, u32[]{:S(2)}) async-start(bf16[128,36,128]{2,1,0:T(8,128)(2,1)} %convert_element_type.71), calls=%async_computation | async-start | bytes 2621440 | tf_op jit(solution)/shard_map/all_to_all | solution.py:152
  96.9 3.6 %collective-permute-start.4 = (bf16[70,3,768]{2,1,0:T(4,128)(2,1)S(1)}, bf16[70,3,768]{2,1,0:T(4,128)(2,1)S(1)}, u32[]{:S(2)}, u32[]{:S(2)}) collective-permute-start(bf16[70,3,768]{2,1,0:T(4,128)(2,1)S(1)} %get-tuple-element.24), channel_id=1, source_target_pairs={{0,1},{1,2},{2,3},{3,4},{4,5},{5,6},{6,7},{7,8},{8,9},{9,10},{10,1... | collective-permute-start | bytes 967688 | tf_op jit(solution)/shard_map/ppermute | solution.py:139
  100.5 4.0 %fusion.13 = f32[2048,384]{1,0:T(8,128)} fusion(bf16[2048,384]{1,0:T(8,128)(2,1)S(1)} %copy-done.4, bf16[384,1152]{1,0:T(8,128)(2,1)} %wp_ref.1), kind=kOutput, calls=%fused_computation.30 | convolution fusion | flops 603979776 | bytes 5013504 | tf_op jit(solution)/shard_map/dot_general | solution.py:252
  104.5 17.3 %collective-permute-done.4 = bf16[70,3,768]{2,1,0:T(4,128)(2,1)S(1)} collective-permute-done((bf16[70,3,768]{2,1,0:T(4,128)(2,1)S(1)}, bf16[70,3,768]{2,1,0:T(4,128)(2,1)S(1)}, u32[]{:S(2)}, u32[]{:S(2)}) %collective-permute-start.4) | collective-permute-done | bytes 322592 | tf_op jit(solution)/shard_map/ppermute | solution.py:139
  121.8 2.9 %collective-permute-done.5 = bf16[70,3,768]{2,1,0:T(4,128)(2,1)S(1)} collective-permute-done((bf16[70,3,768]{2,1,0:T(4,128)(2,1)S(1)}, bf16[70,3,768]{2,1,0:T(4,128)(2,1)S(1)}, u32[]{:S(2)}, u32[]{:S(2)}) %collective-permute-start.5) | collective-permute-done | bytes 322592 | tf_op jit(solution)/shard_map/ppermute | solution.py:144
  124.8 3.5 %fusion.26 = (bf16[70,32,768]{2,1,0:T(8,128)(2,1)S(1)}, f32[70,32,768]{2,1,0:T(8,128)}) fusion(f32[70,32,768]{2,1,0:T(8,128)S(1)} %bitcast.37, bf16[70,3,768]{2,1,0:T(4,128)(2,1)S(1)} %collective-permute-done.5, bf16[32]{0:T(256)(128)(2,1)S(1)} %pad.7.clone, bf16[70,3,768]{2,1,0:T(4,128)(2,1)S(1)} %collective-permute-done.4), kind=kLoop, calls=%fused_computation.66 | loop fusion | flops 13762560 | bytes 17848384 | tf_op jit(solution)/shard_map/convert.6
  129.8 2.8 %collective-permute-start.7 = (bf16[3,32,768]{2,1,0:T(8,128)(2,1)}, bf16[3,32,768]{2,1,0:T(8,128)(2,1)}, u32[]{:S(2)}, u32[]{:S(2)}) collective-permute-start(bf16[3,32,768]{2,1,0:T(8,128)(2,1)} %get-tuple-element.19), channel_id=1, source_target_pairs={{16,0},{32,16},{48,32},{64,48},{80,64},{96,80},{112,96},{0,112},{1... | collective-permute-start | bytes 442376 | tf_op jit(solution)/shard_map/ppermute | solution.py:144
  135.4 5.1 %all-to-all-start.1 = ((bf16[128,36,128]{2,1,0:T(8,128)(2,1)}), bf16[128,36,128]{2,1,0:T(8,128)(2,1)}, u32[]{:S(2)}, u32[]{:S(2)}) async-start(bf16[128,36,128]{2,1,0:T(8,128)(2,1)} %broadcast_in_dim.119), calls=%async_computation.1 | async-start | bytes 2621440 | tf_op jit(solution)/shard_map/all_to_all | solution.py:155
  140.5 2.2 %add_convert_fusion.1 = bf16[2048,384]{1,0:T(8,128)(2,1)} fusion(bf16[2048,384]{1,0:T(8,128)(2,1)S(1)} %bitcast.39, bf16[2048,384]{1,0:T(8,128)(2,1)S(1)} %copy-done.8, bf16[384,384]{1,0:T(8,128)(2,1)S(1)} %copy-done.13), kind=kOutput, calls=%fused_computation.6 | convolution fusion | flops 606339072 | bytes 5013504 | tf_op jit(solution)/shard_map/dot_general | solution.py:248
  142.8 3.9 %fusion = bf16[64,32,768]{2,1,0:T(8,128)(2,1)S(1)} fusion(f32[70,32,768]{2,1,0:T(8,128)} %get-tuple-element.13, bf16[3,32,768]{2,1,0:T(8,128)(2,1)} %collective-permute-done.7, bf16[3,32,768]{2,1,0:T(8,128)(2,1)} %collective-permute-done.6, bf16[64]{0:T(256)(128)(2,1)S(1)} %pad.4.clone), kind=kLoop, calls=%fused_computation.2 | loop fusion | flops 7864320 | bytes 9732224 | tf_op jit(solution)/shard_map/convert_element_type | solution.py:245
  147.3 3.0 %add_convert_fusion = bf16[2048,384]{1,0:T(8,128)(2,1)} fusion(f32[2048,384]{1,0:T(8,128)S(1)} %copy-done.5, bf16[2048,384]{1,0:T(8,128)(2,1)S(1)} %bitcast.44, bf16[2048,768]{1,0:T(8,128)(2,1)S(1)} %bitcast.48, bf16[384,1152]{1,0:T(8,128)(2,1)S(1)} %copy-done.12), kind=kOutput, calls=%fused_computation.5 | convolution fusion | flops 1211105280 | bytes 10027008 | tf_op jit(solution)/shard_map/dot_general | solution.py:253
  150.3 11.7 %all-to-all-done.1 = bf16[128,36,128]{2,1,0:T(8,128)(2,1)} async-done(((bf16[128,36,128]{2,1,0:T(8,128)(2,1)}), bf16[128,36,128]{2,1,0:T(8,128)(2,1)}, u32[]{:S(2)}, u32[]{:S(2)}) %all-to-all-start.1) | async-done | bytes 1179680 | tf_op jit(solution)/shard_map/all_to_all | solution.py:155
  165.1 2.8 %slice.135 = f32[384,1152]{1,0:T(8,128)} slice(f32[384,1536]{1,0:T(8,128)} %mul.19), slice={[0:384], [0:1152]} | slice | bytes 3538944 | tf_op jit(solution)/shard_map/slice | solution.py:259
  167.9 1.9 %slice.136 = f32[384,384]{1,0:T(8,128)} slice(f32[384,1536]{1,0:T(8,128)} %mul.19), slice={[0:384], [1152:1536]} | slice | bytes 1179648 | tf_op jit(solution)/shard_map/slice | solution.py:260
  (116 shorter events, 26.3 us)
Async XLA Ops:
  2.8 11.3 %collective-permute-start = (bf16[3,32,385]{2,1,0:T(8,128)(2,1)S(1)}, bf16[3,32,385]{2,1,0:T(8,128)(2,1)S(1)}, u32[]{:S(2)}, u32[]{:S(2)}) collective-permute-start(bf16[3,32,385]{2,1,0:T(8,128)(2,1)S(1)} %pad_maximum_fusion.5), channel_id=1, source_target_pairs={{0,16},{16,32},{32,48},{48,64},{64,80},{80,96},{96,112},{112,0},{1... | collective-permute-start | bytes 221768 | tf_op jit(solution)/shard_map/ppermute | solution.py:139
  5.3 8.9 %collective-permute-start.1 = (bf16[3,32,385]{2,1,0:T(8,128)(2,1)S(1)}, bf16[3,32,385]{2,1,0:T(8,128)(2,1)S(1)}, u32[]{:S(2)}, u32[]{:S(2)}) collective-permute-start(bf16[3,32,385]{2,1,0:T(8,128)(2,1)S(1)} %pad_maximum_fusion.6), channel_id=1, source_target_pairs={{16,0},{32,16},{48,32},{64,48},{80,64},{96,80},{112,96},{0,112},{1... | collective-permute-start | bytes 221768 | tf_op jit(solution)/shard_map/ppermute | solution.py:144
  12.3 7.6 %copy-start = (bf16[64,32,384]{2,1,0:T(8,128)(2,1)S(1)}, bf16[64,32,384]{2,1,0:T(8,128)(2,1)}, u32[]{:S(2)}) copy-start(bf16[64,32,384]{2,1,0:T(8,128)(2,1)} %param.6) | copy-start | bytes 4718596
  14.3 9.8 %collective-permute-start.2 = (bf16[70,3,385]{2,0,1:T(8,128)(2,1)S(1)}, bf16[70,3,385]{2,0,1:T(8,128)(2,1)S(1)}, u32[]{:S(2)}, u32[]{:S(2)}) collective-permute-start(bf16[70,3,385]{2,0,1:T(8,128)(2,1)S(1)} %pad_maximum_fusion.3), channel_id=1, source_target_pairs={{0,1},{1,2},{2,3},{3,4},{4,5},{5,6},{6,7},{7,8},{8,9},{9,10},{10,1... | collective-permute-start | bytes 485108 | tf_op jit(solution)/shard_map/ppermute | solution.py:139
  18.9 7.1 %collective-permute-start.3 = (bf16[70,3,385]{2,0,1:T(8,128)(2,1)S(1)}, bf16[70,3,385]{2,0,1:T(8,128)(2,1)S(1)}, u32[]{:S(2)}, u32[]{:S(2)}) collective-permute-start(bf16[70,3,385]{2,0,1:T(8,128)(2,1)S(1)} %pad_maximum_fusion.4), channel_id=1, source_target_pairs={{1,0},{2,1},{3,2},{4,3},{5,4},{6,5},{7,6},{8,7},{9,8},{10,9},{11,1... | collective-permute-start | bytes 485108 | tf_op jit(solution)/shard_map/ppermute | solution.py:144
  73.9 3.3 %copy-start.6 = (f32[560,768]{1,0:T(8,128)S(1)}, f32[560,768]{1,0:T(8,128)}, u32[]{:S(2)}) copy-start(f32[560,768]{1,0:T(8,128)} %get-tuple-element.11) | copy-start | bytes 5160964
  80.3 2.6 %copy-start.2 = (bf16[70,32,384]{2,1,0:T(8,128)(2,1)S(1)}, bf16[70,32,384]{2,1,0:T(8,128)(2,1)}, u32[]{:S(2)}) copy-start(bf16[70,32,384]{2,1,0:T(8,128)(2,1)} %pad_maximum_fusion) | copy-start | bytes 5160964
  80.3 2.6 %copy-start.10 = (f32[384,768]{1,0:T(8,128)S(1)}, f32[384,768]{1,0:T(8,128)}, u32[]{:S(2)}) copy-start(f32[384,768]{1,0:T(8,128)} %fusion.11) | copy-start | bytes 3538948
  87.6 9.1 %copy-start.11 = (bf16[70,8,768]{2,1,0:T(8,128)(2,1)S(1)}, bf16[70,8,768]{2,1,0:T(8,128)(2,1)}, u32[]{:S(2)}) copy-start(bf16[70,8,768]{2,1,0:T(8,128)(2,1)} %convert_bitcast_fusion) | copy-start | bytes 2580484
  89.9 34.9 %slice-start = ((s8[6881280]{0:T(1024)(128)(4,1)}), s8[2686976]{0:T(1024)(128)(4,1)S(1)}, s32[]{:S(2)}) async-start(s8[6881280]{0:T(1024)(128)(4,1)} %bitcast.35), calls=%async_computation.2 | async-start | bytes 5373952
  89.9 42.7 %all-to-all-start = ((bf16[128,36,128]{2,1,0:T(8,128)(2,1)}), bf16[128,36,128]{2,1,0:T(8,128)(2,1)}, u32[]{:S(2)}, u32[]{:S(2)}) async-start(bf16[128,36,128]{2,1,0:T(8,128)(2,1)} %convert_element_type.71), calls=%async_computation | async-start | bytes 2621440 | tf_op jit(solution)/shard_map/all_to_all | solution.py:152
  96.6 3.9 %copy-start.4 = (bf16[2048,384]{1,0:T(8,128)(2,1)S(1)}, bf16[2048,384]{1,0:T(8,128)(2,1)}, u32[]{:S(2)}) copy-start(bf16[2048,384]{1,0:T(8,128)(2,1)} %get-tuple-element.9) | copy-start | bytes 4718596
  96.9 24.9 %collective-permute-start.4 = (bf16[70,3,768]{2,1,0:T(4,128)(2,1)S(1)}, bf16[70,3,768]{2,1,0:T(4,128)(2,1)S(1)}, u32[]{:S(2)}, u32[]{:S(2)}) collective-permute-start(bf16[70,3,768]{2,1,0:T(4,128)(2,1)S(1)} %get-tuple-element.24), channel_id=1, source_target_pairs={{0,1},{1,2},{2,3},{3,4},{4,5},{5,6},{6,7},{7,8},{8,9},{9,10},{10,1... | collective-permute-start | bytes 967688 | tf_op jit(solution)/shard_map/ppermute | solution.py:139
  100.5 24.2 %slice-start.1 = ((s8[6881280]{0:T(1024)(128)(4,1)}), s8[4194304]{0:T(1024)(128)(4,1)S(1)}, s32[]{:S(2)}) async-start(s8[6881280]{0:T(1024)(128)(4,1)} %bitcast.35), calls=%async_computation.3 | async-start | bytes 8388608
  100.5 24.2 %collective-permute-start.5 = (bf16[70,3,768]{2,1,0:T(4,128)(2,1)S(1)}, bf16[70,3,768]{2,1,0:T(4,128)(2,1)S(1)}, u32[]{:S(2)}, u32[]{:S(2)}) collective-permute-start(bf16[70,3,768]{2,1,0:T(4,128)(2,1)S(1)} %get-tuple-element.25), channel_id=1, source_target_pairs={{1,0},{2,1},{3,2},{4,3},{5,4},{6,5},{7,6},{8,7},{9,8},{10,9},{11,1... | collective-permute-start | bytes 967688 | tf_op jit(solution)/shard_map/ppermute | solution.py:144
  129.0 13.8 %collective-permute-start.6 = (bf16[3,32,768]{2,1,0:T(8,128)(2,1)}, bf16[3,32,768]{2,1,0:T(8,128)(2,1)}, u32[]{:S(2)}, u32[]{:S(2)}) collective-permute-start(bf16[3,32,768]{2,1,0:T(8,128)(2,1)} %get-tuple-element.18), channel_id=1, source_target_pairs={{0,16},{16,32},{32,48},{48,64},{64,80},{80,96},{96,112},{112,0},{1... | collective-permute-start | bytes 442376 | tf_op jit(solution)/shard_map/ppermute | solution.py:139
  129.8 13.0 %collective-permute-start.7 = (bf16[3,32,768]{2,1,0:T(8,128)(2,1)}, bf16[3,32,768]{2,1,0:T(8,128)(2,1)}, u32[]{:S(2)}, u32[]{:S(2)}) collective-permute-start(bf16[3,32,768]{2,1,0:T(8,128)(2,1)} %get-tuple-element.19), channel_id=1, source_target_pairs={{16,0},{32,16},{48,32},{64,48},{80,64},{96,80},{112,96},{0,112},{1... | collective-permute-start | bytes 442376 | tf_op jit(solution)/shard_map/ppermute | solution.py:144
  134.1 6.4 %copy-start.1 = (bf16[64,32,384]{2,1,0:T(8,128)(2,1)S(1)}, bf16[64,32,384]{2,1,0:T(8,128)(2,1)}, u32[]{:S(2)}) copy-start(bf16[64,32,384]{2,1,0:T(8,128)(2,1)} %param.6) | copy-start | bytes 4718596
  134.1 6.4 %copy-start.8 = (bf16[2048,384]{1,0:T(8,128)(2,1)S(1)}, bf16[2048,384]{1,0:T(8,128)(2,1)}, u32[]{:S(2)}) copy-start(bf16[2048,384]{1,0:T(8,128)(2,1)} %get-tuple-element.8) | copy-start | bytes 4718596
  134.1 6.4 %copy-start.13 = (bf16[384,384]{1,0:T(8,128)(2,1)S(1)}, bf16[384,384]{1,0:T(8,128)(2,1)}, u32[]{:S(2)}) copy-start(bf16[384,384]{1,0:T(8,128)(2,1)} %wo_ref.1) | copy-start | bytes 884740
  135.4 26.6 %all-to-all-start.1 = ((bf16[128,36,128]{2,1,0:T(8,128)(2,1)}), bf16[128,36,128]{2,1,0:T(8,128)(2,1)}, u32[]{:S(2)}, u32[]{:S(2)}) async-start(bf16[128,36,128]{2,1,0:T(8,128)(2,1)} %broadcast_in_dim.119), calls=%async_computation.1 | async-start | bytes 2621440 | tf_op jit(solution)/shard_map/all_to_all | solution.py:155
  142.8 4.0 %copy-start.5 = (f32[2048,384]{1,0:T(8,128)S(1)}, f32[2048,384]{1,0:T(8,128)}, u32[]{:S(2)}) copy-start(f32[2048,384]{1,0:T(8,128)} %fusion.13) | copy-start | bytes 9437188
  142.8 4.3 %copy-start.9 = (bf16[64,32,384]{2,1,0:T(8,128)(2,1)S(1)}, bf16[64,32,384]{2,1,0:T(8,128)(2,1)}, u32[]{:S(2)}) copy-start(bf16[64,32,384]{2,1,0:T(8,128)(2,1)} %param.8) | copy-start | bytes 4718596
  142.8 4.5 %copy-start.12 = (bf16[384,1152]{1,0:T(8,128)(2,1)S(1)}, bf16[384,1152]{1,0:T(8,128)(2,1)}, u32[]{:S(2)}) copy-start(bf16[384,1152]{1,0:T(8,128)(2,1)} %wp_ref.1) | copy-start | bytes 2654212
  (2 other events, 3.1 us)

commit v2 on v1

v2 whole, which is shorter than its diff:
```python
import functools

import jax
import jax.numpy as jnp
from jax import lax
from jax.experimental import pallas as pl
from jax.experimental.pallas import tpu as pltpu
from jax.sharding import PartitionSpec as P

HEADS = 6
HEAD = 64
KERNEL = 7
RADIUS = 3
PAIR = 2 * HEAD
PAIRS = HEADS // 2
SIDE = 8
TILE_ROWS = 4
KEY_ROWS = TILE_ROWS + 2 * RADIUS
CHUNK = 80
FACTOR = HEAD ** (-0.5)
NEG = float("-inf")
MIB = 1024 * 1024
f32 = jnp.float32
bf16 = jnp.bfloat16


def dims(lhs, rhs):
    return (((lhs,), (rhs,)), ((), ()))


def attention_kernel(
    extents,
    above_ref, below_ref, side_ref, tok_hbm, cot_hbm, wp_ref, wo_ref, base_ref, tissue_ref,
    att_hbm, dq_hbm, dkv_own_hbm, to_left_ref, to_right_ref, part_ref,
    tok_ref, cot_ref, q_ref, g_ref, tok_t_ref, att_ref, dq_ref, dkv_own_ref, dkv_side_ref,
    kv_own_s, kv_side_s, tis_own_s, tis_side_s, bias_s, win_ref, self_ref, att_t_s, acc_own, acc_side, sems, *stage,
):
    tokens_dev, width = q_ref.shape
    halo = above_ref.shape[0]
    rows_own = tokens_dev + 2 * halo
    cols = halo // RADIUS
    tile = TILE_ROWS * cols
    tiles = tokens_dev // tile
    own_keys = rows_own - tokens_dev + tile
    side_keys = KEY_ROWS * SIDE
    keys_all = own_keys + side_keys
    x_s, dp_s, top_s, pl_s, sg_s = (stage[i * PAIRS : (i + 1) * PAIRS] for i in range(5))

    middle = pl.ds(halo, tokens_dev)
    early = [
        pltpu.make_async_copy(tok_hbm, tok_ref, sems.at[0]),
        pltpu.make_async_copy(cot_hbm, cot_ref, sems.at[1]),
    ]
    for copy in early:
        copy.start()

    def lanes(column):
        bias = jnp.where(column.astype(f32) > 0.5, 0.0, NEG)
        return jnp.broadcast_to(bias, (bias.shape[0], tile))

    def outer(rows_ref):
        return jnp.dot(
            rows_ref[:, :width], wp_ref[:, width:], preferred_element_type=f32
        ).astype(bf16)

    kv_own_s[:halo] = outer(above_ref)
    kv_own_s[halo + tokens_dev :] = outer(below_ref)
    kv_side_s[...] = outer(side_ref)
    tis_own_s[:halo] = lanes(above_ref[:, width : width + 1])
    tis_own_s[halo + tokens_dev :] = lanes(below_ref[:, width : width + 1])
    tis_side_s[...] = lanes(side_ref[:, width : width + 1])
    lane = lax.broadcasted_iota(jnp.int32, (1, tile), 1)
    query_row = sum((lane >= i * cols).astype(jnp.int32) for i in range(1, TILE_ROWS))
    query_col = lane - query_row * cols

    def window(key, query, base, extent):
        start = jnp.clip(base + query - RADIUS, 0, extent - KERNEL) - base
        return jnp.where((key >= start) & (key < start + KERNEL), 0.0, NEG)

    own_col = lax.broadcasted_iota(jnp.int32, (cols, tile), 0)
    side_col = lax.broadcasted_iota(jnp.int32, (SIDE, tile), 0) - RADIUS
    side_col = jnp.where(side_col < 0, side_col, side_col + cols)
    side_col = jnp.where(side_col < cols + RADIUS, side_col, -(2**20))
    own_in = window(own_col, query_col, base_ref[1], extents[1])
    side_in = window(side_col, query_col, base_ref[1], extents[1])
    own_same = jnp.where(own_col == query_col, 0.0, NEG)
    for key_row in range(KEY_ROWS):
        own_rows = slice(key_row * cols, (key_row + 1) * cols)
        side_rows = slice(own_keys + key_row * SIDE, own_keys + (key_row + 1) * SIDE)
        for kind, first in enumerate((0, 2 * TILE_ROWS, (tiles - 1) * TILE_ROWS)):
            row_in = window(key_row - RADIUS, query_row, base_ref[0] + first, extents[0])
            win_ref[kind, own_rows] = own_in + row_in
            win_ref[kind, side_rows] = side_in + row_in
        row_same = jnp.where(query_row == key_row - RADIUS, 0.0, NEG)
        self_ref[own_rows] = own_same + row_same
        self_ref[side_rows] = jnp.full((SIDE, tile), NEG, f32)
    for index in range(tiles):
        across = jnp.broadcast_to(tissue_ref[index].astype(f32), (tile, tile)).T
        rows = slice(halo + index * tile, halo + (index + 1) * tile)
        tis_own_s[rows] = jnp.where(across > 0.5, 0.0, NEG)
    for copy in early:
        copy.wait()
    kv_own_s[middle] = outer(tok_ref)
    q = jnp.dot(tok_ref[...], wp_ref[:, :width], preferred_element_type=f32).astype(bf16)
    q_ref[...] = (q * FACTOR).astype(bf16)
    g_ref[...] = lax.dot_general(
        cot_ref[...], wo_ref[...], dims(1, 1), preferred_element_type=f32
    ).astype(bf16)
    tok_t_ref[...] = tok_ref[...].T
    seen_own = own_keys - tile
    seen_side = side_keys - TILE_ROWS * SIDE
    acc_own[:seen_own] = jnp.zeros((seen_own, 2 * width), f32)
    acc_side[:seen_side] = jnp.zeros((seen_side, 2 * width), f32)
    pl_s[-1][...] = jnp.zeros((keys_all, 2 * tile), bf16)
    sg_s[-1][...] = jnp.zeros((keys_all, 2 * tile), bf16)

    first_head = lax.broadcasted_iota(jnp.int32, (tile, PAIR), 1) < HEAD

    def split(block):
        zero = jnp.zeros_like(block)
        return jnp.concatenate(
            [jnp.where(first_head, block, zero), jnp.where(first_head, zero, block)], axis=0
        )

    def joined(both):
        return jnp.concatenate([both[:HEAD, :tile], both[HEAD:, tile:]], axis=0)

    def places(index, base, size, step):
        return pl.ds(pl.multiple_of(index * step, step) + base, size)

    def q_at(index):
        return places(index, 0, tile, tile)

    def own_at(index, base=0, size=own_keys):
        return places(index, base, size, tile)

    def side_at(index, base=0, size=side_keys):
        return places(index, base, size, TILE_ROWS * SIDE)

    def pair_cols(pair):
        return slice(pair * PAIR, (pair + 1) * PAIR), slice(
            width + pair * PAIR, width + (pair + 1) * PAIR
        )

    def key_rows(index, at):
        return jnp.concatenate([kv_own_s[own_at(index), at], kv_side_s[side_at(index), at]], axis=0)

    def make_bias(index):
        kind = jnp.where(index == 0, 0, jnp.where(index == tiles - 1, 2, 1))
        tis_keys = jnp.concatenate([tis_own_s[own_at(index)], tis_side_s[side_at(index)]], axis=0)
        bias_s[...] = jnp.maximum(tis_keys, self_ref[...]) + win_ref[kind]

    def score_stage(index, pair):
        k_at, v_at = pair_cols(pair)
        bias = bias_s[...]
        scores = lax.dot_general(
            key_rows(index, k_at), split(q_ref[q_at(index), k_at]), dims(1, 1),
            preferred_element_type=f32,
        ) + jnp.concatenate([bias, bias], axis=1)
        x_s[pair][...] = scores
        top_s[pair][...] = jnp.max(scores, axis=0, keepdims=True)
        dp_s[pair][...] = lax.dot_general(
            key_rows(index, v_at), split(g_ref[q_at(index), k_at]), dims(1, 1),
            preferred_element_type=f32,
        )

    def softmax_stage(index, pair):
        top = top_s[pair][...]
        total = jnp.zeros((8, 2 * tile), f32)
        inner = jnp.zeros((8, 2 * tile), f32)
        fold = lambda a: jnp.sum(a.reshape(CHUNK // 8, 8, 2 * tile), axis=0)
        for begin in range(0, keys_all, CHUNK):
            at = slice(begin, begin + CHUNK)
            terms = jnp.exp(x_s[pair][at] - top)
            x_s[pair][at] = terms
            total = total + fold(terms)
            inner = inner + fold(terms * dp_s[pair][at])
        inverse = 1.0 / jnp.sum(total, axis=0, keepdims=True)
        delta = jnp.sum(inner, axis=0, keepdims=True) * inverse
        gate = tissue_ref[index].astype(f32)
        weight = inverse * jnp.concatenate([gate, gate], axis=1)
        for begin in range(0, keys_all, CHUNK):
            at = slice(begin, begin + CHUNK)
            probs = x_s[pair][at] * weight
            pl_s[pair][at] = probs.astype(bf16)
            sg_s[pair][at] = (probs * (dp_s[pair][at] - delta)).astype(bf16)

    def product_stage(index, pair):
        k_at, v_at = pair_cols(pair)
        keys = key_rows(index, k_at)
        values = key_rows(index, v_at)
        probs_low = pl_s[pair][...]
        score_grad = sg_s[pair][...]
        mix = joined(
            lax.dot_general(values, probs_low, dims(0, 0), preferred_element_type=f32)
        )
        att_t_s[k_at, q_at(index)] = mix.astype(bf16)
        att_ref[q_at(index), k_at] = mix.T.astype(bf16)
        dq = joined(lax.dot_general(keys, score_grad, dims(0, 0), preferred_element_type=f32))
        dq_ref[q_at(index), k_at] = (dq.T * FACTOR).astype(bf16)
        dk = jnp.dot(score_grad, split(q_ref[q_at(index), k_at]), preferred_element_type=f32)
        dv = jnp.dot(probs_low, split(g_ref[q_at(index), k_at]), preferred_element_type=f32)
        for grad, at in ((dk, k_at), (dv, v_at)):
            acc_own[own_at(index, 0, seen_own), at] += grad[:seen_own]
            acc_own[own_at(index, seen_own, tile), at] = grad[seen_own:own_keys]
            acc_side[side_at(index, 0, seen_side), at] += grad[own_keys : own_keys + seen_side]
            acc_side[side_at(index, seen_side, TILE_ROWS * SIDE), at] = grad[own_keys + seen_side :]

    make_bias(0)
    score_stage(0, 0)

    def step(index, carry):
        for pair in range(PAIRS):
            if pair + 1 < PAIRS:
                score_stage(index, pair + 1)
            else:
                later = jnp.minimum(index + 1, tiles - 1)
                make_bias(later)
                score_stage(later, 0)
            softmax_stage(index, pair)
            if pair > 0:
                product_stage(index, pair - 1)
            else:
                product_stage(jnp.maximum(index - 1, 0), PAIRS - 1)
        return carry

    lax.fori_loop(0, tiles, step, 0)
    product_stage(tiles - 1, PAIRS - 1)

    dkv_own_ref[...] = acc_own[...].astype(bf16)
    dkv_side_ref[...] = acc_side[...].astype(bf16)
    results = [
        pltpu.make_async_copy(source, target, sems.at[2 + i])
        for i, (source, target) in enumerate(
            [
                (dkv_own_ref, dkv_own_hbm),
                (att_ref, att_hbm),
                (dq_ref, dq_hbm),
            ]
        )
    ]
    for copy in results:
        copy.start()
    send_row = lax.broadcasted_iota(jnp.int32, (to_left_ref.shape[0], dkv_side_ref.shape[0]), 0)
    side_row = lax.broadcasted_iota(jnp.int32, send_row.shape, 1)
    for begin, send_ref in ((0, to_left_ref), (RADIUS, to_right_ref)):
        place = (send_row // (SIDE // 2)) * SIDE + send_row % (SIDE // 2) + begin
        pick = jnp.where(side_row == place, 1.0, 0.0).astype(bf16)
        send_ref[...] = jnp.dot(pick, dkv_side_ref[...], preferred_element_type=f32).astype(bf16)
    outside = jnp.concatenate(
        [above_ref[:, :width], below_ref[:, :width], side_ref[:, :width]], axis=0
    )

    def put(block, value):
        value = value.astype(bf16)
        for i in range(value.shape[1] // 128):
            part_ref[(block + i) * width : (block + i + 1) * width] = value[
                :, i * 128 : (i + 1) * 128
            ]

    columns = width // 128
    put(0, jnp.dot(tok_t_ref[...], dq_ref[...], preferred_element_type=f32))
    for begin in range(0, 2 * width, 256):
        at = slice(begin, begin + 256)
        grad_outside = jnp.concatenate(
            [dkv_own_ref[:halo, at], dkv_own_ref[halo + tokens_dev :, at], dkv_side_ref[:, at]],
            axis=0,
        )
        put(
            columns + begin // 128,
            jnp.dot(
                tok_t_ref[...],
                dkv_own_ref[halo : halo + tokens_dev, at],
                preferred_element_type=f32,
            )
            + lax.dot_general(outside, grad_outside, dims(0, 0), preferred_element_type=f32),
        )
    put(3 * columns, jnp.dot(att_t_s[...], cot_ref[...], preferred_element_type=f32))
    used = 4 * width * columns
    if used < part_ref.shape[0]:
        part_ref[used:] = jnp.zeros((part_ref.shape[0] - used, 128), bf16)
    for copy in results:
        copy.wait()


def attention(above, below, side, tok, cot, wp, wo, base, tissue, extents, rows_part):
    tokens_dev, width = cot.shape
    rows_own = tokens_dev + 2 * above.shape[0]
    rows_side = side.shape[0]
    tile = tissue.shape[2]
    keys_all = rows_own - tokens_dev + tile + KEY_ROWS * SIDE
    rows_send = -(-rows_side // 32) * 16
    vmem = pl.BlockSpec(memory_space=pltpu.VMEM)
    hbm = pl.BlockSpec(memory_space=pl.ANY)
    smem = pl.BlockSpec(memory_space=pltpu.SMEM)
    stage = []
    for shape, kind in (
        ((keys_all, 2 * tile), f32),
        ((keys_all, 2 * tile), f32),
        ((1, 2 * tile), f32),
        ((keys_all, 2 * tile), bf16),
        ((keys_all, 2 * tile), bf16),
    ):
        stage += [pltpu.VMEM(shape, kind)] * PAIRS
    return pl.pallas_call(
        functools.partial(attention_kernel, extents),
        out_shape=[
            jax.ShapeDtypeStruct((tokens_dev, width), bf16),
            jax.ShapeDtypeStruct((tokens_dev, width), bf16),
            jax.ShapeDtypeStruct((rows_own, 2 * width), bf16),
            jax.ShapeDtypeStruct((rows_send, 2 * width), bf16),
            jax.ShapeDtypeStruct((rows_send, 2 * width), bf16),
            jax.ShapeDtypeStruct((rows_part, 128), bf16),
        ],
        in_specs=[vmem] * 3 + [hbm] * 2 + [vmem] * 2 + [smem, vmem],
        out_specs=[hbm] * 3 + [vmem] * 3,
        scratch_shapes=[
            pltpu.VMEM((tokens_dev, width), bf16),
            pltpu.VMEM((tokens_dev, width), bf16),
            pltpu.VMEM((tokens_dev, width), bf16),
            pltpu.VMEM((tokens_dev, width), bf16),
            pltpu.VMEM((width, tokens_dev), bf16),
            pltpu.VMEM((tokens_dev, width), bf16),
            pltpu.VMEM((tokens_dev, width), bf16),
            pltpu.VMEM((rows_own, 2 * width), bf16),
            pltpu.VMEM((rows_side, 2 * width), bf16),
            pltpu.VMEM((rows_own, 2 * width), bf16),
            pltpu.VMEM((rows_side, 2 * width), bf16),
            pltpu.VMEM((rows_own, tile), f32),
            pltpu.VMEM((rows_side, tile), f32),
            pltpu.VMEM((keys_all, tile), f32),
            pltpu.VMEM((3, keys_all, tile), f32),
            pltpu.VMEM((keys_all, tile), f32),
            pltpu.VMEM((width, tokens_dev), bf16),
            pltpu.VMEM((rows_own, 2 * width), f32),
            pltpu.VMEM((rows_side, 2 * width), f32),
            pltpu.SemaphoreType.DMA((5,)),
        ]
        + stage,
        compiler_params=pltpu.CompilerParams(vmem_limit_bytes=56 * MIB),
        name="attention",
    )(above, below, side, tok, cot, wp, wo, base, tissue)


def to_next(array, axis):
    count = lax.axis_size(axis)
    return lax.ppermute(array, axis, [(i, (i + 1) % count) for i in range(count)])


def to_last(array, axis):
    count = lax.axis_size(axis)
    return lax.ppermute(array, axis, [((i + 1) % count, i) for i in range(count)])


def sum_kernel(pieces, pieces_ref, copies_ref):
    rows = pieces_ref.shape[0] // pieces
    pair = 2 * rows
    total = jnp.zeros((pair, 128), f32)
    for i in range(pieces // 2):
        total = total + pieces_ref[i * pair : (i + 1) * pair].astype(f32)
    total = total[:rows] + total[rows:]
    total = jnp.concatenate([total, total], axis=0).astype(bf16)
    for i in range(pieces // 2):
        copies_ref[i * pair : (i + 1) * pair] = total


def summed_copies(pieces, count):
    return pl.pallas_call(
        functools.partial(sum_kernel, count),
        out_shape=jax.ShapeDtypeStruct(pieces.shape, bf16),
        compiler_params=pltpu.CompilerParams(vmem_limit_bytes=16 * MIB),
        name="summed_copies",
    )(pieces)


def total_over_devices(partial):
    axes = ("row", "col")
    count = lax.axis_size("row") * lax.axis_size("col")
    pieces = lax.all_to_all(partial.reshape(count, -1, 128), axes, 0, 0, tiled=True)
    copies = summed_copies(pieces.reshape(partial.shape), count).reshape(pieces.shape)
    return lax.all_to_all(copies, axes, 0, 0, tiled=True).reshape(partial.shape)


def unpack_kernel(scale, whole_ref, packed_ref, output_ref):
    width = output_ref.shape[0]
    for block in range((packed_ref.shape[1] + output_ref.shape[1]) // 128):
        value = whole_ref[block * width : (block + 1) * width].astype(f32) * scale
        column = block * 128
        if column < packed_ref.shape[1]:
            packed_ref[:, column : column + 128] = value
        else:
            column -= packed_ref.shape[1]
            output_ref[:, column : column + 128] = value


def unpack(whole, width, scale):
    return pl.pallas_call(
        functools.partial(unpack_kernel, scale),
        out_shape=[
            jax.ShapeDtypeStruct((width, 3 * width), f32),
            jax.ShapeDtypeStruct((width, width), f32),
        ],
        compiler_params=pltpu.CompilerParams(vmem_limit_bytes=24 * MIB),
        name="unpack",
    )(whole)


def per_device(tokens, tissue, cotangent, packed_weight, output_weight):
    rows_dev, cols_dev, width = tokens.shape
    ext_rows = rows_dev + 2 * RADIUS
    devices = lax.axis_size("row") * lax.axis_size("col")
    rows_part = -(-4 * width * (width // 128) // (8 * devices)) * 8 * devices
    tile = TILE_ROWS * cols_dev
    total_scale = float(rows_dev * lax.axis_size("row") * cols_dev * lax.axis_size("col")) ** (-0.5)
    token_rows = tokens.reshape(-1, width)
    cotangent_rows = cotangent.reshape(-1, width)

    with_tissue = lambda a, b: jnp.concatenate([a, b.astype(bf16)[..., None]], axis=-1)
    above = to_next(with_tissue(tokens[-RADIUS:], tissue[-RADIUS:]), "row")
    below = to_last(with_tissue(tokens[:RADIUS], tissue[:RADIUS]), "row")
    left_cols = with_tissue(tokens[:, :RADIUS], tissue[:, :RADIUS])
    right_cols = with_tissue(tokens[:, -RADIUS:], tissue[:, -RADIUS:])
    left_cols = jnp.concatenate([above[:, :RADIUS], left_cols, below[:, :RADIUS]], axis=0)
    right_cols = jnp.concatenate([above[:, -RADIUS:], right_cols, below[:, -RADIUS:]], axis=0)
    from_left = to_next(right_cols, "col")
    from_right = to_last(left_cols, "col")
    pad = jnp.zeros((ext_rows, SIDE - 2 * RADIUS, width + 1), bf16)
    side = jnp.concatenate([from_left, from_right, pad], axis=1).reshape(-1, width + 1)

    base = jnp.stack([lax.axis_index("row") * rows_dev, lax.axis_index("col") * cols_dev])
    attended, dq, dkv_own, to_left, to_right, partial = attention(
        above.reshape(-1, width + 1), below.reshape(-1, width + 1), side,
        token_rows, cotangent_rows, packed_weight, output_weight,
        base.astype(jnp.int32), tissue.reshape(-1, 1, tile),
        (rows_dev * lax.axis_size("row"), cols_dev * lax.axis_size("col")), rows_part,
    )

    half = SIDE // 2

    def columns(sent):
        return sent[: ext_rows * half].reshape(ext_rows, half, 2 * width)[:, :RADIUS]

    from_right = columns(to_last(to_left, "col"))
    from_left = columns(to_next(to_right, "col"))
    dkv_own = dkv_own.reshape(ext_rows, cols_dev, 2 * width)
    first, last, inner = slice(None, RADIUS), slice(-RADIUS, None), slice(RADIUS, -RADIUS)

    def with_columns(rows):
        between = jnp.zeros((dkv_own[rows].shape[0], cols_dev - 2 * RADIUS, 2 * width), bf16)
        beside = jnp.concatenate([from_left[rows], between, from_right[rows]], axis=1)
        return dkv_own[rows].astype(f32) + beside.astype(f32)

    from_below = to_last(with_columns(first).astype(bf16), "row")
    from_above = to_next(with_columns(last).astype(bf16), "row")
    between = jnp.zeros((rows_dev - 2 * RADIUS, cols_dev, 2 * width), bf16)
    beside = jnp.concatenate([from_above, between, from_below], axis=0)
    dkv = with_columns(inner) + beside.astype(f32)
    dkv = dkv.astype(bf16).reshape(-1, 2 * width)

    contract = functools.partial(lax.dot_general, preferred_element_type=f32)
    layer_out = (
        token_rows.astype(f32) + jnp.dot(attended, output_weight, preferred_element_type=f32)
    ).astype(bf16)
    grad_tokens = (
        cotangent_rows.astype(f32)
        + contract(dq, packed_weight[:, :width], dims(1, 1))
        + contract(dkv, packed_weight[:, width:], dims(1, 1))
    ).astype(bf16)
    grad_packed, grad_output = unpack(total_over_devices(partial), width, total_scale)
    return (
        layer_out.reshape(rows_dev, cols_dev, width),
        grad_tokens.reshape(rows_dev, cols_dev, width),
        grad_packed,
        grad_output,
    )


def solution(mesh):
    in_specs = (P("row", "col", None), P("row", "col"), P("row", "col", None), P(), P())
    out_specs = (P("row", "col", None), P("row", "col", None), P(), P())
    return jax.shard_map(
        per_device, mesh=mesh, in_specs=in_specs, out_specs=out_specs, check_vma=False
    )
```

time: 170 us -> 128 us (0.75)
  other arithmetic: 17.2 us -> 2.93 us
  local copies, waits for them, and re-layouts: 21.7 us -> 10.3 us
  matrix products: 20.6 us -> 11.4 us
  waiting for transfers between devices: 36.5 us -> 28.7 us
  starting transfers between devices: 28.4 us -> 32.8 us
  Pallas kernels: 44.4 us -> 40.5 us
    ppermute x4, waiting for transfers between devices: 20 us -> 1.37 us  [to_next(): lax.ppermute(array, axis, [(i, (i + 1) % count) for i in range(count)])]
    dot_general x4 -> x0, matrix products: 11.4 us -> none  [the longest x1 4.6 us: per_device(): contract(own, dkv_own.astype(bf16), dims(0, 0))]
    all_to_all x2, waiting for transfers between devices: 11.7 us -> 22.9 us  [the longest x1 14 us: total_over_devices(): return lax.all_to_all(copies, axes, 0, 0, tiled=True).reshape(partial.shape)]
    all_to_all x2, starting transfers between devices: 11.8 us -> 18.7 us  [the longest x1 12.6 us: total_over_devices(): lax.all_to_all(partial.reshape(count, -1, 128), axes, 0, 0, tiled=True)]
    convert_element_type x2 -> x1, other arithmetic: 4.73 us -> 0.14 us  [per_device(): from_above = to_next(with_columns(last).astype(bf16), 'row')]
    another operation x3 -> x2, other arithmetic: 5.41 us -> 1.38 us
    pallas_call x1 -> x3, Pallas kernels: 44.4 us -> 40.5 us  [the longest x1 37.7 us: attention(): pl.pallas_call(functools.partial(attention_kernel, extents), out_shape=[j...]
    broadcast_in_dim x8 -> x2, local copies, waits for them, and re-layouts: 3.61 us -> 0.01 us  [the longest x1 0.01 us: with_columns(): jnp.zeros((dkv_own[rows].shape[0], cols_dev - 2 * RADIUS, 2 * width), bf16)]
  transfers between devices with their start and end apart: 10 -> 10, of which waited for: 5 -> 5; matrix products, arithmetic and copies ran while one was open for 17% -> 16% of each run, Pallas kernels for 0% -> 1%
where the time goes in v2:
time: 128 us
  Pallas kernels  40.5 us (32%)
  starting transfers between devices  32.8 us (26%)
  waiting for transfers between devices  28.7 us (22%)
  matrix products  11.4 us (9%)
  local copies, waits for them, and re-layouts  10.3 us (8%)
  other arithmetic  2.93 us (2%)
    pallas_call x1, Pallas kernels, attention(): pl.pallas_call(functools.partial(attention_kernel, extents), out_shape=[j...  37.7 us
    all_to_all x1, waiting for transfers between devices, total_over_devices(): return lax.all_to_all(copies, axes, 0, 0, tiled=True).reshape(partial.shape)  14 us
    all_to_all x1, starting transfers between devices, total_over_devices(): lax.all_to_all(partial.reshape(count, -1, 128), axes, 0, 0, tiled=True)  12.6 us
    all_to_all x1, waiting for transfers between devices, total_over_devices(): lax.all_to_all(partial.reshape(count, -1, 128), axes, 0, 0, tiled=True)  8.93 us
    ppermute x4, starting transfers between devices, to_next(): lax.ppermute(array, axis, [(i, (i + 1) % count) for i in range(count)])  8.24 us
    all_to_all x1, starting transfers between devices, total_over_devices(): return lax.all_to_all(copies, axes, 0, 0, tiled=True).reshape(partial.shape)  6.1 us
    ppermute x4, starting transfers between devices, to_last(): lax.ppermute(array, axis, [((i + 1) % count, i) for i in range(count)])  5.82 us
    dot_general x1, matrix products, per_device(): contract(dkv, packed_weight[:, width:], dims(1, 1))  5.21 us
  transfers between devices with their start and end apart: 10, of which 5 were waited for; matrix products, arithmetic and copies ran while one was open for 16% of the time, Pallas kernels for 1%

profile of v2, /device:TPU:1, one launch (start us, length us, event | category | flops | bytes accessed | tf_op | source)
XLA Modules:
  0.0 127.7 jit_solution(17223600467247081302)
XLA Ops:
  1.8 0.9 fusion.15
  2.8 2.1 %collective-permute-start = (bf16[3,32,385]{2,1,0:T(8,128)(2,1)S(1)}, bf16[3,32,385]{2,1,0:T(8,128)(2,1)S(1)}, u32[]{:S(2)}, u32[]{:S(2)}) collective-permute-start(bf16[3,32,385]{2,1,0:T(8,128)(2,1)S(1)} %pad_maximum_fusion.4), channel_id=1, source_target_pairs={{0,16},{16,32},{32,48},{48,64},{64,80},{80,96},{96,112},{112,0},{1... | collective-permute-start | bytes 221768 | tf_op jit(solution)/shard_map/ppermute | solution.py:347
  5.3 2.7 %collective-permute-start.1 = (bf16[3,32,385]{2,1,0:T(8,128)(2,1)S(1)}, bf16[3,32,385]{2,1,0:T(8,128)(2,1)S(1)}, u32[]{:S(2)}, u32[]{:S(2)}) collective-permute-start(bf16[3,32,385]{2,1,0:T(8,128)(2,1)S(1)} %pad_maximum_fusion.5), channel_id=1, source_target_pairs={{16,0},{32,16},{48,32},{64,48},{80,64},{96,80},{112,96},{0,112},{1... | collective-permute-start | bytes 221768 | tf_op jit(solution)/shard_map/ppermute | solution.py:352
  8.0 1.3 fusion.14
  10.2 4.6 %collective-permute-start.2 = (bf16[70,3,385]{2,0,1:T(8,128)(2,1)S(1)}, bf16[70,3,385]{2,0,1:T(8,128)(2,1)S(1)}, u32[]{:S(2)}, u32[]{:S(2)}) collective-permute-start(bf16[70,3,385]{2,0,1:T(8,128)(2,1)S(1)} %pad_maximum_fusion.2), channel_id=1, source_target_pairs={{0,1},{1,2},{2,3},{3,4},{4,5},{5,6},{6,7},{7,8},{8,9},{9,10},{10,1... | collective-permute-start | bytes 485108 | tf_op jit(solution)/shard_map/ppermute | solution.py:347
  16.8 0.9 collective-permute-done.2
  17.7 4.5 %collective-permute-done.3 = bf16[70,3,385]{2,0,1:T(8,128)(2,1)S(1)} collective-permute-done((bf16[70,3,385]{2,0,1:T(8,128)(2,1)S(1)}, bf16[70,3,385]{2,0,1:T(8,128)(2,1)S(1)}, u32[]{:S(2)}, u32[]{:S(2)}) %collective-permute-start.3) | collective-permute-done | bytes 161732 | tf_op jit(solution)/shard_map/ppermute | solution.py:352
  22.3 1.0 copy.89
  23.3 37.7 %attention.1 = (bf16[2048,384]{1,0:T(8,128)(2,1)}, bf16[2048,384]{1,0:T(8,128)(2,1)}, bf16[2240,768]{1,0:T(8,128)(2,1)}, bf16[288,768]{1,0:T(8,128)(2,1)}, bf16[...) custom-call(bf16[96,385]{1,0:T(8,128)(2,1)} %bitcast.48, bf16[96,385]{1,0:T(8,128)(2,1)} %bitcast.49, ...), custom_call_target="tpu_custom_call" | custom-call | tf_op jit(solution)/shard_map/attention/pallas_call | solution.py:305
  61.6 12.6 %all-to-all-start = ((bf16[128,40,128]{2,1,0:T(8,128)(2,1)}), bf16[128,40,128]{2,1,0:T(8,128)(2,1)S(1)}, u32[]{:S(2)}, u32[]{:S(2)}) async-start(bf16[128,40,128]{2,1,0:T(8,128)(2,1)} %bitcast.45), calls=%async_computation | async-start | bytes 2621440 | tf_op jit(solution)/shard_map/all_to_all | solution.py:379
  74.3 3.9 %fusion.11 = f32[2048,384]{1,0:T(8,128)} fusion(bf16[2048,384]{1,0:T(8,128)(2,1)S(1)} %copy-done.2, bf16[384,1152]{1,0:T(8,128)(2,1)} %wp_ref.1), kind=kOutput, calls=%fused_computation.16 | convolution fusion | flops 603979776 | bytes 5013504 | tf_op jit(solution)/shard_map/dot_general | solution.py:466
  78.2 1.0 fusion.13
  79.2 2.3 %add_convert_fusion.1 = bf16[2048,384]{1,0:T(8,128)(2,1)} fusion(bf16[2048,384]{1,0:T(8,128)(2,1)S(1)} %bitcast.38, bf16[2048,384]{1,0:T(8,128)(2,1)S(1)} %copy-done.3, bf16[384,384]{1,0:T(8,128)(2,1)S(1)} %copy-done.6), kind=kOutput, calls=%fused_computation.8 | convolution fusion | flops 606339072 | bytes 5013504 | tf_op jit(solution)/shard_map/dot_general | solution.py:462
  81.5 1.0 slice.123
  82.7 1.0 slice.125
  84.3 1.5 %collective-permute-start.6 = (bf16[3,32,768]{2,1,0:T(8,128)(2,1)S(1)}, bf16[3,32,768]{2,1,0:T(8,128)(2,1)S(1)}, u32[]{:S(2)}, u32[]{:S(2)}) collective-permute-start(bf16[3,32,768]{2,1,0:T(8,128)(2,1)S(1)} %get-tuple-element.38), channel_id=1, source_target_pairs={{0,16},{16,32},{32,48},{48,64},{64,80},{80,96},{96,112},{112,0},{1... | collective-permute-start | bytes 442376 | tf_op jit(solution)/shard_map/ppermute | solution.py:347
  85.7 2.4 %collective-permute-start.7 = (bf16[3,32,768]{2,1,0:T(8,128)(2,1)S(1)}, bf16[3,32,768]{2,1,0:T(8,128)(2,1)S(1)}, u32[]{:S(2)}, u32[]{:S(2)}) collective-permute-start(bf16[3,32,768]{2,1,0:T(8,128)(2,1)S(1)} %get-tuple-element.39), channel_id=1, source_target_pairs={{16,0},{32,16},{48,32},{64,48},{80,64},{96,80},{112,96},{0,112},{1... | collective-permute-start | bytes 442376 | tf_op jit(solution)/shard_map/ppermute | solution.py:352
  88.1 8.9 %all-to-all-done = bf16[128,40,128]{2,1,0:T(8,128)(2,1)S(1)} async-done(((bf16[128,40,128]{2,1,0:T(8,128)(2,1)}), bf16[128,40,128]{2,1,0:T(8,128)(2,1)S(1)}, u32[]{:S(2)}, u32[]{:S(2)}) %all-to-all-start) | async-done | bytes 1310752 | tf_op jit(solution)/shard_map/all_to_all | solution.py:379
  97.0 1.3 %summed_copies.1 = bf16[5120,128]{1,0:T(8,128)(2,1)} custom-call(bf16[5120,128]{1,0:T(8,128)(2,1)S(1)} %bitcast.35), custom_call_target="tpu_custom_call" | custom-call | tf_op jit(solution)/shard_map/summed_copies/pallas_call | solution.py:368
  98.3 6.1 %all-to-all-start.1 = ((bf16[128,40,128]{2,1,0:T(8,128)(2,1)}), bf16[128,40,128]{2,1,0:T(8,128)(2,1)S(1)}, u32[]{:S(2)}, u32[]{:S(2)}) async-start(bf16[128,40,128]{2,1,0:T(8,128)(2,1)} %bitcast.20), calls=%async_computation.1 | async-start | bytes 2621440 | tf_op jit(solution)/shard_map/all_to_all | solution.py:381
  104.5 0.8 pad_maximum_fusion
  107.0 5.2 %add_convert_fusion = bf16[2048,384]{1,0:T(8,128)(2,1)} fusion(f32[2048,384]{1,0:T(8,128)S(1)} %copy-done, bf16[2048,384]{1,0:T(8,128)(2,1)S(1)} %bitcast.44, bf16[384,1152]{1,0:T(8,128)(2,1)S(1)} %copy-done.5, bf16[2048,768]{1,0:T(8,128)(2,1)S(1)} %bitcast.40, bf16[2048,768]{1,0:T(8,128)(2,1)S(1)} %bitcast.39, bf16[2240,768]{1,0:T(8,128)(2,1)} %get-tuple-element.14), kind=kOutput, calls=%fused_computation.6 | convolution fusion | flops 1220542464 | bytes 16318464 | tf_op jit(solution)/shard_map/dot_general | solution.py:467
  112.3 14.0 %all-to-all-done.1 = bf16[128,40,128]{2,1,0:T(8,128)(2,1)S(1)} async-done(((bf16[128,40,128]{2,1,0:T(8,128)(2,1)}), bf16[128,40,128]{2,1,0:T(8,128)(2,1)S(1)}, u32[]{:S(2)}, u32[]{:S(2)}) %all-to-all-start.1) | async-done | bytes 1310752 | tf_op jit(solution)/shard_map/all_to_all | solution.py:381
  126.2 1.5 %unpack.1 = (f32[384,1152]{1,0:T(8,128)}, f32[384,384]{1,0:T(8,128)}) custom-call(bf16[5120,128]{1,0:T(8,128)(2,1)S(1)} %bitcast.36), custom_call_target="tpu_custom_call" | custom-call | tf_op jit(solution)/shard_map/unpack/pallas_call | solution.py:397
  (65 shorter events, 7.5 us)
Async XLA Ops:
  0.6 14.6 %copy-start.9 = (s32[64,32]{0,1:T(8,128)S(1)}, s32[64,32]{0,1:T(8,128)}, u32[]{:S(2)}) copy-start(s32[64,32]{0,1:T(8,128)} %param.6) | copy-start | bytes 24580
  2.8 7.3 %collective-permute-start = (bf16[3,32,385]{2,1,0:T(8,128)(2,1)S(1)}, bf16[3,32,385]{2,1,0:T(8,128)(2,1)S(1)}, u32[]{:S(2)}, u32[]{:S(2)}) collective-permute-start(bf16[3,32,385]{2,1,0:T(8,128)(2,1)S(1)} %pad_maximum_fusion.4), channel_id=1, source_target_pairs={{0,16},{16,32},{32,48},{48,64},{64,80},{80,96},{96,112},{112,0},{1... | collective-permute-start | bytes 221768 | tf_op jit(solution)/shard_map/ppermute | solution.py:347
  5.3 4.8 %collective-permute-start.1 = (bf16[3,32,385]{2,1,0:T(8,128)(2,1)S(1)}, bf16[3,32,385]{2,1,0:T(8,128)(2,1)S(1)}, u32[]{:S(2)}, u32[]{:S(2)}) collective-permute-start(bf16[3,32,385]{2,1,0:T(8,128)(2,1)S(1)} %pad_maximum_fusion.5), channel_id=1, source_target_pairs={{16,0},{32,16},{48,32},{64,48},{80,64},{96,80},{112,96},{0,112},{1... | collective-permute-start | bytes 221768 | tf_op jit(solution)/shard_map/ppermute | solution.py:352
  10.1 13.2 %copy-start.7 = (bf16[3,32,385]{2,1,0:T(8,128)(2,1)}, bf16[3,32,385]{2,1,0:T(8,128)(2,1)S(1)}, u32[]{:S(2)}) copy-start(bf16[3,32,385]{2,1,0:T(8,128)(2,1)S(1)} %collective-permute-done) | copy-start | bytes 221764
  10.1 13.2 %copy-start.8 = (bf16[3,32,385]{2,1,0:T(8,128)(2,1)}, bf16[3,32,385]{2,1,0:T(8,128)(2,1)S(1)}, u32[]{:S(2)}) copy-start(bf16[3,32,385]{2,1,0:T(8,128)(2,1)S(1)} %collective-permute-done.1) | copy-start | bytes 221764
  10.2 7.5 %collective-permute-start.2 = (bf16[70,3,385]{2,0,1:T(8,128)(2,1)S(1)}, bf16[70,3,385]{2,0,1:T(8,128)(2,1)S(1)}, u32[]{:S(2)}, u32[]{:S(2)}) collective-permute-start(bf16[70,3,385]{2,0,1:T(8,128)(2,1)S(1)} %pad_maximum_fusion.2), channel_id=1, source_target_pairs={{0,1},{1,2},{2,3},{3,4},{4,5},{5,6},{6,7},{7,8},{8,9},{9,10},{10,1... | collective-permute-start | bytes 485108 | tf_op jit(solution)/shard_map/ppermute | solution.py:347
  14.9 7.3 %collective-permute-start.3 = (bf16[70,3,385]{2,0,1:T(8,128)(2,1)S(1)}, bf16[70,3,385]{2,0,1:T(8,128)(2,1)S(1)}, u32[]{:S(2)}, u32[]{:S(2)}) collective-permute-start(bf16[70,3,385]{2,0,1:T(8,128)(2,1)S(1)} %pad_maximum_fusion.3), channel_id=1, source_target_pairs={{1,0},{2,1},{3,2},{4,3},{5,4},{6,5},{7,6},{8,7},{9,8},{10,9},{11,1... | collective-permute-start | bytes 485108 | tf_op jit(solution)/shard_map/ppermute | solution.py:352
  61.0 13.2 %copy-start.2 = (bf16[2048,384]{1,0:T(8,128)(2,1)S(1)}, bf16[2048,384]{1,0:T(8,128)(2,1)}, u32[]{:S(2)}) copy-start(bf16[2048,384]{1,0:T(8,128)(2,1)} %get-tuple-element.13) | copy-start | bytes 4718596
  61.0 20.5 %collective-permute-start.4 = (bf16[288,768]{1,0:T(8,128)(2,1)}, bf16[288,768]{1,0:T(8,128)(2,1)}, u32[]{:S(2)}, u32[]{:S(2)}) collective-permute-start(bf16[288,768]{1,0:T(8,128)(2,1)} %get-tuple-element.15), channel_id=1, source_target_pairs={{0,1},{1,2},{2,3},{3,4},{4,5},{5,6},{6,7},{7,8},{8,9},{9,10},{10,1... | collective-permute-start | bytes 1327112 | tf_op jit(solution)/shard_map/ppermute | solution.py:347
  61.1 21.6 %collective-permute-start.5 = (bf16[288,768]{1,0:T(8,128)(2,1)}, bf16[288,768]{1,0:T(8,128)(2,1)}, u32[]{:S(2)}, u32[]{:S(2)}) collective-permute-start(bf16[288,768]{1,0:T(8,128)(2,1)} %get-tuple-element.16), channel_id=1, source_target_pairs={{1,0},{2,1},{3,2},{4,3},{5,4},{6,5},{7,6},{8,7},{9,8},{10,9},{11,1... | collective-permute-start | bytes 1327112 | tf_op jit(solution)/shard_map/ppermute | solution.py:352
  61.6 35.4 %all-to-all-start = ((bf16[128,40,128]{2,1,0:T(8,128)(2,1)}), bf16[128,40,128]{2,1,0:T(8,128)(2,1)S(1)}, u32[]{:S(2)}, u32[]{:S(2)}) async-start(bf16[128,40,128]{2,1,0:T(8,128)(2,1)} %bitcast.45), calls=%async_computation | async-start | bytes 2621440 | tf_op jit(solution)/shard_map/all_to_all | solution.py:379
  74.2 4.9 %copy-start.1 = (bf16[64,32,384]{2,1,0:T(8,128)(2,1)S(1)}, bf16[64,32,384]{2,1,0:T(8,128)(2,1)}, u32[]{:S(2)}) copy-start(bf16[64,32,384]{2,1,0:T(8,128)(2,1)} %param.5) | copy-start | bytes 4718596
  74.2 4.9 %copy-start.3 = (bf16[2048,384]{1,0:T(8,128)(2,1)S(1)}, bf16[2048,384]{1,0:T(8,128)(2,1)}, u32[]{:S(2)}) copy-start(bf16[2048,384]{1,0:T(8,128)(2,1)} %get-tuple-element.12) | copy-start | bytes 4718596
  74.3 4.9 %copy-start.6 = (bf16[384,384]{1,0:T(8,128)(2,1)S(1)}, bf16[384,384]{1,0:T(8,128)(2,1)}, u32[]{:S(2)}) copy-start(bf16[384,384]{1,0:T(8,128)(2,1)} %wo_ref.1) | copy-start | bytes 884740
  84.3 21.1 %collective-permute-start.6 = (bf16[3,32,768]{2,1,0:T(8,128)(2,1)S(1)}, bf16[3,32,768]{2,1,0:T(8,128)(2,1)S(1)}, u32[]{:S(2)}, u32[]{:S(2)}) collective-permute-start(bf16[3,32,768]{2,1,0:T(8,128)(2,1)S(1)} %get-tuple-element.38), channel_id=1, source_target_pairs={{0,16},{16,32},{32,48},{48,64},{64,80},{80,96},{96,112},{112,0},{1... | collective-permute-start | bytes 442376 | tf_op jit(solution)/shard_map/ppermute | solution.py:347
  85.7 19.6 %collective-permute-start.7 = (bf16[3,32,768]{2,1,0:T(8,128)(2,1)S(1)}, bf16[3,32,768]{2,1,0:T(8,128)(2,1)S(1)}, u32[]{:S(2)}, u32[]{:S(2)}) collective-permute-start(bf16[3,32,768]{2,1,0:T(8,128)(2,1)S(1)} %get-tuple-element.39), channel_id=1, source_target_pairs={{16,0},{32,16},{48,32},{64,48},{80,64},{96,80},{112,96},{0,112},{1... | collective-permute-start | bytes 442376 | tf_op jit(solution)/shard_map/ppermute | solution.py:352
  98.3 27.9 %all-to-all-start.1 = ((bf16[128,40,128]{2,1,0:T(8,128)(2,1)}), bf16[128,40,128]{2,1,0:T(8,128)(2,1)S(1)}, u32[]{:S(2)}, u32[]{:S(2)}) async-start(bf16[128,40,128]{2,1,0:T(8,128)(2,1)} %bitcast.20), calls=%async_computation.1 | async-start | bytes 2621440 | tf_op jit(solution)/shard_map/all_to_all | solution.py:381
  104.5 1.9 %copy-start = (f32[2048,384]{1,0:T(8,128)S(1)}, f32[2048,384]{1,0:T(8,128)}, u32[]{:S(2)}) copy-start(f32[2048,384]{1,0:T(8,128)} %fusion.11) | copy-start | bytes 9437188
  104.5 2.3 %copy-start.4 = (bf16[64,32,384]{2,1,0:T(8,128)(2,1)S(1)}, bf16[64,32,384]{2,1,0:T(8,128)(2,1)}, u32[]{:S(2)}) copy-start(bf16[64,32,384]{2,1,0:T(8,128)(2,1)} %param.7) | copy-start | bytes 4718596
  104.5 2.6 %copy-start.5 = (bf16[384,1152]{1,0:T(8,128)(2,1)S(1)}, bf16[384,1152]{1,0:T(8,128)(2,1)}, u32[]{:S(2)}) copy-start(bf16[384,1152]{1,0:T(8,128)(2,1)} %wp_ref.1) | copy-start | bytes 2654212

commit v3 on v2

v3 whole, which is shorter than its diff:
```python
import functools

import jax
import jax.numpy as jnp
from jax import lax
from jax.experimental import pallas as pl
from jax.experimental.pallas import tpu as pltpu
from jax.sharding import PartitionSpec as P

HEADS = 6
HEAD = 64
KERNEL = 7
RADIUS = 3
PAIR = 2 * HEAD
PAIRS = HEADS // 2
SIDE = 8
TILE_ROWS = 4
KEY_ROWS = TILE_ROWS + 2 * RADIUS
CHUNK = 48
SPAN = 2
PROJECT_TILES = 4
FACTOR = HEAD ** (-0.5)
NEG = float("-inf")
MIB = 1024 * 1024
f32 = jnp.float32
bf16 = jnp.bfloat16


def dims(lhs, rhs):
    return (((lhs,), (rhs,)), ((), ()))


def project_kernel(
    tok_ref, cot_ref, wp_ref, wo_ref, tissue_ref, q_ref, kv_ref, g_ref, tok_t_ref, tis_ref
):
    width = tok_ref.shape[1]
    tile = tis_ref.shape[1]
    tok = tok_ref[...]
    q = jnp.dot(tok, wp_ref[:, :width], preferred_element_type=f32).astype(bf16)
    q_ref[...] = (q * FACTOR).astype(bf16)
    kv_ref[...] = jnp.dot(tok, wp_ref[:, width:], preferred_element_type=f32).astype(bf16)
    g_ref[...] = lax.dot_general(
        cot_ref[...], wo_ref[...], dims(1, 1), preferred_element_type=f32
    ).astype(bf16)
    tok_t_ref[...] = tok.T
    for i in range(tissue_ref.shape[0]):
        across = jnp.broadcast_to(tissue_ref[i].astype(f32), (tile, tile)).T
        tis_ref[i * tile : (i + 1) * tile] = jnp.where(across > 0.5, 0.0, NEG)


def project(tok, cot, wp, wo, tissue):
    count, width = tok.shape
    tile = tissue.shape[2]
    rows = PROJECT_TILES * tile
    block = lambda cols: pl.BlockSpec((rows, cols), lambda i: (i, 0))
    whole = lambda a: pl.BlockSpec(a.shape, lambda i: (0, 0))
    return pl.pallas_call(
        project_kernel,
        grid=(count // rows,),
        out_shape=[
            jax.ShapeDtypeStruct((count, width), bf16),
            jax.ShapeDtypeStruct((count, 2 * width), bf16),
            jax.ShapeDtypeStruct((count, width), bf16),
            jax.ShapeDtypeStruct((width, count), bf16),
            jax.ShapeDtypeStruct((count, tile), f32),
        ],
        in_specs=[
            block(width),
            block(width),
            whole(wp),
            whole(wo),
            pl.BlockSpec((PROJECT_TILES, 1, tile), lambda i: (i, 0, 0)),
        ],
        out_specs=[
            block(width),
            block(2 * width),
            block(width),
            pl.BlockSpec((width, rows), lambda i: (0, i)),
            block(tile),
        ],
        compiler_params=pltpu.CompilerParams(vmem_limit_bytes=56 * MIB),
        cost_estimate=pl.CostEstimate(
            flops=2 * count * width * 4 * width, bytes_accessed=14 * count * width, transcendentals=0
        ),
        name="project",
    )(tok, cot, wp, wo, tissue)


def attention_kernel(
    extents,
    above_ref, below_ref, side_ref, q_hbm, kv_hbm, g_hbm, tis_hbm, tok_t_hbm, cot_hbm, wp_ref, base_ref,
    tissue_ref,
    att_hbm, dq_hbm, dkv_own_hbm, to_left_ref, to_right_ref, part_ref,
    cot_ref, q_ref, g_ref, tok_t_ref, att_ref, dq_ref, dkv_own_ref, dkv_side_ref,
    kv_own_s, kv_aux_s, tis_own_s, tis_aux_s, win_s, self_s, gate_s, acc_own, acc_aux, sems, *stage,
):
    tokens_dev, width = q_ref.shape
    halo = above_ref.shape[0]
    rows_own = tokens_dev + 2 * halo
    rows_aux = side_ref.shape[0]
    cols = halo // RADIUS
    wide = cols // 2
    tile = TILE_ROWS * wide
    band = TILE_ROWS * cols
    bands = tokens_dev // band
    own_keys = KEY_ROWS * wide
    aux_keys = KEY_ROWS * SIDE
    keys_all = own_keys + aux_keys
    most = 4 * HEAD
    x_s, dp_s, top_s, pl_s, sg_s = (stage[2 * i : 2 * i + 2] for i in range(5))

    middle = pl.ds(halo, tokens_dev)
    copies = [
        pltpu.make_async_copy(source, target, sems.at[i])
        for i, (source, target) in enumerate(
            [
                (kv_hbm, kv_own_s.at[middle]),
                (tis_hbm, tis_own_s.at[middle]),
                (q_hbm, q_ref),
                (g_hbm, g_ref),
                (tok_t_hbm, tok_t_ref),
                (cot_hbm, cot_ref),
            ]
        )
    ]
    for copy in copies:
        copy.start()

    def lanes(column):
        bias = jnp.where(column.astype(f32) > 0.5, 0.0, NEG)
        return jnp.broadcast_to(bias, (bias.shape[0], 2 * tile))

    def outer(rows_ref):
        return jnp.dot(
            rows_ref[:, :width], wp_ref[:, width:], preferred_element_type=f32
        ).astype(bf16)

    kv_own_s[:halo] = outer(above_ref)
    kv_own_s[halo + tokens_dev :] = outer(below_ref)
    kv_side = outer(side_ref)
    tis_own_s[:halo] = lanes(above_ref[:, width : width + 1])
    tis_own_s[halo + tokens_dev :] = lanes(below_ref[:, width : width + 1])
    tis_side = lanes(side_ref[:, width : width + 1])

    lane = lax.broadcasted_iota(jnp.int32, (1, 2 * tile), 1) % tile
    query_row = lane // wide
    query_col = lane % wide

    def window(key, query, base, extent):
        start = jnp.clip(base + query - RADIUS, 0, extent - KERNEL) - base
        return jnp.where((key >= start) & (key < start + KERNEL), 0.0, NEG)

    own_col = lax.broadcasted_iota(jnp.int32, (wide, 2 * tile), 0)
    aux_place = lax.broadcasted_iota(jnp.int32, (SIDE, 2 * tile), 0)
    far = -(2**20)
    first_in = jnp.where(aux_place < RADIUS, aux_place - RADIUS, aux_place - RADIUS + wide)
    second_in = jnp.where(
        aux_place < RADIUS, aux_place - RADIUS + wide, aux_place - RADIUS + cols
    )
    for half, aux_col in enumerate((first_in, second_in)):
        aux_col = jnp.where(aux_place < 2 * RADIUS, aux_col, far)
        shift = half * wide
        own_in = window(own_col + shift, query_col + shift, base_ref[1], extents[1])
        aux_in = window(aux_col, query_col + shift, base_ref[1], extents[1])
        own_same = jnp.where(own_col == query_col, 0.0, NEG)
        for key_row in range(KEY_ROWS):
            own_rows = slice(key_row * wide, (key_row + 1) * wide)
            aux_rows = slice(own_keys + key_row * SIDE, own_keys + (key_row + 1) * SIDE)
            for kind, first in enumerate((0, 2 * TILE_ROWS, (bands - 1) * TILE_ROWS)):
                row_in = window(key_row - RADIUS, query_row, base_ref[0] + first, extents[0])
                win_s[half, kind, own_rows] = own_in + row_in
                win_s[half, kind, aux_rows] = aux_in + row_in
            if half == 0:
                row_same = jnp.where(query_row == key_row - RADIUS, 0.0, NEG)
                self_s[own_rows] = own_same + row_same
                self_s[aux_rows] = jnp.full((SIDE, 2 * tile), NEG, f32)
    tissue = tissue_ref[...].astype(f32)
    for index in range(bands):
        for half in range(2):
            pieces = [
                tissue[
                    index * TILE_ROWS + row : index * TILE_ROWS + row + 1,
                    half * wide : (half + 1) * wide,
                ]
                for row in range(TILE_ROWS)
            ]
            gate_s[2 * index + half] = jnp.concatenate(pieces * 2, axis=1)

    place = lax.broadcasted_iota(jnp.int32, (rows_aux, 1), 0) % SIDE
    outer_left, outer_right = place < RADIUS, (place >= RADIUS) & (place < 2 * RADIUS)

    def parts(array, begin, count):
        across = array.shape[1]
        return array.reshape(rows_own // cols, cols, across)[:, begin : begin + count].reshape(
            -1, across
        )

    def with_inner(own, side):
        first = parts(own, wide, SIDE)
        second = parts(own, wide - SIDE, SIDE)
        return (
            jnp.where(outer_left, side, pltpu.roll(first, RADIUS, 0)),
            jnp.where(outer_right, side, pltpu.roll(second, rows_aux - SIDE + RADIUS, 0)),
        )

    for copy in copies[:2]:
        copy.wait()
    tis_aux_s[0], tis_aux_s[1] = with_inner(tis_own_s[...], tis_side)
    for begin in range(0, 2 * width, 256):
        at = slice(begin, begin + 256)
        one, two = with_inner(kv_own_s[:, at].astype(f32), kv_side[:, at].astype(f32))
        kv_aux_s[0, :, at] = one.astype(bf16)
        kv_aux_s[1, :, at] = two.astype(bf16)
    seen_rows = KEY_ROWS - TILE_ROWS
    acc_own[: seen_rows * cols] = jnp.zeros((seen_rows * cols, 2 * width), f32)
    acc_aux[:, : seen_rows * SIDE] = jnp.zeros((2, seen_rows * SIDE, 2 * width), f32)
    pl_s[1][...] = jnp.zeros((keys_all, HEADS * tile), bf16)
    sg_s[1][...] = jnp.zeros((keys_all, HEADS * tile), bf16)
    for copy in copies[2:4]:
        copy.wait()

    def split(block):
        head = lax.broadcasted_iota(jnp.int32, block.shape, 1) // HEAD
        zero = jnp.zeros_like(block)
        return jnp.concatenate(
            [jnp.where(head == i, block, zero) for i in range(block.shape[1] // HEAD)], axis=0
        )

    def corner(one, two):
        zero = jnp.zeros_like(one)
        return jnp.concatenate(
            [jnp.concatenate([one, zero], axis=1), jnp.concatenate([zero, two], axis=1)], axis=0
        )

    def own_at(index, half, row):
        return pl.ds(pl.multiple_of(index * band, band) + row * cols + half * wide, wide)

    def aux_at(index, begin, count):
        step = TILE_ROWS * SIDE
        return pl.ds(pl.multiple_of(index * step, step) + begin * SIDE, count * SIDE)

    def queries(ref, index, half):
        return jnp.concatenate([ref[own_at(index, half, row), :] for row in range(TILE_ROWS)], axis=0)

    def key_rows(index, half, at):
        rows = [kv_own_s[own_at(index, half, row), at] for row in range(KEY_ROWS)]
        return jnp.concatenate(rows + [kv_aux_s[half, aux_at(index, 0, KEY_ROWS), at]], axis=0)

    def score_stage(index, half):
        kind = jnp.where(index == 0, 0, jnp.where(index == bands - 1, 2, 1))
        tis_keys = jnp.concatenate(
            [tis_own_s[own_at(index, half, row)] for row in range(KEY_ROWS)]
            + [tis_aux_s[half, aux_at(index, 0, KEY_ROWS)]],
            axis=0,
        )
        bias = jnp.maximum(tis_keys, self_s[...]) + win_s[half, kind]
        q, g = queries(q_ref, index, half), queries(g_ref, index, half)
        keys = key_rows(index, half, slice(0, width))
        values = key_rows(index, half, slice(width, 2 * width))
        product = functools.partial(
            lax.dot_general, dimension_numbers=dims(1, 1), preferred_element_type=f32
        )
        rest = product(
            jnp.concatenate([keys[:, most:], values[:, most:]], axis=1),
            corner(split(q[:, most:]), split(g[:, most:])),
        )
        cut = HEADS * tile - 4 * tile
        scores = jnp.concatenate(
            [product(keys[:, :most], split(q[:, :most])), rest[:, :cut]], axis=1
        )
        scores = scores + jnp.concatenate([bias] * PAIRS, axis=1)
        x_s[half][...] = scores
        top_s[half][...] = jnp.max(scores, axis=0, keepdims=True)
        dp_s[half][:, : 4 * tile] = product(values[:, :most], split(g[:, :most]))
        dp_s[half][:, 4 * tile :] = rest[:, cut:]

    def softmax_stage(index, half):
        top = top_s[half][...]
        total = jnp.zeros((8, HEADS * tile), f32)
        inner = jnp.zeros((8, HEADS * tile), f32)
        fold = lambda a: jnp.sum(a.reshape(CHUNK // 8, 8, HEADS * tile), axis=0)
        for begin in range(0, keys_all, CHUNK):
            at = slice(begin, begin + CHUNK)
            terms = jnp.exp(x_s[half][at] - top)
            x_s[half][at] = terms
            total = total + fold(terms)
            inner = inner + fold(terms * dp_s[half][at])
        inverse = 1.0 / jnp.sum(total, axis=0, keepdims=True)
        delta = jnp.sum(inner, axis=0, keepdims=True) * inverse
        weight = inverse * jnp.concatenate([gate_s[2 * index + half]] * PAIRS, axis=1)
        for begin in range(0, keys_all, CHUNK):
            at = slice(begin, begin + CHUNK)
            probs = x_s[half][at] * weight
            pl_s[half][at] = probs.astype(bf16)
            sg_s[half][at] = (probs * (dp_s[half][at] - delta)).astype(bf16)

    def product_stage(index, half):
        keys = key_rows(index, half, slice(0, width))
        values = key_rows(index, half, slice(width, 2 * width))
        probs_low = pl_s[half][...]
        score_grad = sg_s[half][...]
        first_head = lax.broadcasted_iota(jnp.int32, (tile, PAIR), 1) < HEAD
        for pair in range(PAIRS):
            at = slice(pair * PAIR, (pair + 1) * PAIR)
            for rows, weight, scale, out_ref in (
                (values, probs_low, 1.0, att_ref),
                (keys, score_grad, FACTOR, dq_ref),
            ):
                both = lax.dot_general(
                    rows[:, at], weight[:, at], dims(0, 0), preferred_element_type=f32
                ).T
                mixed = (jnp.where(first_head, both[:tile], both[tile:]) * scale).astype(bf16)
                for row in range(TILE_ROWS):
                    out_ref[own_at(index, half, row), at] = mixed[row * wide : (row + 1) * wide]
        q, g = queries(q_ref, index, half), queries(g_ref, index, half)
        rest = jnp.dot(
            jnp.concatenate([probs_low[:, 4 * tile :], score_grad[:, 4 * tile :]], axis=1),
            corner(split(g[:, most:]), split(q[:, most:])),
            preferred_element_type=f32,
        )
        cut = width - most
        dk = jnp.dot(score_grad[:, : 4 * tile], split(q[:, :most]), preferred_element_type=f32)
        dv = jnp.dot(probs_low[:, : 4 * tile], split(g[:, :most]), preferred_element_type=f32)
        for grad, at in (
            (dk, slice(0, most)),
            (rest[:, cut:], slice(most, width)),
            (dv, slice(width, width + most)),
            (rest[:, :cut], slice(width + most, 2 * width)),
        ):
            for row in range(KEY_ROWS):
                piece = grad[row * wide : (row + 1) * wide]
                if row < seen_rows:
                    acc_own[own_at(index, half, row), at] += piece
                else:
                    acc_own[own_at(index, half, row), at] = piece
            seen = own_keys + seen_rows * SIDE
            acc_aux[half, aux_at(index, 0, seen_rows), at] += grad[own_keys:seen]
            acc_aux[half, aux_at(index, seen_rows, TILE_ROWS), at] = grad[seen:]

    score_stage(0, 0)

    def step(group, carry):
        for slot in range(2 * SPAN):
            index = group * SPAN + slot // 2
            half = slot % 2
            if half == 0:
                product_stage(jnp.maximum(index - 1, 0), 1)
            else:
                product_stage(index, 0)
            softmax_stage(index, half)
            if half == 0:
                score_stage(index, 1)
            else:
                score_stage(jnp.minimum(index + 1, bands - 1), 0)
        return carry

    lax.fori_loop(0, bands // SPAN, step, 0)
    product_stage(bands - 1, 1)

    for begin in range(0, 2 * width, 128):
        at = slice(begin, begin + 128)
        one, two = acc_aux[0, :, at], acc_aux[1, :, at]
        dkv_side_ref[:, at] = jnp.where(
            outer_left, one, jnp.where(outer_right, two, 0.0)
        ).astype(bf16)
        first = jnp.where(place < RADIUS, pltpu.roll(one, rows_aux - RADIUS, 0), 0.0)
        second = jnp.where(
            place >= SIDE - RADIUS, pltpu.roll(two, SIDE - RADIUS, 0), 0.0
        )
        shape = (rows_aux // SIDE, SIDE, 128)
        blank = lambda count: jnp.zeros((shape[0], count, 128), f32)
        inner = jnp.concatenate(
            [
                blank(wide - SIDE),
                second.reshape(shape),
                first.reshape(shape),
                blank(cols - wide - SIDE),
            ],
            axis=1,
        ).reshape(rows_own, 128)
        dkv_own_ref[:, at] = (acc_own[:, at] + inner).astype(bf16)
    results = [
        pltpu.make_async_copy(source, target, sems.at[6 + i])
        for i, (source, target) in enumerate(
            [(dkv_own_ref, dkv_own_hbm), (att_ref, att_hbm), (dq_ref, dq_hbm)]
        )
    ]
    for copy in results:
        copy.start()
    for copy in copies[4:]:
        copy.wait()
    send_row = lax.broadcasted_iota(jnp.int32, (128, 256), 0)
    side_row = lax.broadcasted_iota(jnp.int32, (128, 256), 1)
    place = (send_row // (SIDE // 2)) * SIDE + send_row % (SIDE // 2)
    for begin, send_ref in ((0, to_left_ref), (RADIUS, to_right_ref)):
        pick = jnp.where(side_row == place + begin, 1.0, 0.0).astype(bf16)
        for first in range(0, send_ref.shape[0], 128):
            count = min(128, send_ref.shape[0] - first)
            source = dkv_side_ref[2 * first : min(2 * (first + count), dkv_side_ref.shape[0])]
            send_ref[first : first + count] = jnp.dot(
                pick[:count, : source.shape[0]], source, preferred_element_type=f32
            ).astype(bf16)
    outside = jnp.concatenate(
        [above_ref[:, :width], below_ref[:, :width], side_ref[:, :width]], axis=0
    )

    def put(block, value):
        value = value.astype(bf16)
        for i in range(value.shape[1] // 128):
            part_ref[(block + i) * width : (block + i + 1) * width] = value[
                :, i * 128 : (i + 1) * 128
            ]

    columns = width // 128
    put(0, jnp.dot(tok_t_ref[...], dq_ref[...], preferred_element_type=f32))
    for begin in range(0, 2 * width, 256):
        at = slice(begin, begin + 256)
        grad_outside = jnp.concatenate(
            [dkv_own_ref[:halo, at], dkv_own_ref[halo + tokens_dev :, at], dkv_side_ref[:, at]],
            axis=0,
        )
        put(
            columns + begin // 128,
            jnp.dot(
                tok_t_ref[...],
                dkv_own_ref[halo : halo + tokens_dev, at],
                preferred_element_type=f32,
            )
            + lax.dot_general(outside, grad_outside, dims(0, 0), preferred_element_type=f32),
        )
    put(3 * columns, lax.dot_general(
            att_ref[...], cot_ref[...], dims(0, 0), preferred_element_type=f32
        ))
    used = 4 * width * columns
    if used < part_ref.shape[0]:
        part_ref[used:] = jnp.zeros((part_ref.shape[0] - used, 128), bf16)
    for copy in results:
        copy.wait()


def attention(
    above, below, side, q, kv, g, tis, tok_t, cot, wp, base, tissue, extents, rows_part
):
    tokens_dev, width = cot.shape
    rows_own = tokens_dev + 2 * above.shape[0]
    rows_side = side.shape[0]
    cols = tissue.shape[1]
    tile = TILE_ROWS * cols // 2
    keys_all = KEY_ROWS * (cols // 2 + SIDE)
    rows_send = -(-rows_side // 32) * 16
    vmem = pl.BlockSpec(memory_space=pltpu.VMEM)
    hbm = pl.BlockSpec(memory_space=pl.ANY)
    smem = pl.BlockSpec(memory_space=pltpu.SMEM)
    stage = []
    for shape, kind in (
        ((keys_all, HEADS * tile), f32),
        ((keys_all, HEADS * tile), f32),
        ((1, HEADS * tile), f32),
        ((keys_all, HEADS * tile), bf16),
        ((keys_all, HEADS * tile), bf16),
    ):
        stage += [pltpu.VMEM(shape, kind)] * 2
    return pl.pallas_call(
        functools.partial(attention_kernel, extents),
        out_shape=[
            jax.ShapeDtypeStruct((tokens_dev, width), bf16),
            jax.ShapeDtypeStruct((tokens_dev, width), bf16),
            jax.ShapeDtypeStruct((rows_own, 2 * width), bf16),
            jax.ShapeDtypeStruct((rows_send, 2 * width), bf16),
            jax.ShapeDtypeStruct((rows_send, 2 * width), bf16),
            jax.ShapeDtypeStruct((rows_part, 128), bf16),
        ],
        in_specs=[vmem] * 3 + [hbm] * 6 + [vmem, smem, vmem],
        out_specs=[hbm] * 3 + [vmem] * 3,
        scratch_shapes=[
            pltpu.VMEM((tokens_dev, width), bf16),
            pltpu.VMEM((tokens_dev, width), bf16),
            pltpu.VMEM((tokens_dev, width), bf16),
            pltpu.VMEM((width, tokens_dev), bf16),
            pltpu.VMEM((tokens_dev, width), bf16),
            pltpu.VMEM((tokens_dev, width), bf16),
            pltpu.VMEM((rows_own, 2 * width), bf16),
            pltpu.VMEM((rows_side, 2 * width), bf16),
            pltpu.VMEM((rows_own, 2 * width), bf16),
            pltpu.VMEM((2, rows_side, 2 * width), bf16),
            pltpu.VMEM((rows_own, 2 * tile), f32),
            pltpu.VMEM((2, rows_side, 2 * tile), f32),
            pltpu.VMEM((2, 3, keys_all, 2 * tile), f32),
            pltpu.VMEM((keys_all, 2 * tile), f32),
            pltpu.VMEM((2 * tokens_dev // (2 * tile), 1, 2 * tile), f32),
            pltpu.VMEM((rows_own, 2 * width), f32),
            pltpu.VMEM((2, rows_side, 2 * width), f32),
            pltpu.SemaphoreType.DMA((9,)),
        ]
        + stage,
        compiler_params=pltpu.CompilerParams(vmem_limit_bytes=56 * MIB),
        name="attention",
    )(above, below, side, q, kv, g, tis, tok_t, cot, wp, base, tissue)


def to_next(array, axis):
    count = lax.axis_size(axis)
    return lax.ppermute(array, axis, [(i, (i + 1) % count) for i in range(count)])


def to_last(array, axis):
    count = lax.axis_size(axis)
    return lax.ppermute(array, axis, [((i + 1) % count, i) for i in range(count)])


def sum_kernel(pieces, pieces_ref, copies_ref):
    rows = pieces_ref.shape[0] // pieces
    pair = 2 * rows
    total = jnp.zeros((pair, 128), f32)
    for i in range(pieces // 2):
        total = total + pieces_ref[i * pair : (i + 1) * pair].astype(f32)
    total = total[:rows] + total[rows:]
    total = jnp.concatenate([total, total], axis=0).astype(bf16)
    for i in range(pieces // 2):
        copies_ref[i * pair : (i + 1) * pair] = total


def summed_copies(pieces, count):
    return pl.pallas_call(
        functools.partial(sum_kernel, count),
        out_shape=jax.ShapeDtypeStruct(pieces.shape, bf16),
        compiler_params=pltpu.CompilerParams(vmem_limit_bytes=16 * MIB),
        name="summed_copies",
    )(pieces)


def total_over_devices(partial):
    axes = ("row", "col")
    count = lax.axis_size("row") * lax.axis_size("col")
    pieces = lax.all_to_all(partial.reshape(count, -1, 128), axes, 0, 0, tiled=True)
    copies = summed_copies(pieces.reshape(partial.shape), count).reshape(pieces.shape)
    return lax.all_to_all(copies, axes, 0, 0, tiled=True).reshape(partial.shape)


def unpack_kernel(scale, whole_ref, packed_ref, output_ref):
    width = output_ref.shape[0]
    for block in range((packed_ref.shape[1] + output_ref.shape[1]) // 128):
        value = whole_ref[block * width : (block + 1) * width].astype(f32) * scale
        column = block * 128
        if column < packed_ref.shape[1]:
            packed_ref[:, column : column + 128] = value
        else:
            column -= packed_ref.shape[1]
            output_ref[:, column : column + 128] = value


def unpack(whole, width, scale):
    return pl.pallas_call(
        functools.partial(unpack_kernel, scale),
        out_shape=[
            jax.ShapeDtypeStruct((width, 3 * width), f32),
            jax.ShapeDtypeStruct((width, width), f32),
        ],
        compiler_params=pltpu.CompilerParams(vmem_limit_bytes=24 * MIB),
        name="unpack",
    )(whole)


def per_device(tokens, tissue, cotangent, packed_weight, output_weight):
    rows_dev, cols_dev, width = tokens.shape
    ext_rows = rows_dev + 2 * RADIUS
    devices = lax.axis_size("row") * lax.axis_size("col")
    rows_part = -(-4 * width * (width // 128) // (8 * devices)) * 8 * devices
    tile = TILE_ROWS * cols_dev
    total_scale = float(rows_dev * lax.axis_size("row") * cols_dev * lax.axis_size("col")) ** (-0.5)
    token_rows = tokens.reshape(-1, width)
    cotangent_rows = cotangent.reshape(-1, width)

    with_tissue = lambda a, b: jnp.concatenate([a, b.astype(bf16)[..., None]], axis=-1)
    above = to_next(with_tissue(tokens[-RADIUS:], tissue[-RADIUS:]), "row")
    below = to_last(with_tissue(tokens[:RADIUS], tissue[:RADIUS]), "row")
    left_cols = with_tissue(tokens[:, :RADIUS], tissue[:, :RADIUS])
    right_cols = with_tissue(tokens[:, -RADIUS:], tissue[:, -RADIUS:])
    left_cols = jnp.concatenate([above[:, :RADIUS], left_cols, below[:, :RADIUS]], axis=0)
    right_cols = jnp.concatenate([above[:, -RADIUS:], right_cols, below[:, -RADIUS:]], axis=0)
    tiles = tissue.reshape(-1, 1, tile)
    token_rows, left_cols, right_cols = lax.optimization_barrier(
        (token_rows, left_cols, right_cols)
    )
    from_left = to_next(right_cols, "col")
    from_right = to_last(left_cols, "col")
    pad = jnp.zeros((ext_rows, SIDE - 2 * RADIUS, width + 1), bf16)
    side = jnp.concatenate([from_left, from_right, pad], axis=1).reshape(-1, width + 1)

    q, kv, g, tok_t, tis = project(
        token_rows, cotangent_rows, packed_weight, output_weight, tiles
    )
    base = jnp.stack([lax.axis_index("row") * rows_dev, lax.axis_index("col") * cols_dev])
    attended, dq, dkv_own, to_left, to_right, partial = attention(
        above.reshape(-1, width + 1), below.reshape(-1, width + 1), side,
        q, kv, g, tis, tok_t, cotangent_rows, packed_weight, base.astype(jnp.int32), tissue,
        (rows_dev * lax.axis_size("row"), cols_dev * lax.axis_size("col")), rows_part,
    )

    half = SIDE // 2

    def columns(sent):
        return sent[: ext_rows * half].reshape(ext_rows, half, 2 * width)[:, :RADIUS]

    from_right = columns(to_last(to_left, "col"))
    from_left = columns(to_next(to_right, "col"))
    dkv_own = dkv_own.reshape(ext_rows, cols_dev, 2 * width)
    first, last, inner = slice(None, RADIUS), slice(-RADIUS, None), slice(RADIUS, -RADIUS)

    def with_columns(rows):
        between = jnp.zeros((dkv_own[rows].shape[0], cols_dev - 2 * RADIUS, 2 * width), bf16)
        beside = jnp.concatenate([from_left[rows], between, from_right[rows]], axis=1)
        return dkv_own[rows].astype(f32) + beside.astype(f32)

    from_below = to_last(with_columns(first).astype(bf16), "row")
    from_above = to_next(with_columns(last).astype(bf16), "row")
    between = jnp.zeros((rows_dev - 2 * RADIUS, cols_dev, 2 * width), bf16)
    beside = jnp.concatenate([from_above, between, from_below], axis=0)
    dkv = with_columns(inner) + beside.astype(f32)
    dkv = dkv.astype(bf16).reshape(-1, 2 * width)

    contract = functools.partial(lax.dot_general, preferred_element_type=f32)
    layer_out = (
        token_rows.astype(f32) + jnp.dot(attended, output_weight, preferred_element_type=f32)
    ).astype(bf16)
    grad_tokens = (
        cotangent_rows.astype(f32)
        + contract(dq, packed_weight[:, :width], dims(1, 1))
        + contract(dkv, packed_weight[:, width:], dims(1, 1))
    ).astype(bf16)
    grad_packed, grad_output = unpack(total_over_devices(partial), width, total_scale)
    return (
        layer_out.reshape(rows_dev, cols_dev, width),
        grad_tokens.reshape(rows_dev, cols_dev, width),
        grad_packed,
        grad_output,
    )


def solution(mesh):
    in_specs = (P("row", "col", None), P("row", "col"), P("row", "col", None), P(), P())
    out_specs = (P("row", "col", None), P("row", "col", None), P(), P())
    return jax.shard_map(
        per_device, mesh=mesh, in_specs=in_specs, out_specs=out_specs, check_vma=False
    )
```

time: 128 us -> 121 us (0.945)
  waiting for transfers between devices: 28.7 us -> 22.3 us
  Pallas kernels: 40.5 us -> 38.8 us
    pallas_call x1, Pallas kernels: 37.7 us -> 28.1 us  [attention(): pl.pallas_call(functools.partial(attention_kernel, extents), out_shape=[j...]
    pallas_call x0 -> x1, Pallas kernels: none -> 7.88 us  [project(): pl.pallas_call(project_kernel, grid=(count // rows,), out_shape=[jax.Shap...]
    ppermute x4, waiting for transfers between devices: 4.48 us -> 0.01 us  [to_last(): lax.ppermute(array, axis, [((i + 1) % count, i) for i in range(count)])]
    all_to_all x1, starting transfers between devices: 12.6 us -> 9.39 us  [total_over_devices(): lax.all_to_all(partial.reshape(count, -1, 128), axes, 0, 0, tiled=True)]
    ppermute x4, starting transfers between devices: 8.24 us -> 11.4 us  [to_next(): lax.ppermute(array, axis, [(i, (i + 1) % count) for i in range(count)])]
    ppermute x4, waiting for transfers between devices: 1.37 us -> 0.01 us  [to_next(): lax.ppermute(array, axis, [(i, (i + 1) % count) for i in range(count)])]
  transfers between devices with their start and end apart: 10 -> 10, of which waited for: 5 -> 2; matrix products, arithmetic and copies ran while one was open for 16% -> 18% of each run, Pallas kernels for 1% -> 8%
where the time goes in v3:
time: 121 us; the launch traced here: 120 us
  Pallas kernels  38.8 us (32%)
  starting transfers between devices  32.2 us (27%)
  waiting for transfers between devices  22.3 us (18%)
  matrix products  11.4 us (9%)
  local copies, waits for them, and re-layouts  10.7 us (9%)
  other arithmetic  3.84 us (3%)
    pallas_call x1, Pallas kernels, attention(): pl.pallas_call(functools.partial(attention_kernel, extents), out_shape=[j...  28.1 us
    all_to_all x1, waiting for transfers between devices, total_over_devices(): return lax.all_to_all(copies, axes, 0, 0, tiled=True).reshape(partial.shape)  13.9 us
    ppermute x4, starting transfers between devices, to_next(): lax.ppermute(array, axis, [(i, (i + 1) % count) for i in range(count)])  11.4 us
    all_to_all x1, starting transfers between devices, total_over_devices(): lax.all_to_all(partial.reshape(count, -1, 128), axes, 0, 0, tiled=True)  9.39 us
    all_to_all x1, waiting for transfers between devices, total_over_devices(): lax.all_to_all(partial.reshape(count, -1, 128), axes, 0, 0, tiled=True)  8.38 us
    pallas_call x1, Pallas kernels, project(): pl.pallas_call(project_kernel, grid=(count // rows,), out_shape=[jax.Shap...  7.88 us
    all_to_all x1, starting transfers between devices, total_over_devices(): return lax.all_to_all(copies, axes, 0, 0, tiled=True).reshape(partial.shape)  6.4 us
    dot_general x1, matrix products, per_device(): contract(dkv, packed_weight[:, width:], dims(1, 1))  5.21 us
  transfers between devices with their start and end apart: 10, of which 2 were waited for; matrix products, arithmetic and copies ran while one was open for 18% of the time, Pallas kernels for 8%

profile of v3, /device:TPU:1, one launch (start us, length us, event | category | flops | bytes accessed | tf_op | source)
XLA Modules:
  0.0 120.3 jit_solution(9007157767416716081)
XLA Ops:
  1.8 0.9 fusion.15
  2.7 2.1 %collective-permute-start = (bf16[3,32,385]{2,1,0:T(8,128)(2,1)S(1)}, bf16[3,32,385]{2,1,0:T(8,128)(2,1)S(1)}, u32[]{:S(2)}, u32[]{:S(2)}) collective-permute-start(bf16[3,32,385]{2,1,0:T(8,128)(2,1)S(1)} %pad_maximum_fusion.4), channel_id=1, source_target_pairs={{0,16},{16,32},{32,48},{48,64},{64,80},{80,96},{96,112},{112,0},{1... | collective-permute-start | bytes 221768 | tf_op jit(solution)/shard_map/ppermute | solution.py:503
  5.2 2.7 %collective-permute-start.1 = (bf16[3,32,385]{2,1,0:T(8,128)(2,1)S(1)}, bf16[3,32,385]{2,1,0:T(8,128)(2,1)S(1)}, u32[]{:S(2)}, u32[]{:S(2)}) collective-permute-start(bf16[3,32,385]{2,1,0:T(8,128)(2,1)S(1)} %pad_maximum_fusion.5), channel_id=1, source_target_pairs={{16,0},{32,16},{48,32},{64,48},{80,64},{96,80},{112,96},{0,112},{1... | collective-permute-start | bytes 221768 | tf_op jit(solution)/shard_map/ppermute | solution.py:508
  7.9 1.3 %fusion.14 = (bf16[64,3,384]{2,1,0:T(4,128)(2,1)S(1)}, bf16[64,3,384]{2,1,0:T(4,128)(2,1)S(1)}) fusion(bf16[64,32,384]{2,1,0:T(8,128)(2,1)} %param.5), kind=kLoop, calls=%fused_computation.28 | loop fusion | bytes 589824 | tf_op jit(solution)/shard_map/slice | solution.py:578
  12.2 4.5 %collective-permute-start.2 = (bf16[70,3,385]{2,0,1:T(8,128)(2,1)S(1)}, bf16[70,3,385]{2,0,1:T(8,128)(2,1)S(1)}, u32[]{:S(2)}, u32[]{:S(2)}) collective-permute-start(bf16[70,3,385]{2,0,1:T(8,128)(2,1)S(1)} %get-tuple-element.21), channel_id=1, source_target_pairs={{0,1},{1,2},{2,3},{3,4},{4,5},{5,6},{6,7},{7,8},{8,9},{9,10},{10,1... | collective-permute-start | bytes 485108 | tf_op jit(solution)/shard_map/ppermute | solution.py:503
  16.7 7.9 %project.1 = (bf16[2048,384]{1,0:T(8,128)(2,1)}, bf16[2048,768]{1,0:T(8,128)(2,1)}, bf16[2048,384]{1,0:T(8,128)(2,1)}, bf16[384,2048]{1,0:T(8,128)(2,1)}, f32[2048,128]{1,0:T(8,128)}) custom-call(bf16[2048,384]{1,0:T(8,128)(2,1)} %bitcast.39, bf16[2048,384]{1,0:T(8,128)(2,1)} %bitcast.42, bf16[384,1152]{1,0:T(8,128)(2,1)} %wp_ref.3, ...), custom_call_target="tpu_custom_call" | custom-call | flops 2415919104 | bytes 11010048 | tf_op jit(solution)/shard_map/project/pallas_call | solution.py:57
  24.7 1.0 copy.95
  25.7 28.1 %attention.1 = (bf16[2048,384]{1,0:T(8,128)(2,1)}, bf16[2048,384]{1,0:T(8,128)(2,1)}, bf16[2240,768]{1,0:T(8,128)(2,1)}, bf16[288,768]{1,0:T(8,128)(2,1)}, bf16[...) custom-call(bf16[96,385]{1,0:T(8,128)(2,1)} %bitcast.49, bf16[96,385]{1,0:T(8,128)(2,1)} %bitcast.50, ...), custom_call_target="tpu_custom_call" | custom-call | tf_op jit(solution)/shard_map/attention/pallas_call | solution.py:463
  53.8 3.3 %collective-permute-start.4 = (bf16[288,768]{1,0:T(8,128)(2,1)}, bf16[288,768]{1,0:T(8,128)(2,1)S(1)}, u32[]{:S(2)}, u32[]{:S(2)}) collective-permute-start(bf16[288,768]{1,0:T(8,128)(2,1)} %get-tuple-element.31), channel_id=1, source_target_pairs={{0,1},{1,2},{2,3},{3,4},{4,5},{5,6},{6,7},{7,8},{8,9},{9,10},{10,1... | collective-permute-start | bytes 1327112 | tf_op jit(solution)/shard_map/ppermute | solution.py:503
  57.1 9.4 %all-to-all-start = ((bf16[128,40,128]{2,1,0:T(8,128)(2,1)}), bf16[128,40,128]{2,1,0:T(8,128)(2,1)S(1)}, u32[]{:S(2)}, u32[]{:S(2)}) async-start(bf16[128,40,128]{2,1,0:T(8,128)(2,1)} %bitcast.46), calls=%async_computation | async-start | bytes 2621440 | tf_op jit(solution)/shard_map/all_to_all | solution.py:535
  66.6 3.9 %fusion.11 = f32[2048,384]{1,0:T(8,128)} fusion(bf16[2048,384]{1,0:T(8,128)(2,1)S(1)} %copy-done.1, bf16[384,1152]{1,0:T(8,128)(2,1)} %wp_ref.3), kind=kOutput, calls=%fused_computation.16 | convolution fusion | flops 603979776 | bytes 5013504 | tf_op jit(solution)/shard_map/dot_general | solution.py:628
  70.5 1.7 %fusion.13 = (bf16[96,768]{1,0:T(8,128)(2,1)S(1)}, bf16[96,768]{1,0:T(8,128)(2,1)}) fusion(bf16[2240,768]{1,0:T(8,128)(2,1)} %get-tuple-element.30), kind=kLoop, calls=%fused_computation.27 | loop fusion | bytes 589824 | tf_op jit(solution)/shard_map/slice | solution.py:613
  72.1 2.3 %add_convert_fusion.1 = bf16[2048,384]{1,0:T(8,128)(2,1)} fusion(bf16[2048,384]{1,0:T(8,128)(2,1)S(1)} %bitcast.40, bf16[2048,384]{1,0:T(8,128)(2,1)S(1)} %copy-done.5, bf16[384,384]{1,0:T(8,128)(2,1)S(1)} %copy-done.7), kind=kOutput, calls=%fused_computation.8 | convolution fusion | flops 606339072 | bytes 5013504 | tf_op jit(solution)/shard_map/dot_general | solution.py:624
  74.7 1.0 slice.125
  76.1 1.0 fusion.10
  77.1 1.5 %collective-permute-start.6 = (bf16[3,32,768]{2,1,0:T(8,128)(2,1)S(1)}, bf16[3,32,768]{2,1,0:T(8,128)(2,1)S(1)}, u32[]{:S(2)}, u32[]{:S(2)}) collective-permute-start(bf16[3,32,768]{2,1,0:T(8,128)(2,1)S(1)} %get-tuple-element.54), channel_id=1, source_target_pairs={{0,16},{16,32},{32,48},{48,64},{64,80},{80,96},{96,112},{112,0},{1... | collective-permute-start | bytes 442376 | tf_op jit(solution)/shard_map/ppermute | solution.py:503
  78.6 2.4 %collective-permute-start.7 = (bf16[3,32,768]{2,1,0:T(8,128)(2,1)S(1)}, bf16[3,32,768]{2,1,0:T(8,128)(2,1)S(1)}, u32[]{:S(2)}, u32[]{:S(2)}) collective-permute-start(bf16[3,32,768]{2,1,0:T(8,128)(2,1)S(1)} %get-tuple-element.55), channel_id=1, source_target_pairs={{16,0},{32,16},{48,32},{64,48},{80,64},{96,80},{112,96},{0,112},{1... | collective-permute-start | bytes 442376 | tf_op jit(solution)/shard_map/ppermute | solution.py:508
  80.9 8.4 %all-to-all-done = bf16[128,40,128]{2,1,0:T(8,128)(2,1)S(1)} async-done(((bf16[128,40,128]{2,1,0:T(8,128)(2,1)}), bf16[128,40,128]{2,1,0:T(8,128)(2,1)S(1)}, u32[]{:S(2)}, u32[]{:S(2)}) %all-to-all-start) | async-done | bytes 1310752 | tf_op jit(solution)/shard_map/all_to_all | solution.py:535
  89.3 1.3 %summed_copies.1 = bf16[5120,128]{1,0:T(8,128)(2,1)} custom-call(bf16[5120,128]{1,0:T(8,128)(2,1)S(1)} %bitcast.35), custom_call_target="tpu_custom_call" | custom-call | tf_op jit(solution)/shard_map/summed_copies/pallas_call | solution.py:524
  90.6 6.4 %all-to-all-start.1 = ((bf16[128,40,128]{2,1,0:T(8,128)(2,1)}), bf16[128,40,128]{2,1,0:T(8,128)(2,1)S(1)}, u32[]{:S(2)}, u32[]{:S(2)}) async-start(bf16[128,40,128]{2,1,0:T(8,128)(2,1)} %bitcast.20), calls=%async_computation.1 | async-start | bytes 2621440 | tf_op jit(solution)/shard_map/all_to_all | solution.py:537
  97.1 0.8 pad_maximum_fusion
  99.7 5.2 %add_convert_fusion = bf16[2048,384]{1,0:T(8,128)(2,1)} fusion(f32[2048,384]{1,0:T(8,128)S(1)} %copy-done, bf16[2048,384]{1,0:T(8,128)(2,1)S(1)} %bitcast.44, bf16[384,1152]{1,0:T(8,128)(2,1)S(1)} %copy-done.3, bf16[2048,768]{1,0:T(8,128)(2,1)S(1)} %bitcast.38, bf16[2048,768]{1,0:T(8,128)(2,1)S(1)} %bitcast.37, bf16[2240,768]{1,0:T(8,128)(2,1)} %get-tuple-element.30), kind=kOutput, calls=%fused_computation.6 | convolution fusion | flops 1220542464 | bytes 16318464 | tf_op jit(solution)/shard_map/dot_general | solution.py:629
  104.9 13.9 %all-to-all-done.1 = bf16[128,40,128]{2,1,0:T(8,128)(2,1)S(1)} async-done(((bf16[128,40,128]{2,1,0:T(8,128)(2,1)}), bf16[128,40,128]{2,1,0:T(8,128)(2,1)S(1)}, u32[]{:S(2)}, u32[]{:S(2)}) %all-to-all-start.1) | async-done | bytes 1310752 | tf_op jit(solution)/shard_map/all_to_all | solution.py:537
  118.8 1.5 %unpack.1 = (f32[384,1152]{1,0:T(8,128)}, f32[384,384]{1,0:T(8,128)}) custom-call(bf16[5120,128]{1,0:T(8,128)(2,1)S(1)} %bitcast.36), custom_call_target="tpu_custom_call" | custom-call | tf_op jit(solution)/shard_map/unpack/pallas_call | solution.py:553
  (66 shorter events, 6.8 us)
Async XLA Ops:
  2.7 9.2 %collective-permute-start = (bf16[3,32,385]{2,1,0:T(8,128)(2,1)S(1)}, bf16[3,32,385]{2,1,0:T(8,128)(2,1)S(1)}, u32[]{:S(2)}, u32[]{:S(2)}) collective-permute-start(bf16[3,32,385]{2,1,0:T(8,128)(2,1)S(1)} %pad_maximum_fusion.4), channel_id=1, source_target_pairs={{0,16},{16,32},{32,48},{48,64},{64,80},{80,96},{96,112},{112,0},{1... | collective-permute-start | bytes 221768 | tf_op jit(solution)/shard_map/ppermute | solution.py:503
  5.2 6.8 %collective-permute-start.1 = (bf16[3,32,385]{2,1,0:T(8,128)(2,1)S(1)}, bf16[3,32,385]{2,1,0:T(8,128)(2,1)S(1)}, u32[]{:S(2)}, u32[]{:S(2)}) collective-permute-start(bf16[3,32,385]{2,1,0:T(8,128)(2,1)S(1)} %pad_maximum_fusion.5), channel_id=1, source_target_pairs={{16,0},{32,16},{48,32},{64,48},{80,64},{96,80},{112,96},{0,112},{1... | collective-permute-start | bytes 221768 | tf_op jit(solution)/shard_map/ppermute | solution.py:508
  10.0 14.6 %copy-start.6 = (s32[64,32]{1,0:T(8,128)}, s32[64,32]{1,0:T(8,128)S(1)}, u32[]{:S(2)}) copy-start(s32[64,32]{1,0:T(8,128)S(1)} %copy.85.tissue_ref) | copy-start | bytes 24580
  11.9 12.7 %copy-start.8 = (bf16[3,32,385]{2,1,0:T(8,128)(2,1)}, bf16[3,32,385]{2,1,0:T(8,128)(2,1)S(1)}, u32[]{:S(2)}) copy-start(bf16[3,32,385]{2,1,0:T(8,128)(2,1)S(1)} %collective-permute-done) | copy-start | bytes 221764
  12.0 12.6 %copy-start.9 = (bf16[3,32,385]{2,1,0:T(8,128)(2,1)}, bf16[3,32,385]{2,1,0:T(8,128)(2,1)S(1)}, u32[]{:S(2)}) copy-start(bf16[3,32,385]{2,1,0:T(8,128)(2,1)S(1)} %collective-permute-done.1) | copy-start | bytes 221764
  12.2 12.4 %collective-permute-start.2 = (bf16[70,3,385]{2,0,1:T(8,128)(2,1)S(1)}, bf16[70,3,385]{2,0,1:T(8,128)(2,1)S(1)}, u32[]{:S(2)}, u32[]{:S(2)}) collective-permute-start(bf16[70,3,385]{2,0,1:T(8,128)(2,1)S(1)} %get-tuple-element.21), channel_id=1, source_target_pairs={{0,1},{1,2},{2,3},{3,4},{4,5},{5,6},{6,7},{7,8},{8,9},{9,10},{10,1... | collective-permute-start | bytes 485108 | tf_op jit(solution)/shard_map/ppermute | solution.py:503
  16.7 7.9 %collective-permute-start.3 = (bf16[70,3,385]{2,0,1:T(8,128)(2,1)S(1)}, bf16[70,3,385]{2,0,1:T(8,128)(2,1)S(1)}, u32[]{:S(2)}, u32[]{:S(2)}) collective-permute-start(bf16[70,3,385]{2,0,1:T(8,128)(2,1)S(1)} %get-tuple-element.22), channel_id=1, source_target_pairs={{1,0},{2,1},{3,2},{4,3},{5,4},{6,5},{7,6},{8,7},{9,8},{10,9},{11,1... | collective-permute-start | bytes 485108 | tf_op jit(solution)/shard_map/ppermute | solution.py:508
  53.8 12.7 %copy-start.1 = (bf16[2048,384]{1,0:T(8,128)(2,1)S(1)}, bf16[2048,384]{1,0:T(8,128)(2,1)}, u32[]{:S(2)}) copy-start(bf16[2048,384]{1,0:T(8,128)(2,1)} %get-tuple-element.29) | copy-start | bytes 4718596
  53.8 20.6 %collective-permute-start.4 = (bf16[288,768]{1,0:T(8,128)(2,1)}, bf16[288,768]{1,0:T(8,128)(2,1)S(1)}, u32[]{:S(2)}, u32[]{:S(2)}) collective-permute-start(bf16[288,768]{1,0:T(8,128)(2,1)} %get-tuple-element.31), channel_id=1, source_target_pairs={{0,1},{1,2},{2,3},{3,4},{4,5},{5,6},{6,7},{7,8},{8,9},{9,10},{10,1... | collective-permute-start | bytes 1327112 | tf_op jit(solution)/shard_map/ppermute | solution.py:503
  57.1 17.6 %collective-permute-start.5 = (bf16[288,768]{1,0:T(8,128)(2,1)}, bf16[288,768]{1,0:T(8,128)(2,1)}, u32[]{:S(2)}, u32[]{:S(2)}) collective-permute-start(bf16[288,768]{1,0:T(8,128)(2,1)} %get-tuple-element.32), channel_id=1, source_target_pairs={{1,0},{2,1},{3,2},{4,3},{5,4},{6,5},{7,6},{8,7},{9,8},{10,9},{11,1... | collective-permute-start | bytes 1327112 | tf_op jit(solution)/shard_map/ppermute | solution.py:508
  57.1 32.2 %all-to-all-start = ((bf16[128,40,128]{2,1,0:T(8,128)(2,1)}), bf16[128,40,128]{2,1,0:T(8,128)(2,1)S(1)}, u32[]{:S(2)}, u32[]{:S(2)}) async-start(bf16[128,40,128]{2,1,0:T(8,128)(2,1)} %bitcast.46), calls=%async_computation | async-start | bytes 2621440 | tf_op jit(solution)/shard_map/all_to_all | solution.py:535
  66.5 5.6 %copy-start.2 = (bf16[64,32,384]{2,1,0:T(8,128)(2,1)S(1)}, bf16[64,32,384]{2,1,0:T(8,128)(2,1)}, u32[]{:S(2)}) copy-start(bf16[64,32,384]{2,1,0:T(8,128)(2,1)} %param.5) | copy-start | bytes 4718596
  66.5 5.6 %copy-start.5 = (bf16[2048,384]{1,0:T(8,128)(2,1)S(1)}, bf16[2048,384]{1,0:T(8,128)(2,1)}, u32[]{:S(2)}) copy-start(bf16[2048,384]{1,0:T(8,128)(2,1)} %get-tuple-element.28) | copy-start | bytes 4718596
  66.5 5.6 %copy-start.7 = (bf16[384,384]{1,0:T(8,128)(2,1)S(1)}, bf16[384,384]{1,0:T(8,128)(2,1)}, u32[]{:S(2)}) copy-start(bf16[384,384]{1,0:T(8,128)(2,1)} %wo_ref.1) | copy-start | bytes 884740
  77.1 20.8 %collective-permute-start.6 = (bf16[3,32,768]{2,1,0:T(8,128)(2,1)S(1)}, bf16[3,32,768]{2,1,0:T(8,128)(2,1)S(1)}, u32[]{:S(2)}, u32[]{:S(2)}) collective-permute-start(bf16[3,32,768]{2,1,0:T(8,128)(2,1)S(1)} %get-tuple-element.54), channel_id=1, source_target_pairs={{0,16},{16,32},{32,48},{48,64},{64,80},{80,96},{96,112},{112,0},{1... | collective-permute-start | bytes 442376 | tf_op jit(solution)/shard_map/ppermute | solution.py:503
  78.6 19.4 %collective-permute-start.7 = (bf16[3,32,768]{2,1,0:T(8,128)(2,1)S(1)}, bf16[3,32,768]{2,1,0:T(8,128)(2,1)S(1)}, u32[]{:S(2)}, u32[]{:S(2)}) collective-permute-start(bf16[3,32,768]{2,1,0:T(8,128)(2,1)S(1)} %get-tuple-element.55), channel_id=1, source_target_pairs={{16,0},{32,16},{48,32},{64,48},{80,64},{96,80},{112,96},{0,112},{1... | collective-permute-start | bytes 442376 | tf_op jit(solution)/shard_map/ppermute | solution.py:508
  90.6 28.2 %all-to-all-start.1 = ((bf16[128,40,128]{2,1,0:T(8,128)(2,1)}), bf16[128,40,128]{2,1,0:T(8,128)(2,1)S(1)}, u32[]{:S(2)}, u32[]{:S(2)}) async-start(bf16[128,40,128]{2,1,0:T(8,128)(2,1)} %bitcast.20), calls=%async_computation.1 | async-start | bytes 2621440 | tf_op jit(solution)/shard_map/all_to_all | solution.py:537
  97.0 1.9 %copy-start = (f32[2048,384]{1,0:T(8,128)S(1)}, f32[2048,384]{1,0:T(8,128)}, u32[]{:S(2)}) copy-start(f32[2048,384]{1,0:T(8,128)} %fusion.11) | copy-start | bytes 9437188
  97.1 2.1 %copy-start.3 = (bf16[384,1152]{1,0:T(8,128)(2,1)S(1)}, bf16[384,1152]{1,0:T(8,128)(2,1)}, u32[]{:S(2)}) copy-start(bf16[384,1152]{1,0:T(8,128)(2,1)} %wp_ref.3) | copy-start | bytes 2654212
  97.1 2.6 %copy-start.4 = (bf16[64,32,384]{2,1,0:T(8,128)(2,1)S(1)}, bf16[64,32,384]{2,1,0:T(8,128)(2,1)}, u32[]{:S(2)}) copy-start(bf16[64,32,384]{2,1,0:T(8,128)(2,1)} %param.7) | copy-start | bytes 4718596

commit v4 on v3

--- a/solution.py
+++ b/solution.py
@@ -18,7 +18,7 @@
 KEY_ROWS = TILE_ROWS + 2 * RADIUS
 CHUNK = 48
 SPAN = 2
-PROJECT_TILES = 4
+PROJECT_STEPS = 2
 FACTOR = HEAD ** (-0.5)
 NEG = float("-inf")
 MIB = 1024 * 1024
@@ -31,10 +31,9 @@
 
 
 def project_kernel(
-    tok_ref, cot_ref, wp_ref, wo_ref, tissue_ref, q_ref, kv_ref, g_ref, tok_t_ref, tis_ref
+    tok_ref, cot_ref, wp_ref, wo_ref, q_ref, kv_ref, g_ref, tok_t_ref
 ):
     width = tok_ref.shape[1]
-    tile = tis_ref.shape[1]
     tok = tok_ref[...]
     q = jnp.dot(tok, wp_ref[:, :width], preferred_element_type=f32).astype(bf16)
     q_ref[...] = (q * FACTOR).astype(bf16)
@@ -43,15 +42,11 @@
         cot_ref[...], wo_ref[...], dims(1, 1), preferred_element_type=f32
     ).astype(bf16)
     tok_t_ref[...] = tok.T
-    for i in range(tissue_ref.shape[0]):
-        across = jnp.broadcast_to(tissue_ref[i].astype(f32), (tile, tile)).T
-        tis_ref[i * tile : (i + 1) * tile] = jnp.where(across > 0.5, 0.0, NEG)
-
-
-def project(tok, cot, wp, wo, tissue):
+
+
+def project(tok, cot, wp, wo):
     count, width = tok.shape
-    tile = tissue.shape[2]
-    rows = PROJECT_TILES * tile
+    rows = count // PROJECT_STEPS
     block = lambda cols: pl.BlockSpec((rows, cols), lambda i: (i, 0))
     whole = lambda a: pl.BlockSpec(a.shape, lambda i: (0, 0))
     return pl.pallas_call(
@@ -62,34 +57,25 @@
             jax.ShapeDtypeStruct((count, 2 * width), bf16),
             jax.ShapeDtypeStruct((count, width), bf16),
             jax.ShapeDtypeStruct((width, count), bf16),
-            jax.ShapeDtypeStruct((count, tile), f32),
         ],
-        in_specs=[
-            block(width),
-            block(width),
-            whole(wp),
-            whole(wo),
-            pl.BlockSpec((PROJECT_TILES, 1, tile), lambda i: (i, 0, 0)),
-        ],
+        in_specs=[block(width), block(width), whole(wp), whole(wo)],
         out_specs=[
             block(width),
             block(2 * width),
             block(width),
             pl.BlockSpec((width, rows), lambda i: (0, i)),
-            block(tile),
         ],
         compiler_params=pltpu.CompilerParams(vmem_limit_bytes=56 * MIB),
         cost_estimate=pl.CostEstimate(
             flops=2 * count * width * 4 * width, bytes_accessed=14 * count * width, transcendentals=0
         ),
         name="project",
-    )(tok, cot, wp, wo, tissue)
+    )(tok, cot, wp, wo)
 
 
 def attention_kernel(
     extents,
-    above_ref, below_ref, side_ref, q_hbm, kv_hbm, g_hbm, tis_hbm, tok_t_hbm, cot_hbm, wp_ref, base_ref,
-    tissue_ref,
+    above_ref, below_ref, side_ref, q_hbm, kv_hbm, g_hbm, tok_t_hbm, cot_hbm, wp_ref, tissue_ref,
     att_hbm, dq_hbm, dkv_own_hbm, to_left_ref, to_right_ref, part_ref,
     cot_ref, q_ref, g_ref, tok_t_ref, att_ref, dq_ref, dkv_own_ref, dkv_side_ref,
     kv_own_s, kv_aux_s, tis_own_s, tis_aux_s, win_s, self_s, gate_s, acc_own, acc_aux, sems, *stage,
@@ -109,22 +95,34 @@
     most = 4 * HEAD
     x_s, dp_s, top_s, pl_s, sg_s = (stage[2 * i : 2 * i + 2] for i in range(5))
 
-    middle = pl.ds(halo, tokens_dev)
-    copies = [
-        pltpu.make_async_copy(source, target, sems.at[i])
-        for i, (source, target) in enumerate(
+    part = tokens_dev // 2
+    early = []
+    for i in range(2):
+        rows = pl.ds(i * part, part)
+        targets = (kv_own_s.at[pl.ds(halo + i * part, part)], q_ref.at[rows], g_ref.at[rows])
+        for k, (source, target) in enumerate(zip((kv_hbm, q_hbm, g_hbm), targets)):
+            early.append(pltpu.make_async_copy(source.at[rows], target, sems.at[3 * i + k]))
+    for copy in early:
+        copy.start()
+    late = [
+        pltpu.make_async_copy(tok_t_hbm, tok_t_ref, sems.at[6]),
+        pltpu.make_async_copy(cot_hbm, cot_ref, sems.at[7]),
+    ]
+    done = tokens_dev // 2
+    results = []
+    for i in range(2):
+        rows = pl.ds(i * done, done)
+        ext = rows if i == 0 else pl.ds(done, rows_own - done)
+        for k, (source, target, at) in enumerate(
             [
-                (kv_hbm, kv_own_s.at[middle]),
-                (tis_hbm, tis_own_s.at[middle]),
-                (q_hbm, q_ref),
-                (g_hbm, g_ref),
-                (tok_t_hbm, tok_t_ref),
-                (cot_hbm, cot_ref),
+                (att_ref, att_hbm, rows),
+                (dq_ref, dq_hbm, rows),
+                (dkv_own_ref, dkv_own_hbm, ext),
             ]
-        )
-    ]
-    for copy in copies:
-        copy.start()
+        ):
+            results.append(
+                pltpu.make_async_copy(source.at[at], target.at[at], sems.at[8 + 3 * i + k])
+            )
 
     def lanes(column):
         bias = jnp.where(column.astype(f32) > 0.5, 0.0, NEG)
@@ -137,7 +135,7 @@
 
     kv_own_s[:halo] = outer(above_ref)
     kv_own_s[halo + tokens_dev :] = outer(below_ref)
-    kv_side = outer(side_ref)
+    kv_aux_s[0] = outer(side_ref)
     tis_own_s[:halo] = lanes(above_ref[:, width : width + 1])
     tis_own_s[halo + tokens_dev :] = lanes(below_ref[:, width : width + 1])
     tis_side = lanes(side_ref[:, width : width + 1])
@@ -146,6 +144,9 @@
     query_row = lane // wide
     query_col = lane % wide
 
+    row_base = lax.axis_index("row") * (bands * TILE_ROWS)
+    col_base = lax.axis_index("col") * cols
+
     def window(key, query, base, extent):
         start = jnp.clip(base + query - RADIUS, 0, extent - KERNEL) - base
         return jnp.where((key >= start) & (key < start + KERNEL), 0.0, NEG)
@@ -153,29 +154,38 @@
     own_col = lax.broadcasted_iota(jnp.int32, (wide, 2 * tile), 0)
     aux_place = lax.broadcasted_iota(jnp.int32, (SIDE, 2 * tile), 0)
     far = -(2**20)
-    first_in = jnp.where(aux_place < RADIUS, aux_place - RADIUS, aux_place - RADIUS + wide)
-    second_in = jnp.where(
-        aux_place < RADIUS, aux_place - RADIUS + wide, aux_place - RADIUS + cols
+    first_col = jnp.where(aux_place < RADIUS, aux_place + wide, aux_place - 2 * RADIUS)
+    first_col = jnp.where(aux_place < 2 * RADIUS, first_col, far)
+    second_col = jnp.where(aux_place < RADIUS, aux_place + cols, aux_place + wide - SIDE)
+    second_col = jnp.where(
+        (aux_place < RADIUS) | (aux_place >= SIDE - RADIUS), second_col, far
     )
-    for half, aux_col in enumerate((first_in, second_in)):
-        aux_col = jnp.where(aux_place < 2 * RADIUS, aux_col, far)
+    for half, aux_col in enumerate((first_col, second_col)):
         shift = half * wide
-        own_in = window(own_col + shift, query_col + shift, base_ref[1], extents[1])
-        aux_in = window(aux_col, query_col + shift, base_ref[1], extents[1])
+        own_in = window(own_col + shift, query_col + shift, col_base, extents[1])
+        aux_in = window(aux_col, query_col + shift, col_base, extents[1])
         own_same = jnp.where(own_col == query_col, 0.0, NEG)
         for key_row in range(KEY_ROWS):
             own_rows = slice(key_row * wide, (key_row + 1) * wide)
             aux_rows = slice(own_keys + key_row * SIDE, own_keys + (key_row + 1) * SIDE)
             for kind, first in enumerate((0, 2 * TILE_ROWS, (bands - 1) * TILE_ROWS)):
-                row_in = window(key_row - RADIUS, query_row, base_ref[0] + first, extents[0])
+                row_in = window(key_row - RADIUS, query_row, row_base + first, extents[0])
                 win_s[half, kind, own_rows] = own_in + row_in
                 win_s[half, kind, aux_rows] = aux_in + row_in
             if half == 0:
                 row_same = jnp.where(query_row == key_row - RADIUS, 0.0, NEG)
                 self_s[own_rows] = own_same + row_same
                 self_s[aux_rows] = jnp.full((SIDE, 2 * tile), NEG, f32)
-    tissue = tissue_ref[...].astype(f32)
+    tissue = tissue_ref[...].astype(f32).T
     for index in range(bands):
+        row = jnp.concatenate(
+            [tissue[index * TILE_ROWS + k : index * TILE_ROWS + k + 1] for k in range(TILE_ROWS)],
+            axis=1,
+        )
+        across = jnp.broadcast_to(row, (2 * tile, band)).T
+        tis_own_s[halo + index * band : halo + (index + 1) * band] = jnp.where(
+            across > 0.5, 0.0, NEG
+        )
         for half in range(2):
             pieces = [
                 tissue[
@@ -187,7 +197,6 @@
             gate_s[2 * index + half] = jnp.concatenate(pieces * 2, axis=1)
 
     place = lax.broadcasted_iota(jnp.int32, (rows_aux, 1), 0) % SIDE
-    outer_left, outer_right = place < RADIUS, (place >= RADIUS) & (place < 2 * RADIUS)
 
     def parts(array, begin, count):
         across = array.shape[1]
@@ -199,25 +208,43 @@
         first = parts(own, wide, SIDE)
         second = parts(own, wide - SIDE, SIDE)
         return (
-            jnp.where(outer_left, side, pltpu.roll(first, RADIUS, 0)),
-            jnp.where(outer_right, side, pltpu.roll(second, rows_aux - SIDE + RADIUS, 0)),
-        )
-
-    for copy in copies[:2]:
-        copy.wait()
+            jnp.where(place < RADIUS, first, side),
+            jnp.where(place >= SIDE - RADIUS, second, side),
+        )
+
+    early[0].wait()
     tis_aux_s[0], tis_aux_s[1] = with_inner(tis_own_s[...], tis_side)
-    for begin in range(0, 2 * width, 256):
-        at = slice(begin, begin + 256)
-        one, two = with_inner(kv_own_s[:, at].astype(f32), kv_side[:, at].astype(f32))
-        kv_aux_s[0, :, at] = one.astype(bf16)
-        kv_aux_s[1, :, at] = two.astype(bf16)
+    two_rows = lax.broadcasted_iota(jnp.int32, (2 * SIDE, 1), 0) % SIDE
+
+    def fill(index, carry):
+        rows = pl.ds(pl.multiple_of(index * 2 * SIDE, 2 * SIDE), 2 * SIDE)
+        side = kv_aux_s[0, rows, :].astype(f32)
+
+        def inner(first):
+            at = [
+                pl.ds(pl.multiple_of(index * 2 * cols, 2 * cols) + row * cols + first, 2 * SIDE)
+                for row in range(2)
+            ]
+            return [kv_own_s[place, :].astype(f32) for place in at]
+
+        one = jnp.concatenate([block[:SIDE] for block in inner(wide)], axis=0)
+        two = jnp.concatenate([block[SIDE:] for block in inner(wide - 2 * SIDE)], axis=0)
+        kv_aux_s[0, rows, :] = jnp.where(two_rows < RADIUS, one, side).astype(bf16)
+        kv_aux_s[1, rows, :] = jnp.where(two_rows >= SIDE - RADIUS, two, side).astype(bf16)
+        return carry
+
+    row_pairs = rows_aux // (2 * SIDE)
+    ready = (part // cols + RADIUS) // 2
+    lax.fori_loop(0, ready, fill, 0, unroll=4)
     seen_rows = KEY_ROWS - TILE_ROWS
     acc_own[: seen_rows * cols] = jnp.zeros((seen_rows * cols, 2 * width), f32)
     acc_aux[:, : seen_rows * SIDE] = jnp.zeros((2, seen_rows * SIDE, 2 * width), f32)
     pl_s[1][...] = jnp.zeros((keys_all, HEADS * tile), bf16)
     sg_s[1][...] = jnp.zeros((keys_all, HEADS * tile), bf16)
-    for copy in copies[2:4]:
+    for copy in early[1:3]:
         copy.wait()
+    for copy in late:
+        copy.start()
 
     def split(block):
         head = lax.broadcasted_iota(jnp.int32, block.shape, 1) // HEAD
@@ -337,9 +364,48 @@
             acc_aux[half, aux_at(index, 0, seen_rows), at] += grad[own_keys:seen]
             acc_aux[half, aux_at(index, seen_rows, TILE_ROWS), at] = grad[seen:]
 
+    def merge(index, carry):
+        rows = pl.ds(pl.multiple_of(index * 2 * SIDE, 2 * SIDE), 2 * SIDE)
+        one, two = acc_aux[0, rows, :], acc_aux[1, rows, :]
+        dkv_side_ref[rows, :] = jnp.where(
+            two_rows < RADIUS, two, jnp.where(two_rows < 2 * RADIUS, one, 0.0)
+        ).astype(bf16)
+        one = jnp.where(two_rows < RADIUS, one, 0.0)
+        two = jnp.where(two_rows >= SIDE - RADIUS, two, 0.0)
+        for row in range(2):
+            start = pl.multiple_of(index * 2 * cols, 2 * cols) + row * cols
+            at = slice(row * SIDE, (row + 1) * SIDE)
+            own = acc_own[pl.ds(start, cols), :]
+            own = jnp.concatenate(
+                [
+                    own[: wide - SIDE],
+                    own[wide - SIDE : wide] + two[at],
+                    own[wide : wide + SIDE] + one[at],
+                    own[wide + SIDE :],
+                ],
+                axis=0,
+            )
+            dkv_own_ref[pl.ds(start, cols), :] = own.astype(bf16)
+        return carry
+
+    final = done // (2 * cols)
+    more_keys = (part // cols - TILE_ROWS - RADIUS) // (TILE_ROWS * SPAN)
+    first_done = bands // 2 // SPAN + 1
     score_stage(0, 0)
 
     def step(group, carry):
+        @pl.when(group == more_keys)
+        def _():
+            for copy in early[3:]:
+                copy.wait()
+            lax.fori_loop(ready, row_pairs, fill, 0, unroll=4)
+
+        @pl.when(group == first_done)
+        def _():
+            lax.fori_loop(0, final, merge, 0, unroll=4)
+            for copy in results[:3]:
+                copy.start()
+
         for slot in range(2 * SPAN):
             index = group * SPAN + slot // 2
             half = slot % 2
@@ -357,42 +423,15 @@
     lax.fori_loop(0, bands // SPAN, step, 0)
     product_stage(bands - 1, 1)
 
-    for begin in range(0, 2 * width, 128):
-        at = slice(begin, begin + 128)
-        one, two = acc_aux[0, :, at], acc_aux[1, :, at]
-        dkv_side_ref[:, at] = jnp.where(
-            outer_left, one, jnp.where(outer_right, two, 0.0)
-        ).astype(bf16)
-        first = jnp.where(place < RADIUS, pltpu.roll(one, rows_aux - RADIUS, 0), 0.0)
-        second = jnp.where(
-            place >= SIDE - RADIUS, pltpu.roll(two, SIDE - RADIUS, 0), 0.0
-        )
-        shape = (rows_aux // SIDE, SIDE, 128)
-        blank = lambda count: jnp.zeros((shape[0], count, 128), f32)
-        inner = jnp.concatenate(
-            [
-                blank(wide - SIDE),
-                second.reshape(shape),
-                first.reshape(shape),
-                blank(cols - wide - SIDE),
-            ],
-            axis=1,
-        ).reshape(rows_own, 128)
-        dkv_own_ref[:, at] = (acc_own[:, at] + inner).astype(bf16)
-    results = [
-        pltpu.make_async_copy(source, target, sems.at[6 + i])
-        for i, (source, target) in enumerate(
-            [(dkv_own_ref, dkv_own_hbm), (att_ref, att_hbm), (dq_ref, dq_hbm)]
-        )
-    ]
-    for copy in results:
+    lax.fori_loop(final, row_pairs, merge, 0, unroll=4)
+    for copy in results[3:]:
         copy.start()
-    for copy in copies[4:]:
+    for copy in late:
         copy.wait()
     send_row = lax.broadcasted_iota(jnp.int32, (128, 256), 0)
     side_row = lax.broadcasted_iota(jnp.int32, (128, 256), 1)
     place = (send_row // (SIDE // 2)) * SIDE + send_row % (SIDE // 2)
-    for begin, send_ref in ((0, to_left_ref), (RADIUS, to_right_ref)):
+    for begin, send_ref in ((RADIUS, to_left_ref), (0, to_right_ref)):
         pick = jnp.where(side_row == place + begin, 1.0, 0.0).astype(bf16)
         for first in range(0, send_ref.shape[0], 128):
             count = min(128, send_ref.shape[0] - first)
@@ -439,18 +478,17 @@
 
 
 def attention(
-    above, below, side, q, kv, g, tis, tok_t, cot, wp, base, tissue, extents, rows_part
+    above, below, side, q, kv, g, tok_t, cot, wp, tissue, extents, rows_part
 ):
     tokens_dev, width = cot.shape
     rows_own = tokens_dev + 2 * above.shape[0]
     rows_side = side.shape[0]
-    cols = tissue.shape[1]
+    cols = tissue.shape[0]
     tile = TILE_ROWS * cols // 2
     keys_all = KEY_ROWS * (cols // 2 + SIDE)
     rows_send = -(-rows_side // 32) * 16
     vmem = pl.BlockSpec(memory_space=pltpu.VMEM)
     hbm = pl.BlockSpec(memory_space=pl.ANY)
-    smem = pl.BlockSpec(memory_space=pltpu.SMEM)
     stage = []
     for shape, kind in (
         ((keys_all, HEADS * tile), f32),
@@ -470,7 +508,7 @@
             jax.ShapeDtypeStruct((rows_send, 2 * width), bf16),
             jax.ShapeDtypeStruct((rows_part, 128), bf16),
         ],
-        in_specs=[vmem] * 3 + [hbm] * 6 + [vmem, smem, vmem],
+        in_specs=[vmem] * 3 + [hbm] * 5 + [vmem] * 2,
         out_specs=[hbm] * 3 + [vmem] * 3,
         scratch_shapes=[
             pltpu.VMEM((tokens_dev, width), bf16),
@@ -490,12 +528,12 @@
             pltpu.VMEM((2 * tokens_dev // (2 * tile), 1, 2 * tile), f32),
             pltpu.VMEM((rows_own, 2 * width), f32),
             pltpu.VMEM((2, rows_side, 2 * width), f32),
-            pltpu.SemaphoreType.DMA((9,)),
+            pltpu.SemaphoreType.DMA((14,)),
         ]
         + stage,
         compiler_params=pltpu.CompilerParams(vmem_limit_bytes=56 * MIB),
         name="attention",
-    )(above, below, side, q, kv, g, tis, tok_t, cot, wp, base, tissue)
+    )(above, below, side, q, kv, g, tok_t, cot, wp, tissue)
 
 
 def to_next(array, axis):
@@ -566,7 +604,6 @@
     ext_rows = rows_dev + 2 * RADIUS
     devices = lax.axis_size("row") * lax.axis_size("col")
     rows_part = -(-4 * width * (width // 128) // (8 * devices)) * 8 * devices
-    tile = TILE_ROWS * cols_dev
     total_scale = float(rows_dev * lax.axis_size("row") * cols_dev * lax.axis_size("col")) ** (-0.5)
     token_rows = tokens.reshape(-1, width)
     cotangent_rows = cotangent.reshape(-1, width)
@@ -578,22 +615,15 @@
     right_cols = with_tissue(tokens[:, -RADIUS:], tissue[:, -RADIUS:])
     left_cols = jnp.concatenate([above[:, :RADIUS], left_cols, below[:, :RADIUS]], axis=0)
     right_cols = jnp.concatenate([above[:, -RADIUS:], right_cols, below[:, -RADIUS:]], axis=0)
-    tiles = tissue.reshape(-1, 1, tile)
-    token_rows, left_cols, right_cols = lax.optimization_barrier(
-        (token_rows, left_cols, right_cols)
-    )
     from_left = to_next(right_cols, "col")
     from_right = to_last(left_cols, "col")
     pad = jnp.zeros((ext_rows, SIDE - 2 * RADIUS, width + 1), bf16)
-    side = jnp.concatenate([from_left, from_right, pad], axis=1).reshape(-1, width + 1)
-
-    q, kv, g, tok_t, tis = project(
-        token_rows, cotangent_rows, packed_weight, output_weight, tiles
-    )
-    base = jnp.stack([lax.axis_index("row") * rows_dev, lax.axis_index("col") * cols_dev])
+    side = jnp.concatenate([from_right, from_left, pad], axis=1).reshape(-1, width + 1)
+
+    q, kv, g, tok_t = project(token_rows, cotangent_rows, packed_weight, output_weight)
     attended, dq, dkv_own, to_left, to_right, partial = attention(
         above.reshape(-1, width + 1), below.reshape(-1, width + 1), side,
-        q, kv, g, tis, tok_t, cotangent_rows, packed_weight, base.astype(jnp.int32), tissue,
+        q, kv, g, tok_t, cotangent_rows, packed_weight, tissue.T,
         (rows_dev * lax.axis_size("row"), cols_dev * lax.axis_size("col")), rows_part,
     )
 

time: 121 us -> 118 us (0.975)
  Pallas kernels: 38.8 us -> 36.9 us
  local copies, waits for them, and re-layouts: 10.7 us -> 9.26 us
    ppermute x4, starting transfers between devices: 5.07 us -> 7.71 us  [to_last(): lax.ppermute(array, axis, [((i + 1) % count, i) for i in range(count)])]
    ppermute x4, starting transfers between devices: 11.4 us -> 9.02 us  [to_next(): lax.ppermute(array, axis, [(i, (i + 1) % count) for i in range(count)])]
    pallas_call x1, Pallas kernels: 28.1 us -> 26.8 us  [attention(): pl.pallas_call(functools.partial(attention_kernel, extents), out_shape=[j...]
  transfers between devices with their start and end apart: 10 -> 10, of which waited for: 2 -> 3; matrix products, arithmetic and copies ran while one was open for 18% -> 16% of each run, Pallas kernels for 8% -> 7%
where the time goes in v4:
time: 118 us; the launch traced here: 117 us
  Pallas kernels  36.9 us (31%)
  starting transfers between devices  33.1 us (28%)
  waiting for transfers between devices  22.4 us (19%)
  matrix products  11.5 us (10%)
  local copies, waits for them, and re-layouts  9.26 us (8%)
  other arithmetic  3.19 us (3%)
    pallas_call x1, Pallas kernels, attention(): pl.pallas_call(functools.partial(attention_kernel, extents), out_shape=[j...  26.8 us
    all_to_all x1, waiting for transfers between devices, total_over_devices(): return lax.all_to_all(copies, axes, 0, 0, tiled=True).reshape(partial.shape)  13.9 us
    all_to_all x1, starting transfers between devices, total_over_devices(): lax.all_to_all(partial.reshape(count, -1, 128), axes, 0, 0, tiled=True)  10.2 us
    ppermute x4, starting transfers between devices, to_next(): lax.ppermute(array, axis, [(i, (i + 1) % count) for i in range(count)])  9.02 us
    all_to_all x1, waiting for transfers between devices, total_over_devices(): lax.all_to_all(partial.reshape(count, -1, 128), axes, 0, 0, tiled=True)  8.24 us
    ppermute x4, starting transfers between devices, to_last(): lax.ppermute(array, axis, [((i + 1) % count, i) for i in range(count)])  7.71 us
    pallas_call x1, Pallas kernels, project(): pl.pallas_call(project_kernel, grid=(count // rows,), out_shape=[jax.Shap...  7.26 us
    all_to_all x1, starting transfers between devices, total_over_devices(): return lax.all_to_all(copies, axes, 0, 0, tiled=True).reshape(partial.shape)  6.19 us
  transfers between devices with their start and end apart: 10, of which 3 were waited for; matrix products, arithmetic and copies ran while one was open for 16% of the time, Pallas kernels for 7%

profile of v4, /device:TPU:1, one launch (start us, length us, event | category | flops | bytes accessed | tf_op | source)
XLA Modules:
  0.0 117.3 jit_solution(1404488026860367190)
XLA Ops:
  2.7 2.1 %collective-permute-start = (bf16[3,32,385]{2,1,0:T(8,128)(2,1)S(1)}, bf16[3,32,385]{2,1,0:T(8,128)(2,1)S(1)}, u32[]{:S(2)}, u32[]{:S(2)}) collective-permute-start(bf16[3,32,385]{2,1,0:T(8,128)(2,1)S(1)} %pad_maximum_fusion.4), channel_id=1, source_target_pairs={{0,16},{16,32},{32,48},{48,64},{64,80},{80,96},{96,112},{112,0},{1... | collective-permute-start | bytes 221768 | tf_op jit(solution)/shard_map/ppermute | solution.py:541
  5.2 2.7 %collective-permute-start.1 = (bf16[3,32,385]{2,1,0:T(8,128)(2,1)S(1)}, bf16[3,32,385]{2,1,0:T(8,128)(2,1)S(1)}, u32[]{:S(2)}, u32[]{:S(2)}) collective-permute-start(bf16[3,32,385]{2,1,0:T(8,128)(2,1)S(1)} %pad_maximum_fusion.5), channel_id=1, source_target_pairs={{16,0},{32,16},{48,32},{64,48},{80,64},{96,80},{112,96},{0,112},{1... | collective-permute-start | bytes 221768 | tf_op jit(solution)/shard_map/ppermute | solution.py:546
  7.9 1.3 %fusion.14 = (bf16[64,3,384]{2,1,0:T(4,128)(2,1)S(1)}, bf16[64,3,384]{2,1,0:T(4,128)(2,1)S(1)}) fusion(bf16[64,32,384]{2,1,0:T(8,128)(2,1)} %param.5), kind=kLoop, calls=%fused_computation.27 | loop fusion | bytes 589824 | tf_op jit(solution)/shard_map/slice | solution.py:614
  10.2 1.3 %collective-permute-start.2 = (bf16[70,3,385]{2,0,1:T(8,128)(2,1)S(1)}, bf16[70,3,385]{2,0,1:T(8,128)(2,1)S(1)}, u32[]{:S(2)}, u32[]{:S(2)}) collective-permute-start(bf16[70,3,385]{2,0,1:T(8,128)(2,1)S(1)} %pad_maximum_fusion.2), channel_id=1, source_target_pairs={{1,0},{2,1},{3,2},{4,3},{5,4},{6,5},{7,6},{8,7},{9,8},{10,9},{11,1... | collective-permute-start | bytes 485108 | tf_op jit(solution)/shard_map/ppermute | solution.py:546
  11.5 3.4 %collective-permute-start.3 = (bf16[70,3,385]{2,0,1:T(8,128)(2,1)S(1)}, bf16[70,3,385]{2,0,1:T(8,128)(2,1)S(1)}, u32[]{:S(2)}, u32[]{:S(2)}) collective-permute-start(bf16[70,3,385]{2,0,1:T(8,128)(2,1)S(1)} %pad_maximum_fusion.3), channel_id=1, source_target_pairs={{0,1},{1,2},{2,3},{3,4},{4,5},{5,6},{6,7},{7,8},{8,9},{9,10},{10,1... | collective-permute-start | bytes 485108 | tf_op jit(solution)/shard_map/ppermute | solution.py:541
  14.9 7.3 %project.1 = (bf16[2048,384]{1,0:T(8,128)(2,1)}, bf16[2048,768]{1,0:T(8,128)(2,1)}, bf16[2048,384]{1,0:T(8,128)(2,1)}, bf16[384,2048]{1,0:T(8,128)(2,1)}) custom-call(bf16[2048,384]{1,0:T(8,128)(2,1)} %bitcast.37, bf16[2048,384]{1,0:T(8,128)(2,1)} %bitcast.41, bf16[384,1152]{1,0:T(8,128)(2,1)} %wp_ref.3, bf16[384,384]{1,0:T(8,128)(2,1)} %wo_ref.1), custom_call_target="tpu_custom_call" | custom-call | flops 2415919104 | bytes 11010048 | tf_op jit(solution)/shard_map/project/pallas_call | solution.py:52
  22.4 1.0 copy.72
  23.3 26.8 %attention.1 = (bf16[2048,384]{1,0:T(8,128)(2,1)}, bf16[2048,384]{1,0:T(8,128)(2,1)}, bf16[2240,768]{1,0:T(8,128)(2,1)}, bf16[288,768]{1,0:T(8,128)(2,1)}, bf16[...) custom-call(bf16[96,385]{1,0:T(8,128)(2,1)} %bitcast.47, bf16[96,385]{1,0:T(8,128)(2,1)} %bitcast.48, ...), custom_call_target="tpu_custom_call" | custom-call | tf_op jit(solution)/shard_map/attention/pallas_call | solution.py:501
  50.1 2.1 %collective-permute-start.4 = (bf16[288,768]{1,0:T(8,128)(2,1)}, bf16[288,768]{1,0:T(8,128)(2,1)S(1)}, u32[]{:S(2)}, u32[]{:S(2)}) collective-permute-start(bf16[288,768]{1,0:T(8,128)(2,1)} %get-tuple-element.23), channel_id=1, source_target_pairs={{0,1},{1,2},{2,3},{3,4},{4,5},{5,6},{6,7},{7,8},{8,9},{9,10},{10,1... | collective-permute-start | bytes 1327112 | tf_op jit(solution)/shard_map/ppermute | solution.py:541
  52.2 1.4 %collective-permute-start.5 = (bf16[288,768]{1,0:T(8,128)(2,1)}, bf16[288,768]{1,0:T(8,128)(2,1)}, u32[]{:S(2)}, u32[]{:S(2)}) collective-permute-start(bf16[288,768]{1,0:T(8,128)(2,1)} %get-tuple-element.24), channel_id=1, source_target_pairs={{1,0},{2,1},{3,2},{4,3},{5,4},{6,5},{7,6},{8,7},{9,8},{10,9},{11,1... | collective-permute-start | bytes 1327112 | tf_op jit(solution)/shard_map/ppermute | solution.py:546
  53.5 10.2 %all-to-all-start = ((bf16[128,40,128]{2,1,0:T(8,128)(2,1)}), bf16[128,40,128]{2,1,0:T(8,128)(2,1)S(1)}, u32[]{:S(2)}, u32[]{:S(2)}) async-start(bf16[128,40,128]{2,1,0:T(8,128)(2,1)} %bitcast.44), calls=%async_computation | async-start | bytes 2621440 | tf_op jit(solution)/shard_map/all_to_all | solution.py:573
  63.8 4.0 %fusion.11 = f32[2048,384]{1,0:T(8,128)} fusion(bf16[2048,384]{1,0:T(8,128)(2,1)S(1)} %copy-done.1, bf16[384,1152]{1,0:T(8,128)(2,1)} %wp_ref.3), kind=kOutput, calls=%fused_computation.16 | convolution fusion | flops 603979776 | bytes 5013504 | tf_op jit(solution)/shard_map/dot_general | solution.py:658
  67.8 1.7 %fusion.13 = (bf16[96,768]{1,0:T(8,128)(2,1)S(1)}, bf16[96,768]{1,0:T(8,128)(2,1)}) fusion(bf16[2240,768]{1,0:T(8,128)(2,1)} %get-tuple-element.22), kind=kLoop, calls=%fused_computation.26 | loop fusion | bytes 589824 | tf_op jit(solution)/shard_map/slice | solution.py:643
  69.5 2.3 %add_convert_fusion.1 = bf16[2048,384]{1,0:T(8,128)(2,1)} fusion(bf16[2048,384]{1,0:T(8,128)(2,1)S(1)} %bitcast.38, bf16[2048,384]{1,0:T(8,128)(2,1)S(1)} %copy-done.3, bf16[384,384]{1,0:T(8,128)(2,1)S(1)} %copy-done.6), kind=kOutput, calls=%fused_computation.8 | convolution fusion | flops 606339072 | bytes 5013504 | tf_op jit(solution)/shard_map/dot_general | solution.py:654
  72.1 1.0 slice.125
  73.4 1.1 fusion.10
  74.4 1.5 %collective-permute-start.6 = (bf16[3,32,768]{2,1,0:T(8,128)(2,1)S(1)}, bf16[3,32,768]{2,1,0:T(8,128)(2,1)S(1)}, u32[]{:S(2)}, u32[]{:S(2)}) collective-permute-start(bf16[3,32,768]{2,1,0:T(8,128)(2,1)S(1)} %get-tuple-element.46), channel_id=1, source_target_pairs={{0,16},{16,32},{32,48},{48,64},{64,80},{80,96},{96,112},{112,0},{1... | collective-permute-start | bytes 442376 | tf_op jit(solution)/shard_map/ppermute | solution.py:541
  75.9 2.4 %collective-permute-start.7 = (bf16[3,32,768]{2,1,0:T(8,128)(2,1)S(1)}, bf16[3,32,768]{2,1,0:T(8,128)(2,1)S(1)}, u32[]{:S(2)}, u32[]{:S(2)}) collective-permute-start(bf16[3,32,768]{2,1,0:T(8,128)(2,1)S(1)} %get-tuple-element.47), channel_id=1, source_target_pairs={{16,0},{32,16},{48,32},{64,48},{80,64},{96,80},{112,96},{0,112},{1... | collective-permute-start | bytes 442376 | tf_op jit(solution)/shard_map/ppermute | solution.py:546
  78.3 8.2 %all-to-all-done = bf16[128,40,128]{2,1,0:T(8,128)(2,1)S(1)} async-done(((bf16[128,40,128]{2,1,0:T(8,128)(2,1)}), bf16[128,40,128]{2,1,0:T(8,128)(2,1)S(1)}, u32[]{:S(2)}, u32[]{:S(2)}) %all-to-all-start) | async-done | bytes 1310752 | tf_op jit(solution)/shard_map/all_to_all | solution.py:573
  86.5 1.3 %summed_copies.1 = bf16[5120,128]{1,0:T(8,128)(2,1)} custom-call(bf16[5120,128]{1,0:T(8,128)(2,1)S(1)} %bitcast.33), custom_call_target="tpu_custom_call" | custom-call | tf_op jit(solution)/shard_map/summed_copies/pallas_call | solution.py:562
  87.8 6.2 %all-to-all-start.1 = ((bf16[128,40,128]{2,1,0:T(8,128)(2,1)}), bf16[128,40,128]{2,1,0:T(8,128)(2,1)S(1)}, u32[]{:S(2)}, u32[]{:S(2)}) async-start(bf16[128,40,128]{2,1,0:T(8,128)(2,1)} %bitcast.18), calls=%async_computation.1 | async-start | bytes 2621440 | tf_op jit(solution)/shard_map/all_to_all | solution.py:575
  96.6 5.2 %add_convert_fusion = bf16[2048,384]{1,0:T(8,128)(2,1)} fusion(f32[2048,384]{1,0:T(8,128)S(1)} %copy-done, bf16[2048,384]{1,0:T(8,128)(2,1)S(1)} %bitcast.43, bf16[384,1152]{1,0:T(8,128)(2,1)S(1)} %copy-done.4, bf16[2048,768]{1,0:T(8,128)(2,1)S(1)} %bitcast.36, bf16[2048,768]{1,0:T(8,128)(2,1)S(1)} %bitcast.35, bf16[2240,768]{1,0:T(8,128)(2,1)} %get-tuple-element.22), kind=kOutput, calls=%fused_computation.6 | convolution fusion | flops 1220542464 | bytes 16318464 | tf_op jit(solution)/shard_map/dot_general | solution.py:659
  101.9 13.9 %all-to-all-done.1 = bf16[128,40,128]{2,1,0:T(8,128)(2,1)S(1)} async-done(((bf16[128,40,128]{2,1,0:T(8,128)(2,1)}), bf16[128,40,128]{2,1,0:T(8,128)(2,1)S(1)}, u32[]{:S(2)}, u32[]{:S(2)}) %all-to-all-start.1) | async-done | bytes 1310752 | tf_op jit(solution)/shard_map/all_to_all | solution.py:575
  115.8 1.5 %unpack.1 = (f32[384,1152]{1,0:T(8,128)}, f32[384,384]{1,0:T(8,128)}) custom-call(bf16[5120,128]{1,0:T(8,128)(2,1)S(1)} %bitcast.34), custom_call_target="tpu_custom_call" | custom-call | tf_op jit(solution)/shard_map/unpack/pallas_call | solution.py:591
  (61 shorter events, 6.7 us)
Async XLA Ops:
  2.7 7.3 %collective-permute-start = (bf16[3,32,385]{2,1,0:T(8,128)(2,1)S(1)}, bf16[3,32,385]{2,1,0:T(8,128)(2,1)S(1)}, u32[]{:S(2)}, u32[]{:S(2)}) collective-permute-start(bf16[3,32,385]{2,1,0:T(8,128)(2,1)S(1)} %pad_maximum_fusion.4), channel_id=1, source_target_pairs={{0,16},{16,32},{32,48},{48,64},{64,80},{80,96},{96,112},{112,0},{1... | collective-permute-start | bytes 221768 | tf_op jit(solution)/shard_map/ppermute | solution.py:541
  5.2 4.8 %collective-permute-start.1 = (bf16[3,32,385]{2,1,0:T(8,128)(2,1)S(1)}, bf16[3,32,385]{2,1,0:T(8,128)(2,1)S(1)}, u32[]{:S(2)}, u32[]{:S(2)}) collective-permute-start(bf16[3,32,385]{2,1,0:T(8,128)(2,1)S(1)} %pad_maximum_fusion.5), channel_id=1, source_target_pairs={{16,0},{32,16},{48,32},{64,48},{80,64},{96,80},{112,96},{0,112},{1... | collective-permute-start | bytes 221768 | tf_op jit(solution)/shard_map/ppermute | solution.py:546
  10.0 12.2 %copy-start.7 = (bf16[3,32,385]{2,1,0:T(8,128)(2,1)}, bf16[3,32,385]{2,1,0:T(8,128)(2,1)S(1)}, u32[]{:S(2)}) copy-start(bf16[3,32,385]{2,1,0:T(8,128)(2,1)S(1)} %collective-permute-done) | copy-start | bytes 221764
  10.0 12.2 %copy-start.8 = (bf16[3,32,385]{2,1,0:T(8,128)(2,1)}, bf16[3,32,385]{2,1,0:T(8,128)(2,1)S(1)}, u32[]{:S(2)}) copy-start(bf16[3,32,385]{2,1,0:T(8,128)(2,1)S(1)} %collective-permute-done.1) | copy-start | bytes 221764
  10.2 12.1 %collective-permute-start.2 = (bf16[70,3,385]{2,0,1:T(8,128)(2,1)S(1)}, bf16[70,3,385]{2,0,1:T(8,128)(2,1)S(1)}, u32[]{:S(2)}, u32[]{:S(2)}) collective-permute-start(bf16[70,3,385]{2,0,1:T(8,128)(2,1)S(1)} %pad_maximum_fusion.2), channel_id=1, source_target_pairs={{1,0},{2,1},{3,2},{4,3},{5,4},{6,5},{7,6},{8,7},{9,8},{10,9},{11,1... | collective-permute-start | bytes 485108 | tf_op jit(solution)/shard_map/ppermute | solution.py:546
  11.5 10.7 %collective-permute-start.3 = (bf16[70,3,385]{2,0,1:T(8,128)(2,1)S(1)}, bf16[70,3,385]{2,0,1:T(8,128)(2,1)S(1)}, u32[]{:S(2)}, u32[]{:S(2)}) collective-permute-start(bf16[70,3,385]{2,0,1:T(8,128)(2,1)S(1)} %pad_maximum_fusion.3), channel_id=1, source_target_pairs={{0,1},{1,2},{2,3},{3,4},{4,5},{5,6},{6,7},{7,8},{8,9},{9,10},{10,1... | collective-permute-start | bytes 485108 | tf_op jit(solution)/shard_map/ppermute | solution.py:541
  50.1 13.7 %copy-start.1 = (bf16[2048,384]{1,0:T(8,128)(2,1)S(1)}, bf16[2048,384]{1,0:T(8,128)(2,1)}, u32[]{:S(2)}) copy-start(bf16[2048,384]{1,0:T(8,128)(2,1)} %get-tuple-element.21) | copy-start | bytes 4718596
  50.1 21.6 %collective-permute-start.4 = (bf16[288,768]{1,0:T(8,128)(2,1)}, bf16[288,768]{1,0:T(8,128)(2,1)S(1)}, u32[]{:S(2)}, u32[]{:S(2)}) collective-permute-start(bf16[288,768]{1,0:T(8,128)(2,1)} %get-tuple-element.23), channel_id=1, source_target_pairs={{0,1},{1,2},{2,3},{3,4},{4,5},{5,6},{6,7},{7,8},{8,9},{9,10},{10,1... | collective-permute-start | bytes 1327112 | tf_op jit(solution)/shard_map/ppermute | solution.py:541
  52.2 19.9 %collective-permute-start.5 = (bf16[288,768]{1,0:T(8,128)(2,1)}, bf16[288,768]{1,0:T(8,128)(2,1)}, u32[]{:S(2)}, u32[]{:S(2)}) collective-permute-start(bf16[288,768]{1,0:T(8,128)(2,1)} %get-tuple-element.24), channel_id=1, source_target_pairs={{1,0},{2,1},{3,2},{4,3},{5,4},{6,5},{7,6},{8,7},{9,8},{10,9},{11,1... | collective-permute-start | bytes 1327112 | tf_op jit(solution)/shard_map/ppermute | solution.py:546
  53.5 33.0 %all-to-all-start = ((bf16[128,40,128]{2,1,0:T(8,128)(2,1)}), bf16[128,40,128]{2,1,0:T(8,128)(2,1)S(1)}, u32[]{:S(2)}, u32[]{:S(2)}) async-start(bf16[128,40,128]{2,1,0:T(8,128)(2,1)} %bitcast.44), calls=%async_computation | async-start | bytes 2621440 | tf_op jit(solution)/shard_map/all_to_all | solution.py:573
  63.8 5.7 %copy-start.2 = (bf16[64,32,384]{2,1,0:T(8,128)(2,1)S(1)}, bf16[64,32,384]{2,1,0:T(8,128)(2,1)}, u32[]{:S(2)}) copy-start(bf16[64,32,384]{2,1,0:T(8,128)(2,1)} %param.5) | copy-start | bytes 4718596
  63.8 5.7 %copy-start.3 = (bf16[2048,384]{1,0:T(8,128)(2,1)S(1)}, bf16[2048,384]{1,0:T(8,128)(2,1)}, u32[]{:S(2)}) copy-start(bf16[2048,384]{1,0:T(8,128)(2,1)} %get-tuple-element.20) | copy-start | bytes 4718596
  63.8 5.7 %copy-start.6 = (bf16[384,384]{1,0:T(8,128)(2,1)S(1)}, bf16[384,384]{1,0:T(8,128)(2,1)}, u32[]{:S(2)}) copy-start(bf16[384,384]{1,0:T(8,128)(2,1)} %wo_ref.1) | copy-start | bytes 884740
  74.4 20.5 %collective-permute-start.6 = (bf16[3,32,768]{2,1,0:T(8,128)(2,1)S(1)}, bf16[3,32,768]{2,1,0:T(8,128)(2,1)S(1)}, u32[]{:S(2)}, u32[]{:S(2)}) collective-permute-start(bf16[3,32,768]{2,1,0:T(8,128)(2,1)S(1)} %get-tuple-element.46), channel_id=1, source_target_pairs={{0,16},{16,32},{32,48},{48,64},{64,80},{80,96},{96,112},{112,0},{1... | collective-permute-start | bytes 442376 | tf_op jit(solution)/shard_map/ppermute | solution.py:541
  75.9 19.0 %collective-permute-start.7 = (bf16[3,32,768]{2,1,0:T(8,128)(2,1)S(1)}, bf16[3,32,768]{2,1,0:T(8,128)(2,1)S(1)}, u32[]{:S(2)}, u32[]{:S(2)}) collective-permute-start(bf16[3,32,768]{2,1,0:T(8,128)(2,1)S(1)} %get-tuple-element.47), channel_id=1, source_target_pairs={{16,0},{32,16},{48,32},{64,48},{80,64},{96,80},{112,96},{0,112},{1... | collective-permute-start | bytes 442376 | tf_op jit(solution)/shard_map/ppermute | solution.py:546
  87.8 28.0 %all-to-all-start.1 = ((bf16[128,40,128]{2,1,0:T(8,128)(2,1)}), bf16[128,40,128]{2,1,0:T(8,128)(2,1)S(1)}, u32[]{:S(2)}, u32[]{:S(2)}) async-start(bf16[128,40,128]{2,1,0:T(8,128)(2,1)} %bitcast.18), calls=%async_computation.1 | async-start | bytes 2621440 | tf_op jit(solution)/shard_map/all_to_all | solution.py:575
  94.0 1.9 %copy-start = (f32[2048,384]{1,0:T(8,128)S(1)}, f32[2048,384]{1,0:T(8,128)}, u32[]{:S(2)}) copy-start(f32[2048,384]{1,0:T(8,128)} %fusion.11) | copy-start | bytes 9437188
  94.0 2.1 %copy-start.4 = (bf16[384,1152]{1,0:T(8,128)(2,1)S(1)}, bf16[384,1152]{1,0:T(8,128)(2,1)}, u32[]{:S(2)}) copy-start(bf16[384,1152]{1,0:T(8,128)(2,1)} %wp_ref.3) | copy-start | bytes 2654212
  94.0 2.6 %copy-start.5 = (bf16[64,32,384]{2,1,0:T(8,128)(2,1)S(1)}, bf16[64,32,384]{2,1,0:T(8,128)(2,1)}, u32[]{:S(2)}) copy-start(bf16[64,32,384]{2,1,0:T(8,128)(2,1)} %param.7) | copy-start | bytes 4718596

commit v5 on v4

--- a/solution.py
+++ b/solution.py
@@ -17,7 +17,7 @@
 TILE_ROWS = 4
 KEY_ROWS = TILE_ROWS + 2 * RADIUS
 CHUNK = 48
-SPAN = 2
+SPAN = 4
 PROJECT_STEPS = 2
 FACTOR = HEAD ** (-0.5)
 NEG = float("-inf")

time: 118 us -> 117 us (level)
  no operation moved by 1% of the time
where the time goes in v5:
time: 117 us
  Pallas kernels  36.2 us (31%)
  starting transfers between devices  33.1 us (28%)
  waiting for transfers between devices  22.4 us (19%)
  matrix products  11.5 us (10%)
  local copies, waits for them, and re-layouts  9.26 us (8%)
  other arithmetic  3.19 us (3%)
    pallas_call x1, Pallas kernels, attention(): pl.pallas_call(functools.partial(attention_kernel, extents), out_shape=[j...  26.1 us
    all_to_all x1, waiting for transfers between devices, total_over_devices(): return lax.all_to_all(copies, axes, 0, 0, tiled=True).reshape(partial.shape)  13.9 us
    all_to_all x1, starting transfers between devices, total_over_devices(): lax.all_to_all(partial.reshape(count, -1, 128), axes, 0, 0, tiled=True)  10.2 us
    ppermute x4, starting transfers between devices, to_next(): lax.ppermute(array, axis, [(i, (i + 1) % count) for i in range(count)])  8.83 us
    all_to_all x1, waiting for transfers between devices, total_over_devices(): lax.all_to_all(partial.reshape(count, -1, 128), axes, 0, 0, tiled=True)  8.24 us
    ppermute x4, starting transfers between devices, to_last(): lax.ppermute(array, axis, [((i + 1) % count, i) for i in range(count)])  7.9 us
    pallas_call x1, Pallas kernels, project(): pl.pallas_call(project_kernel, grid=(count // rows,), out_shape=[jax.Shap...  7.26 us
    all_to_all x1, starting transfers between devices, total_over_devices(): return lax.all_to_all(copies, axes, 0, 0, tiled=True).reshape(partial.shape)  6.19 us
  transfers between devices with their start and end apart: 10, of which 3 were waited for; matrix products, arithmetic and copies ran while one was open for 16% of the time, Pallas kernels for 7%

profile of v5, /device:TPU:1, one launch (start us, length us, event | category | flops | bytes accessed | tf_op | source)
XLA Modules:
  0.0 116.6 jit_solution(18302099705761445065)
XLA Ops:
  2.7 2.1 %collective-permute-start = (bf16[3,32,385]{2,1,0:T(8,128)(2,1)S(1)}, bf16[3,32,385]{2,1,0:T(8,128)(2,1)S(1)}, u32[]{:S(2)}, u32[]{:S(2)}) collective-permute-start(bf16[3,32,385]{2,1,0:T(8,128)(2,1)S(1)} %pad_maximum_fusion.4), channel_id=1, source_target_pairs={{0,16},{16,32},{32,48},{48,64},{64,80},{80,96},{96,112},{112,0},{1... | collective-permute-start | bytes 221768 | tf_op jit(solution)/shard_map/ppermute | solution.py:541
  5.2 2.7 %collective-permute-start.1 = (bf16[3,32,385]{2,1,0:T(8,128)(2,1)S(1)}, bf16[3,32,385]{2,1,0:T(8,128)(2,1)S(1)}, u32[]{:S(2)}, u32[]{:S(2)}) collective-permute-start(bf16[3,32,385]{2,1,0:T(8,128)(2,1)S(1)} %pad_maximum_fusion.5), channel_id=1, source_target_pairs={{16,0},{32,16},{48,32},{64,48},{80,64},{96,80},{112,96},{0,112},{1... | collective-permute-start | bytes 221768 | tf_op jit(solution)/shard_map/ppermute | solution.py:546
  7.9 1.3 %fusion.14 = (bf16[64,3,384]{2,1,0:T(4,128)(2,1)S(1)}, bf16[64,3,384]{2,1,0:T(4,128)(2,1)S(1)}) fusion(bf16[64,32,384]{2,1,0:T(8,128)(2,1)} %param.5), kind=kLoop, calls=%fused_computation.27 | loop fusion | bytes 589824 | tf_op jit(solution)/shard_map/slice | solution.py:614
  10.2 1.3 %collective-permute-start.2 = (bf16[70,3,385]{2,0,1:T(8,128)(2,1)S(1)}, bf16[70,3,385]{2,0,1:T(8,128)(2,1)S(1)}, u32[]{:S(2)}, u32[]{:S(2)}) collective-permute-start(bf16[70,3,385]{2,0,1:T(8,128)(2,1)S(1)} %pad_maximum_fusion.2), channel_id=1, source_target_pairs={{1,0},{2,1},{3,2},{4,3},{5,4},{6,5},{7,6},{8,7},{9,8},{10,9},{11,1... | collective-permute-start | bytes 485108 | tf_op jit(solution)/shard_map/ppermute | solution.py:546
  11.5 3.6 %collective-permute-start.3 = (bf16[70,3,385]{2,0,1:T(8,128)(2,1)S(1)}, bf16[70,3,385]{2,0,1:T(8,128)(2,1)S(1)}, u32[]{:S(2)}, u32[]{:S(2)}) collective-permute-start(bf16[70,3,385]{2,0,1:T(8,128)(2,1)S(1)} %pad_maximum_fusion.3), channel_id=1, source_target_pairs={{0,1},{1,2},{2,3},{3,4},{4,5},{5,6},{6,7},{7,8},{8,9},{9,10},{10,1... | collective-permute-start | bytes 485108 | tf_op jit(solution)/shard_map/ppermute | solution.py:541
  15.1 7.3 %project.1 = (bf16[2048,384]{1,0:T(8,128)(2,1)}, bf16[2048,768]{1,0:T(8,128)(2,1)}, bf16[2048,384]{1,0:T(8,128)(2,1)}, bf16[384,2048]{1,0:T(8,128)(2,1)}) custom-call(bf16[2048,384]{1,0:T(8,128)(2,1)} %bitcast.37, bf16[2048,384]{1,0:T(8,128)(2,1)} %bitcast.41, bf16[384,1152]{1,0:T(8,128)(2,1)} %wp_ref.3, bf16[384,384]{1,0:T(8,128)(2,1)} %wo_ref.1), custom_call_target="tpu_custom_call" | custom-call | flops 2415919104 | bytes 11010048 | tf_op jit(solution)/shard_map/project/pallas_call | solution.py:52
  22.5 1.0 copy.72
  23.5 26.1 %attention.1 = (bf16[2048,384]{1,0:T(8,128)(2,1)}, bf16[2048,384]{1,0:T(8,128)(2,1)}, bf16[2240,768]{1,0:T(8,128)(2,1)}, bf16[288,768]{1,0:T(8,128)(2,1)}, bf16[...) custom-call(bf16[96,385]{1,0:T(8,128)(2,1)} %bitcast.47, bf16[96,385]{1,0:T(8,128)(2,1)} %bitcast.48, ...), custom_call_target="tpu_custom_call" | custom-call | tf_op jit(solution)/shard_map/attention/pallas_call | solution.py:501
  49.6 1.7 %collective-permute-start.4 = (bf16[288,768]{1,0:T(8,128)(2,1)}, bf16[288,768]{1,0:T(8,128)(2,1)S(1)}, u32[]{:S(2)}, u32[]{:S(2)}) collective-permute-start(bf16[288,768]{1,0:T(8,128)(2,1)} %get-tuple-element.23), channel_id=1, source_target_pairs={{0,1},{1,2},{2,3},{3,4},{4,5},{5,6},{6,7},{7,8},{8,9},{9,10},{10,1... | collective-permute-start | bytes 1327112 | tf_op jit(solution)/shard_map/ppermute | solution.py:541
  51.3 1.5 %collective-permute-start.5 = (bf16[288,768]{1,0:T(8,128)(2,1)}, bf16[288,768]{1,0:T(8,128)(2,1)}, u32[]{:S(2)}, u32[]{:S(2)}) collective-permute-start(bf16[288,768]{1,0:T(8,128)(2,1)} %get-tuple-element.24), channel_id=1, source_target_pairs={{1,0},{2,1},{3,2},{4,3},{5,4},{6,5},{7,6},{8,7},{9,8},{10,9},{11,1... | collective-permute-start | bytes 1327112 | tf_op jit(solution)/shard_map/ppermute | solution.py:546
  52.9 10.2 %all-to-all-start = ((bf16[128,40,128]{2,1,0:T(8,128)(2,1)}), bf16[128,40,128]{2,1,0:T(8,128)(2,1)S(1)}, u32[]{:S(2)}, u32[]{:S(2)}) async-start(bf16[128,40,128]{2,1,0:T(8,128)(2,1)} %bitcast.44), calls=%async_computation | async-start | bytes 2621440 | tf_op jit(solution)/shard_map/all_to_all | solution.py:573
  63.2 4.0 %fusion.11 = f32[2048,384]{1,0:T(8,128)} fusion(bf16[2048,384]{1,0:T(8,128)(2,1)S(1)} %copy-done.1, bf16[384,1152]{1,0:T(8,128)(2,1)} %wp_ref.3), kind=kOutput, calls=%fused_computation.16 | convolution fusion | flops 603979776 | bytes 5013504 | tf_op jit(solution)/shard_map/dot_general | solution.py:658
  67.1 1.7 %fusion.13 = (bf16[96,768]{1,0:T(8,128)(2,1)S(1)}, bf16[96,768]{1,0:T(8,128)(2,1)}) fusion(bf16[2240,768]{1,0:T(8,128)(2,1)} %get-tuple-element.22), kind=kLoop, calls=%fused_computation.26 | loop fusion | bytes 589824 | tf_op jit(solution)/shard_map/slice | solution.py:643
  68.8 2.3 %add_convert_fusion.1 = bf16[2048,384]{1,0:T(8,128)(2,1)} fusion(bf16[2048,384]{1,0:T(8,128)(2,1)S(1)} %bitcast.38, bf16[2048,384]{1,0:T(8,128)(2,1)S(1)} %copy-done.3, bf16[384,384]{1,0:T(8,128)(2,1)S(1)} %copy-done.6), kind=kOutput, calls=%fused_computation.8 | convolution fusion | flops 606339072 | bytes 5013504 | tf_op jit(solution)/shard_map/dot_general | solution.py:654
  71.4 1.0 slice.125
  72.7 1.1 fusion.10
  73.8 1.5 %collective-permute-start.6 = (bf16[3,32,768]{2,1,0:T(8,128)(2,1)S(1)}, bf16[3,32,768]{2,1,0:T(8,128)(2,1)S(1)}, u32[]{:S(2)}, u32[]{:S(2)}) collective-permute-start(bf16[3,32,768]{2,1,0:T(8,128)(2,1)S(1)} %get-tuple-element.46), channel_id=1, source_target_pairs={{0,16},{16,32},{32,48},{48,64},{64,80},{80,96},{96,112},{112,0},{1... | collective-permute-start | bytes 442376 | tf_op jit(solution)/shard_map/ppermute | solution.py:541
  75.2 2.4 %collective-permute-start.7 = (bf16[3,32,768]{2,1,0:T(8,128)(2,1)S(1)}, bf16[3,32,768]{2,1,0:T(8,128)(2,1)S(1)}, u32[]{:S(2)}, u32[]{:S(2)}) collective-permute-start(bf16[3,32,768]{2,1,0:T(8,128)(2,1)S(1)} %get-tuple-element.47), channel_id=1, source_target_pairs={{16,0},{32,16},{48,32},{64,48},{80,64},{96,80},{112,96},{0,112},{1... | collective-permute-start | bytes 442376 | tf_op jit(solution)/shard_map/ppermute | solution.py:546
  77.6 8.2 %all-to-all-done = bf16[128,40,128]{2,1,0:T(8,128)(2,1)S(1)} async-done(((bf16[128,40,128]{2,1,0:T(8,128)(2,1)}), bf16[128,40,128]{2,1,0:T(8,128)(2,1)S(1)}, u32[]{:S(2)}, u32[]{:S(2)}) %all-to-all-start) | async-done | bytes 1310752 | tf_op jit(solution)/shard_map/all_to_all | solution.py:573
  85.8 1.3 %summed_copies.1 = bf16[5120,128]{1,0:T(8,128)(2,1)} custom-call(bf16[5120,128]{1,0:T(8,128)(2,1)S(1)} %bitcast.33), custom_call_target="tpu_custom_call" | custom-call | tf_op jit(solution)/shard_map/summed_copies/pallas_call | solution.py:562
  87.2 6.2 %all-to-all-start.1 = ((bf16[128,40,128]{2,1,0:T(8,128)(2,1)}), bf16[128,40,128]{2,1,0:T(8,128)(2,1)S(1)}, u32[]{:S(2)}, u32[]{:S(2)}) async-start(bf16[128,40,128]{2,1,0:T(8,128)(2,1)} %bitcast.18), calls=%async_computation.1 | async-start | bytes 2621440 | tf_op jit(solution)/shard_map/all_to_all | solution.py:575
  96.0 5.2 %add_convert_fusion = bf16[2048,384]{1,0:T(8,128)(2,1)} fusion(f32[2048,384]{1,0:T(8,128)S(1)} %copy-done, bf16[2048,384]{1,0:T(8,128)(2,1)S(1)} %bitcast.43, bf16[384,1152]{1,0:T(8,128)(2,1)S(1)} %copy-done.4, bf16[2048,768]{1,0:T(8,128)(2,1)S(1)} %bitcast.36, bf16[2048,768]{1,0:T(8,128)(2,1)S(1)} %bitcast.35, bf16[2240,768]{1,0:T(8,128)(2,1)} %get-tuple-element.22), kind=kOutput, calls=%fused_computation.6 | convolution fusion | flops 1220542464 | bytes 16318464 | tf_op jit(solution)/shard_map/dot_general | solution.py:659
  101.2 13.9 %all-to-all-done.1 = bf16[128,40,128]{2,1,0:T(8,128)(2,1)S(1)} async-done(((bf16[128,40,128]{2,1,0:T(8,128)(2,1)}), bf16[128,40,128]{2,1,0:T(8,128)(2,1)S(1)}, u32[]{:S(2)}, u32[]{:S(2)}) %all-to-all-start.1) | async-done | bytes 1310752 | tf_op jit(solution)/shard_map/all_to_all | solution.py:575
  115.1 1.5 %unpack.1 = (f32[384,1152]{1,0:T(8,128)}, f32[384,384]{1,0:T(8,128)}) custom-call(bf16[5120,128]{1,0:T(8,128)(2,1)S(1)} %bitcast.34), custom_call_target="tpu_custom_call" | custom-call | tf_op jit(solution)/shard_map/unpack/pallas_call | solution.py:591
  (61 shorter events, 6.7 us)
Async XLA Ops:
  2.7 7.3 %collective-permute-start = (bf16[3,32,385]{2,1,0:T(8,128)(2,1)S(1)}, bf16[3,32,385]{2,1,0:T(8,128)(2,1)S(1)}, u32[]{:S(2)}, u32[]{:S(2)}) collective-permute-start(bf16[3,32,385]{2,1,0:T(8,128)(2,1)S(1)} %pad_maximum_fusion.4), channel_id=1, source_target_pairs={{0,16},{16,32},{32,48},{48,64},{64,80},{80,96},{96,112},{112,0},{1... | collective-permute-start | bytes 221768 | tf_op jit(solution)/shard_map/ppermute | solution.py:541
  5.2 4.8 %collective-permute-start.1 = (bf16[3,32,385]{2,1,0:T(8,128)(2,1)S(1)}, bf16[3,32,385]{2,1,0:T(8,128)(2,1)S(1)}, u32[]{:S(2)}, u32[]{:S(2)}) collective-permute-start(bf16[3,32,385]{2,1,0:T(8,128)(2,1)S(1)} %pad_maximum_fusion.5), channel_id=1, source_target_pairs={{16,0},{32,16},{48,32},{64,48},{80,64},{96,80},{112,96},{0,112},{1... | collective-permute-start | bytes 221768 | tf_op jit(solution)/shard_map/ppermute | solution.py:546
  10.0 12.4 %copy-start.7 = (bf16[3,32,385]{2,1,0:T(8,128)(2,1)}, bf16[3,32,385]{2,1,0:T(8,128)(2,1)S(1)}, u32[]{:S(2)}) copy-start(bf16[3,32,385]{2,1,0:T(8,128)(2,1)S(1)} %collective-permute-done) | copy-start | bytes 221764
  10.0 12.4 %copy-start.8 = (bf16[3,32,385]{2,1,0:T(8,128)(2,1)}, bf16[3,32,385]{2,1,0:T(8,128)(2,1)S(1)}, u32[]{:S(2)}) copy-start(bf16[3,32,385]{2,1,0:T(8,128)(2,1)S(1)} %collective-permute-done.1) | copy-start | bytes 221764
  10.2 12.3 %collective-permute-start.2 = (bf16[70,3,385]{2,0,1:T(8,128)(2,1)S(1)}, bf16[70,3,385]{2,0,1:T(8,128)(2,1)S(1)}, u32[]{:S(2)}, u32[]{:S(2)}) collective-permute-start(bf16[70,3,385]{2,0,1:T(8,128)(2,1)S(1)} %pad_maximum_fusion.2), channel_id=1, source_target_pairs={{1,0},{2,1},{3,2},{4,3},{5,4},{6,5},{7,6},{8,7},{9,8},{10,9},{11,1... | collective-permute-start | bytes 485108 | tf_op jit(solution)/shard_map/ppermute | solution.py:546
  11.5 10.9 %collective-permute-start.3 = (bf16[70,3,385]{2,0,1:T(8,128)(2,1)S(1)}, bf16[70,3,385]{2,0,1:T(8,128)(2,1)S(1)}, u32[]{:S(2)}, u32[]{:S(2)}) collective-permute-start(bf16[70,3,385]{2,0,1:T(8,128)(2,1)S(1)} %pad_maximum_fusion.3), channel_id=1, source_target_pairs={{0,1},{1,2},{2,3},{3,4},{4,5},{5,6},{6,7},{7,8},{8,9},{9,10},{10,1... | collective-permute-start | bytes 485108 | tf_op jit(solution)/shard_map/ppermute | solution.py:541
  49.6 13.5 %copy-start.1 = (bf16[2048,384]{1,0:T(8,128)(2,1)S(1)}, bf16[2048,384]{1,0:T(8,128)(2,1)}, u32[]{:S(2)}) copy-start(bf16[2048,384]{1,0:T(8,128)(2,1)} %get-tuple-element.21) | copy-start | bytes 4718596
  49.6 21.5 %collective-permute-start.4 = (bf16[288,768]{1,0:T(8,128)(2,1)}, bf16[288,768]{1,0:T(8,128)(2,1)S(1)}, u32[]{:S(2)}, u32[]{:S(2)}) collective-permute-start(bf16[288,768]{1,0:T(8,128)(2,1)} %get-tuple-element.23), channel_id=1, source_target_pairs={{0,1},{1,2},{2,3},{3,4},{4,5},{5,6},{6,7},{7,8},{8,9},{9,10},{10,1... | collective-permute-start | bytes 1327112 | tf_op jit(solution)/shard_map/ppermute | solution.py:541
  51.3 20.1 %collective-permute-start.5 = (bf16[288,768]{1,0:T(8,128)(2,1)}, bf16[288,768]{1,0:T(8,128)(2,1)}, u32[]{:S(2)}, u32[]{:S(2)}) collective-permute-start(bf16[288,768]{1,0:T(8,128)(2,1)} %get-tuple-element.24), channel_id=1, source_target_pairs={{1,0},{2,1},{3,2},{4,3},{5,4},{6,5},{7,6},{8,7},{9,8},{10,9},{11,1... | collective-permute-start | bytes 1327112 | tf_op jit(solution)/shard_map/ppermute | solution.py:546
  52.9 33.0 %all-to-all-start = ((bf16[128,40,128]{2,1,0:T(8,128)(2,1)}), bf16[128,40,128]{2,1,0:T(8,128)(2,1)S(1)}, u32[]{:S(2)}, u32[]{:S(2)}) async-start(bf16[128,40,128]{2,1,0:T(8,128)(2,1)} %bitcast.44), calls=%async_computation | async-start | bytes 2621440 | tf_op jit(solution)/shard_map/all_to_all | solution.py:573
  63.1 5.7 %copy-start.2 = (bf16[64,32,384]{2,1,0:T(8,128)(2,1)S(1)}, bf16[64,32,384]{2,1,0:T(8,128)(2,1)}, u32[]{:S(2)}) copy-start(bf16[64,32,384]{2,1,0:T(8,128)(2,1)} %param.5) | copy-start | bytes 4718596
  63.1 5.7 %copy-start.3 = (bf16[2048,384]{1,0:T(8,128)(2,1)S(1)}, bf16[2048,384]{1,0:T(8,128)(2,1)}, u32[]{:S(2)}) copy-start(bf16[2048,384]{1,0:T(8,128)(2,1)} %get-tuple-element.20) | copy-start | bytes 4718596
  63.1 5.7 %copy-start.6 = (bf16[384,384]{1,0:T(8,128)(2,1)S(1)}, bf16[384,384]{1,0:T(8,128)(2,1)}, u32[]{:S(2)}) copy-start(bf16[384,384]{1,0:T(8,128)(2,1)} %wo_ref.1) | copy-start | bytes 884740
  73.8 20.5 %collective-permute-start.6 = (bf16[3,32,768]{2,1,0:T(8,128)(2,1)S(1)}, bf16[3,32,768]{2,1,0:T(8,128)(2,1)S(1)}, u32[]{:S(2)}, u32[]{:S(2)}) collective-permute-start(bf16[3,32,768]{2,1,0:T(8,128)(2,1)S(1)} %get-tuple-element.46), channel_id=1, source_target_pairs={{0,16},{16,32},{32,48},{48,64},{64,80},{80,96},{96,112},{112,0},{1... | collective-permute-start | bytes 442376 | tf_op jit(solution)/shard_map/ppermute | solution.py:541
  75.2 19.0 %collective-permute-start.7 = (bf16[3,32,768]{2,1,0:T(8,128)(2,1)S(1)}, bf16[3,32,768]{2,1,0:T(8,128)(2,1)S(1)}, u32[]{:S(2)}, u32[]{:S(2)}) collective-permute-start(bf16[3,32,768]{2,1,0:T(8,128)(2,1)S(1)} %get-tuple-element.47), channel_id=1, source_target_pairs={{16,0},{32,16},{48,32},{64,48},{80,64},{96,80},{112,96},{0,112},{1... | collective-permute-start | bytes 442376 | tf_op jit(solution)/shard_map/ppermute | solution.py:546
  87.2 28.0 %all-to-all-start.1 = ((bf16[128,40,128]{2,1,0:T(8,128)(2,1)}), bf16[128,40,128]{2,1,0:T(8,128)(2,1)S(1)}, u32[]{:S(2)}, u32[]{:S(2)}) async-start(bf16[128,40,128]{2,1,0:T(8,128)(2,1)} %bitcast.18), calls=%async_computation.1 | async-start | bytes 2621440 | tf_op jit(solution)/shard_map/all_to_all | solution.py:575
  93.4 1.9 %copy-start = (f32[2048,384]{1,0:T(8,128)S(1)}, f32[2048,384]{1,0:T(8,128)}, u32[]{:S(2)}) copy-start(f32[2048,384]{1,0:T(8,128)} %fusion.11) | copy-start | bytes 9437188
  93.4 2.1 %copy-start.4 = (bf16[384,1152]{1,0:T(8,128)(2,1)S(1)}, bf16[384,1152]{1,0:T(8,128)(2,1)}, u32[]{:S(2)}) copy-start(bf16[384,1152]{1,0:T(8,128)(2,1)} %wp_ref.3) | copy-start | bytes 2654212
  93.4 2.6 %copy-start.5 = (bf16[64,32,384]{2,1,0:T(8,128)(2,1)S(1)}, bf16[64,32,384]{2,1,0:T(8,128)(2,1)}, u32[]{:S(2)}) copy-start(bf16[64,32,384]{2,1,0:T(8,128)(2,1)} %param.7) | copy-start | bytes 4718596

commit v6 on v5

--- a/solution.py
+++ b/solution.py
@@ -577,22 +577,35 @@
 
 def unpack_kernel(scale, whole_ref, packed_ref, output_ref):
     width = output_ref.shape[0]
-    for block in range((packed_ref.shape[1] + output_ref.shape[1]) // 128):
-        value = whole_ref[block * width : (block + 1) * width].astype(f32) * scale
-        column = block * 128
-        if column < packed_ref.shape[1]:
-            packed_ref[:, column : column + 128] = value
-        else:
-            column -= packed_ref.shape[1]
-            output_ref[:, column : column + 128] = value
+
+    def put(out_ref):
+        for block in range(width // 128):
+            value = whole_ref[block * width : (block + 1) * width].astype(f32) * scale
+            out_ref[:, block * 128 : (block + 1) * 128] = value
+
+    last = pl.program_id(0) == 3
+
+    @pl.when(jnp.logical_not(last))
+    def _():
+        put(packed_ref)
+
+    @pl.when(last)
+    def _():
+        put(output_ref)
 
 
 def unpack(whole, width, scale):
     return pl.pallas_call(
         functools.partial(unpack_kernel, scale),
+        grid=(4,),
         out_shape=[
             jax.ShapeDtypeStruct((width, 3 * width), f32),
             jax.ShapeDtypeStruct((width, width), f32),
+        ],
+        in_specs=[pl.BlockSpec((width * (width // 128), 128), lambda i: (i, 0))],
+        out_specs=[
+            pl.BlockSpec((width, width), lambda i: (0, jnp.minimum(i, 2))),
+            pl.BlockSpec((width, width), lambda i: (0, 0)),
         ],
         compiler_params=pltpu.CompilerParams(vmem_limit_bytes=24 * MIB),
         name="unpack",

time: 117 us -> 118 us (level)
  no operation moved by 1% of the time
where the time goes in v6:
time: 118 us; the launch traced here: 117 us
  Pallas kernels  36.8 us (31%)
  starting transfers between devices  33.1 us (28%)
  waiting for transfers between devices  22.4 us (19%)
  matrix products  11.5 us (10%)
  local copies, waits for them, and re-layouts  9.26 us (8%)
  other arithmetic  3.19 us (3%)
    pallas_call x1, Pallas kernels, attention(): pl.pallas_call(functools.partial(attention_kernel, extents), out_shape=[j...  26.1 us
    all_to_all x1, waiting for transfers between devices, total_over_devices(): return lax.all_to_all(copies, axes, 0, 0, tiled=True).reshape(partial.shape)  13.9 us
    all_to_all x1, starting transfers between devices, total_over_devices(): lax.all_to_all(partial.reshape(count, -1, 128), axes, 0, 0, tiled=True)  10.2 us
    ppermute x4, starting transfers between devices, to_next(): lax.ppermute(array, axis, [(i, (i + 1) % count) for i in range(count)])  8.83 us
    all_to_all x1, waiting for transfers between devices, total_over_devices(): lax.all_to_all(partial.reshape(count, -1, 128), axes, 0, 0, tiled=True)  8.24 us
    ppermute x4, starting transfers between devices, to_last(): lax.ppermute(array, axis, [((i + 1) % count, i) for i in range(count)])  7.9 us
    pallas_call x1, Pallas kernels, project(): pl.pallas_call(project_kernel, grid=(count // rows,), out_shape=[jax.Shap...  7.26 us
    all_to_all x1, starting transfers between devices, total_over_devices(): return lax.all_to_all(copies, axes, 0, 0, tiled=True).reshape(partial.shape)  6.19 us
  transfers between devices with their start and end apart: 10, of which 3 were waited for; matrix products, arithmetic and copies ran while one was open for 16% of the time, Pallas kernels for 7%

profile of v6, /device:TPU:1, one launch (start us, length us, event | category | flops | bytes accessed | tf_op | source)
XLA Modules:
  0.0 117.2 jit_solution(11350781943153818086)
XLA Ops:
  2.7 2.1 %collective-permute-start = (bf16[3,32,385]{2,1,0:T(8,128)(2,1)S(1)}, bf16[3,32,385]{2,1,0:T(8,128)(2,1)S(1)}, u32[]{:S(2)}, u32[]{:S(2)}) collective-permute-start(bf16[3,32,385]{2,1,0:T(8,128)(2,1)S(1)} %pad_maximum_fusion.4), channel_id=1, source_target_pairs={{0,16},{16,32},{32,48},{48,64},{64,80},{80,96},{96,112},{112,0},{1... | collective-permute-start | bytes 221768 | tf_op jit(solution)/shard_map/ppermute | solution.py:541
  5.2 2.7 %collective-permute-start.1 = (bf16[3,32,385]{2,1,0:T(8,128)(2,1)S(1)}, bf16[3,32,385]{2,1,0:T(8,128)(2,1)S(1)}, u32[]{:S(2)}, u32[]{:S(2)}) collective-permute-start(bf16[3,32,385]{2,1,0:T(8,128)(2,1)S(1)} %pad_maximum_fusion.5), channel_id=1, source_target_pairs={{16,0},{32,16},{48,32},{64,48},{80,64},{96,80},{112,96},{0,112},{1... | collective-permute-start | bytes 221768 | tf_op jit(solution)/shard_map/ppermute | solution.py:546
  7.9 1.3 %fusion.14 = (bf16[64,3,384]{2,1,0:T(4,128)(2,1)S(1)}, bf16[64,3,384]{2,1,0:T(4,128)(2,1)S(1)}) fusion(bf16[64,32,384]{2,1,0:T(8,128)(2,1)} %param.5), kind=kLoop, calls=%fused_computation.27 | loop fusion | bytes 589824 | tf_op jit(solution)/shard_map/slice | solution.py:627
  10.2 1.3 %collective-permute-start.2 = (bf16[70,3,385]{2,0,1:T(8,128)(2,1)S(1)}, bf16[70,3,385]{2,0,1:T(8,128)(2,1)S(1)}, u32[]{:S(2)}, u32[]{:S(2)}) collective-permute-start(bf16[70,3,385]{2,0,1:T(8,128)(2,1)S(1)} %pad_maximum_fusion.2), channel_id=1, source_target_pairs={{1,0},{2,1},{3,2},{4,3},{5,4},{6,5},{7,6},{8,7},{9,8},{10,9},{11,1... | collective-permute-start | bytes 485108 | tf_op jit(solution)/shard_map/ppermute | solution.py:546
  11.5 3.6 %collective-permute-start.3 = (bf16[70,3,385]{2,0,1:T(8,128)(2,1)S(1)}, bf16[70,3,385]{2,0,1:T(8,128)(2,1)S(1)}, u32[]{:S(2)}, u32[]{:S(2)}) collective-permute-start(bf16[70,3,385]{2,0,1:T(8,128)(2,1)S(1)} %pad_maximum_fusion.3), channel_id=1, source_target_pairs={{0,1},{1,2},{2,3},{3,4},{4,5},{5,6},{6,7},{7,8},{8,9},{9,10},{10,1... | collective-permute-start | bytes 485108 | tf_op jit(solution)/shard_map/ppermute | solution.py:541
  15.1 7.3 %project.1 = (bf16[2048,384]{1,0:T(8,128)(2,1)}, bf16[2048,768]{1,0:T(8,128)(2,1)}, bf16[2048,384]{1,0:T(8,128)(2,1)}, bf16[384,2048]{1,0:T(8,128)(2,1)}) custom-call(bf16[2048,384]{1,0:T(8,128)(2,1)} %bitcast.37, bf16[2048,384]{1,0:T(8,128)(2,1)} %bitcast.41, bf16[384,1152]{1,0:T(8,128)(2,1)} %wp_ref.3, bf16[384,384]{1,0:T(8,128)(2,1)} %wo_ref.1), custom_call_target="tpu_custom_call" | custom-call | flops 2415919104 | bytes 11010048 | tf_op jit(solution)/shard_map/project/pallas_call | solution.py:52
  22.5 1.0 copy.72
  23.5 26.1 %attention.1 = (bf16[2048,384]{1,0:T(8,128)(2,1)}, bf16[2048,384]{1,0:T(8,128)(2,1)}, bf16[2240,768]{1,0:T(8,128)(2,1)}, bf16[288,768]{1,0:T(8,128)(2,1)}, bf16[...) custom-call(bf16[96,385]{1,0:T(8,128)(2,1)} %bitcast.47, bf16[96,385]{1,0:T(8,128)(2,1)} %bitcast.48, ...), custom_call_target="tpu_custom_call" | custom-call | tf_op jit(solution)/shard_map/attention/pallas_call | solution.py:501
  49.6 1.7 %collective-permute-start.4 = (bf16[288,768]{1,0:T(8,128)(2,1)}, bf16[288,768]{1,0:T(8,128)(2,1)S(1)}, u32[]{:S(2)}, u32[]{:S(2)}) collective-permute-start(bf16[288,768]{1,0:T(8,128)(2,1)} %get-tuple-element.23), channel_id=1, source_target_pairs={{0,1},{1,2},{2,3},{3,4},{4,5},{5,6},{6,7},{7,8},{8,9},{9,10},{10,1... | collective-permute-start | bytes 1327112 | tf_op jit(solution)/shard_map/ppermute | solution.py:541
  51.3 1.5 %collective-permute-start.5 = (bf16[288,768]{1,0:T(8,128)(2,1)}, bf16[288,768]{1,0:T(8,128)(2,1)}, u32[]{:S(2)}, u32[]{:S(2)}) collective-permute-start(bf16[288,768]{1,0:T(8,128)(2,1)} %get-tuple-element.24), channel_id=1, source_target_pairs={{1,0},{2,1},{3,2},{4,3},{5,4},{6,5},{7,6},{8,7},{9,8},{10,9},{11,1... | collective-permute-start | bytes 1327112 | tf_op jit(solution)/shard_map/ppermute | solution.py:546
  52.9 10.2 %all-to-all-start = ((bf16[128,40,128]{2,1,0:T(8,128)(2,1)}), bf16[128,40,128]{2,1,0:T(8,128)(2,1)S(1)}, u32[]{:S(2)}, u32[]{:S(2)}) async-start(bf16[128,40,128]{2,1,0:T(8,128)(2,1)} %bitcast.44), calls=%async_computation | async-start | bytes 2621440 | tf_op jit(solution)/shard_map/all_to_all | solution.py:573
  63.2 4.0 %fusion.11 = f32[2048,384]{1,0:T(8,128)} fusion(bf16[2048,384]{1,0:T(8,128)(2,1)S(1)} %copy-done.1, bf16[384,1152]{1,0:T(8,128)(2,1)} %wp_ref.3), kind=kOutput, calls=%fused_computation.16 | convolution fusion | flops 603979776 | bytes 5013504 | tf_op jit(solution)/shard_map/dot_general | solution.py:671
  67.1 1.7 %fusion.13 = (bf16[96,768]{1,0:T(8,128)(2,1)S(1)}, bf16[96,768]{1,0:T(8,128)(2,1)}) fusion(bf16[2240,768]{1,0:T(8,128)(2,1)} %get-tuple-element.22), kind=kLoop, calls=%fused_computation.26 | loop fusion | bytes 589824 | tf_op jit(solution)/shard_map/slice | solution.py:656
  68.8 2.3 %add_convert_fusion.1 = bf16[2048,384]{1,0:T(8,128)(2,1)} fusion(bf16[2048,384]{1,0:T(8,128)(2,1)S(1)} %bitcast.38, bf16[2048,384]{1,0:T(8,128)(2,1)S(1)} %copy-done.3, bf16[384,384]{1,0:T(8,128)(2,1)S(1)} %copy-done.6), kind=kOutput, calls=%fused_computation.8 | convolution fusion | flops 606339072 | bytes 5013504 | tf_op jit(solution)/shard_map/dot_general | solution.py:667
  71.4 1.0 slice.125
  72.7 1.1 fusion.10
  73.8 1.5 %collective-permute-start.6 = (bf16[3,32,768]{2,1,0:T(8,128)(2,1)S(1)}, bf16[3,32,768]{2,1,0:T(8,128)(2,1)S(1)}, u32[]{:S(2)}, u32[]{:S(2)}) collective-permute-start(bf16[3,32,768]{2,1,0:T(8,128)(2,1)S(1)} %get-tuple-element.46), channel_id=1, source_target_pairs={{0,16},{16,32},{32,48},{48,64},{64,80},{80,96},{96,112},{112,0},{1... | collective-permute-start | bytes 442376 | tf_op jit(solution)/shard_map/ppermute | solution.py:541
  75.2 2.4 %collective-permute-start.7 = (bf16[3,32,768]{2,1,0:T(8,128)(2,1)S(1)}, bf16[3,32,768]{2,1,0:T(8,128)(2,1)S(1)}, u32[]{:S(2)}, u32[]{:S(2)}) collective-permute-start(bf16[3,32,768]{2,1,0:T(8,128)(2,1)S(1)} %get-tuple-element.47), channel_id=1, source_target_pairs={{16,0},{32,16},{48,32},{64,48},{80,64},{96,80},{112,96},{0,112},{1... | collective-permute-start | bytes 442376 | tf_op jit(solution)/shard_map/ppermute | solution.py:546
  77.6 8.2 %all-to-all-done = bf16[128,40,128]{2,1,0:T(8,128)(2,1)S(1)} async-done(((bf16[128,40,128]{2,1,0:T(8,128)(2,1)}), bf16[128,40,128]{2,1,0:T(8,128)(2,1)S(1)}, u32[]{:S(2)}, u32[]{:S(2)}) %all-to-all-start) | async-done | bytes 1310752 | tf_op jit(solution)/shard_map/all_to_all | solution.py:573
  85.8 1.3 %summed_copies.1 = bf16[5120,128]{1,0:T(8,128)(2,1)} custom-call(bf16[5120,128]{1,0:T(8,128)(2,1)S(1)} %bitcast.33), custom_call_target="tpu_custom_call" | custom-call | tf_op jit(solution)/shard_map/summed_copies/pallas_call | solution.py:562
  87.2 6.2 %all-to-all-start.1 = ((bf16[128,40,128]{2,1,0:T(8,128)(2,1)}), bf16[128,40,128]{2,1,0:T(8,128)(2,1)S(1)}, u32[]{:S(2)}, u32[]{:S(2)}) async-start(bf16[128,40,128]{2,1,0:T(8,128)(2,1)} %bitcast.18), calls=%async_computation.1 | async-start | bytes 2621440 | tf_op jit(solution)/shard_map/all_to_all | solution.py:575
  96.0 5.2 %add_convert_fusion = bf16[2048,384]{1,0:T(8,128)(2,1)} fusion(f32[2048,384]{1,0:T(8,128)S(1)} %copy-done, bf16[2048,384]{1,0:T(8,128)(2,1)S(1)} %bitcast.43, bf16[384,1152]{1,0:T(8,128)(2,1)S(1)} %copy-done.4, bf16[2048,768]{1,0:T(8,128)(2,1)S(1)} %bitcast.36, bf16[2048,768]{1,0:T(8,128)(2,1)S(1)} %bitcast.35, bf16[2240,768]{1,0:T(8,128)(2,1)} %get-tuple-element.22), kind=kOutput, calls=%fused_computation.6 | convolution fusion | flops 1220542464 | bytes 16318464 | tf_op jit(solution)/shard_map/dot_general | solution.py:672
  101.2 13.9 %all-to-all-done.1 = bf16[128,40,128]{2,1,0:T(8,128)(2,1)S(1)} async-done(((bf16[128,40,128]{2,1,0:T(8,128)(2,1)}), bf16[128,40,128]{2,1,0:T(8,128)(2,1)S(1)}, u32[]{:S(2)}, u32[]{:S(2)}) %all-to-all-start.1) | async-done | bytes 1310752 | tf_op jit(solution)/shard_map/all_to_all | solution.py:575
  115.1 2.1 %unpack.1 = (f32[384,1152]{1,0:T(8,128)}, f32[384,384]{1,0:T(8,128)}) custom-call(bf16[5120,128]{1,0:T(8,128)(2,1)S(1)} %bitcast.34), custom_call_target="tpu_custom_call" | custom-call | tf_op jit(solution)/shard_map/unpack/pallas_call | solution.py:598
  (61 shorter events, 6.7 us)
Async XLA Ops:
  2.7 7.3 %collective-permute-start = (bf16[3,32,385]{2,1,0:T(8,128)(2,1)S(1)}, bf16[3,32,385]{2,1,0:T(8,128)(2,1)S(1)}, u32[]{:S(2)}, u32[]{:S(2)}) collective-permute-start(bf16[3,32,385]{2,1,0:T(8,128)(2,1)S(1)} %pad_maximum_fusion.4), channel_id=1, source_target_pairs={{0,16},{16,32},{32,48},{48,64},{64,80},{80,96},{96,112},{112,0},{1... | collective-permute-start | bytes 221768 | tf_op jit(solution)/shard_map/ppermute | solution.py:541
  5.2 4.8 %collective-permute-start.1 = (bf16[3,32,385]{2,1,0:T(8,128)(2,1)S(1)}, bf16[3,32,385]{2,1,0:T(8,128)(2,1)S(1)}, u32[]{:S(2)}, u32[]{:S(2)}) collective-permute-start(bf16[3,32,385]{2,1,0:T(8,128)(2,1)S(1)} %pad_maximum_fusion.5), channel_id=1, source_target_pairs={{16,0},{32,16},{48,32},{64,48},{80,64},{96,80},{112,96},{0,112},{1... | collective-permute-start | bytes 221768 | tf_op jit(solution)/shard_map/ppermute | solution.py:546
  10.0 12.4 %copy-start.7 = (bf16[3,32,385]{2,1,0:T(8,128)(2,1)}, bf16[3,32,385]{2,1,0:T(8,128)(2,1)S(1)}, u32[]{:S(2)}) copy-start(bf16[3,32,385]{2,1,0:T(8,128)(2,1)S(1)} %collective-permute-done) | copy-start | bytes 221764
  10.0 12.4 %copy-start.8 = (bf16[3,32,385]{2,1,0:T(8,128)(2,1)}, bf16[3,32,385]{2,1,0:T(8,128)(2,1)S(1)}, u32[]{:S(2)}) copy-start(bf16[3,32,385]{2,1,0:T(8,128)(2,1)S(1)} %collective-permute-done.1) | copy-start | bytes 221764
  10.2 12.3 %collective-permute-start.2 = (bf16[70,3,385]{2,0,1:T(8,128)(2,1)S(1)}, bf16[70,3,385]{2,0,1:T(8,128)(2,1)S(1)}, u32[]{:S(2)}, u32[]{:S(2)}) collective-permute-start(bf16[70,3,385]{2,0,1:T(8,128)(2,1)S(1)} %pad_maximum_fusion.2), channel_id=1, source_target_pairs={{1,0},{2,1},{3,2},{4,3},{5,4},{6,5},{7,6},{8,7},{9,8},{10,9},{11,1... | collective-permute-start | bytes 485108 | tf_op jit(solution)/shard_map/ppermute | solution.py:546
  11.5 10.9 %collective-permute-start.3 = (bf16[70,3,385]{2,0,1:T(8,128)(2,1)S(1)}, bf16[70,3,385]{2,0,1:T(8,128)(2,1)S(1)}, u32[]{:S(2)}, u32[]{:S(2)}) collective-permute-start(bf16[70,3,385]{2,0,1:T(8,128)(2,1)S(1)} %pad_maximum_fusion.3), channel_id=1, source_target_pairs={{0,1},{1,2},{2,3},{3,4},{4,5},{5,6},{6,7},{7,8},{8,9},{9,10},{10,1... | collective-permute-start | bytes 485108 | tf_op jit(solution)/shard_map/ppermute | solution.py:541
  49.6 13.5 %copy-start.1 = (bf16[2048,384]{1,0:T(8,128)(2,1)S(1)}, bf16[2048,384]{1,0:T(8,128)(2,1)}, u32[]{:S(2)}) copy-start(bf16[2048,384]{1,0:T(8,128)(2,1)} %get-tuple-element.21) | copy-start | bytes 4718596
  49.6 21.5 %collective-permute-start.4 = (bf16[288,768]{1,0:T(8,128)(2,1)}, bf16[288,768]{1,0:T(8,128)(2,1)S(1)}, u32[]{:S(2)}, u32[]{:S(2)}) collective-permute-start(bf16[288,768]{1,0:T(8,128)(2,1)} %get-tuple-element.23), channel_id=1, source_target_pairs={{0,1},{1,2},{2,3},{3,4},{4,5},{5,6},{6,7},{7,8},{8,9},{9,10},{10,1... | collective-permute-start | bytes 1327112 | tf_op jit(solution)/shard_map/ppermute | solution.py:541
  51.3 20.1 %collective-permute-start.5 = (bf16[288,768]{1,0:T(8,128)(2,1)}, bf16[288,768]{1,0:T(8,128)(2,1)}, u32[]{:S(2)}, u32[]{:S(2)}) collective-permute-start(bf16[288,768]{1,0:T(8,128)(2,1)} %get-tuple-element.24), channel_id=1, source_target_pairs={{1,0},{2,1},{3,2},{4,3},{5,4},{6,5},{7,6},{8,7},{9,8},{10,9},{11,1... | collective-permute-start | bytes 1327112 | tf_op jit(solution)/shard_map/ppermute | solution.py:546
  52.9 33.0 %all-to-all-start = ((bf16[128,40,128]{2,1,0:T(8,128)(2,1)}), bf16[128,40,128]{2,1,0:T(8,128)(2,1)S(1)}, u32[]{:S(2)}, u32[]{:S(2)}) async-start(bf16[128,40,128]{2,1,0:T(8,128)(2,1)} %bitcast.44), calls=%async_computation | async-start | bytes 2621440 | tf_op jit(solution)/shard_map/all_to_all | solution.py:573
  63.1 5.7 %copy-start.2 = (bf16[64,32,384]{2,1,0:T(8,128)(2,1)S(1)}, bf16[64,32,384]{2,1,0:T(8,128)(2,1)}, u32[]{:S(2)}) copy-start(bf16[64,32,384]{2,1,0:T(8,128)(2,1)} %param.5) | copy-start | bytes 4718596
  63.1 5.7 %copy-start.3 = (bf16[2048,384]{1,0:T(8,128)(2,1)S(1)}, bf16[2048,384]{1,0:T(8,128)(2,1)}, u32[]{:S(2)}) copy-start(bf16[2048,384]{1,0:T(8,128)(2,1)} %get-tuple-element.20) | copy-start | bytes 4718596
  63.1 5.7 %copy-start.6 = (bf16[384,384]{1,0:T(8,128)(2,1)S(1)}, bf16[384,384]{1,0:T(8,128)(2,1)}, u32[]{:S(2)}) copy-start(bf16[384,384]{1,0:T(8,128)(2,1)} %wo_ref.1) | copy-start | bytes 884740
  73.8 20.5 %collective-permute-start.6 = (bf16[3,32,768]{2,1,0:T(8,128)(2,1)S(1)}, bf16[3,32,768]{2,1,0:T(8,128)(2,1)S(1)}, u32[]{:S(2)}, u32[]{:S(2)}) collective-permute-start(bf16[3,32,768]{2,1,0:T(8,128)(2,1)S(1)} %get-tuple-element.46), channel_id=1, source_target_pairs={{0,16},{16,32},{32,48},{48,64},{64,80},{80,96},{96,112},{112,0},{1... | collective-permute-start | bytes 442376 | tf_op jit(solution)/shard_map/ppermute | solution.py:541
  75.2 19.0 %collective-permute-start.7 = (bf16[3,32,768]{2,1,0:T(8,128)(2,1)S(1)}, bf16[3,32,768]{2,1,0:T(8,128)(2,1)S(1)}, u32[]{:S(2)}, u32[]{:S(2)}) collective-permute-start(bf16[3,32,768]{2,1,0:T(8,128)(2,1)S(1)} %get-tuple-element.47), channel_id=1, source_target_pairs={{16,0},{32,16},{48,32},{64,48},{80,64},{96,80},{112,96},{0,112},{1... | collective-permute-start | bytes 442376 | tf_op jit(solution)/shard_map/ppermute | solution.py:546
  87.2 28.0 %all-to-all-start.1 = ((bf16[128,40,128]{2,1,0:T(8,128)(2,1)}), bf16[128,40,128]{2,1,0:T(8,128)(2,1)S(1)}, u32[]{:S(2)}, u32[]{:S(2)}) async-start(bf16[128,40,128]{2,1,0:T(8,128)(2,1)} %bitcast.18), calls=%async_computation.1 | async-start | bytes 2621440 | tf_op jit(solution)/shard_map/all_to_all | solution.py:575
  93.4 1.9 %copy-start = (f32[2048,384]{1,0:T(8,128)S(1)}, f32[2048,384]{1,0:T(8,128)}, u32[]{:S(2)}) copy-start(f32[2048,384]{1,0:T(8,128)} %fusion.11) | copy-start | bytes 9437188
  93.4 2.1 %copy-start.4 = (bf16[384,1152]{1,0:T(8,128)(2,1)S(1)}, bf16[384,1152]{1,0:T(8,128)(2,1)}, u32[]{:S(2)}) copy-start(bf16[384,1152]{1,0:T(8,128)(2,1)} %wp_ref.3) | copy-start | bytes 2654212
  93.4 2.6 %copy-start.5 = (bf16[64,32,384]{2,1,0:T(8,128)(2,1)S(1)}, bf16[64,32,384]{2,1,0:T(8,128)(2,1)}, u32[]{:S(2)}) copy-start(bf16[64,32,384]{2,1,0:T(8,128)(2,1)} %param.7) | copy-start | bytes 4718596
